TPU v7x, 32 devices: a whole 2x2x4 slice. The times are simulated.
32 devices in a mesh: group: 2 (over y), dp: 8 (over z, x), blk: 2 (over core).
Axes of the slice: x: 2, y: 2, z: 4, core: 2. Of those that a mesh axis runs over, the one named last changes fastest.
Arguments:
- activations: bfloat16 [4096, 8192], P(('group', 'dp'), 'blk'), parts along dimension 0, may hold values from -6 to 6
- teacher_out: bfloat16 [4096, 8192], P(('group', 'dp'), 'blk'), parts along dimension 0, may hold values from -6 to 6
- block_order: int32 [64], replicated, may hold values from 0 to 63, each once
- gate_left: bfloat16 [64, 2048], P('blk', 'dp'), may hold values from -0.5 to 0.5
- gate_right: bfloat16 [64, 3584], P('blk', 'dp'), may hold values from -1.5 to 1.5
- up_left: bfloat16 [64, 2048], P('blk', 'dp'), may hold values from -0.5 to 0.5
- up_right: bfloat16 [64, 3584], P('blk', 'dp'), may hold values from -1.5 to 1.5
- down_left: bfloat16 [64, 3584], P('blk', 'dp'), may hold values from -0.375 to 0.375
- down_right: bfloat16 [64, 2048], P('blk', 'dp'), may hold values from -1.5 to 1.5
Outputs:
- grad_gate_left: float32 [128, 2048], P(('group', 'blk'), 'dp'), parts along dimension 0
- grad_gate_right: float32 [128, 3584], P(('group', 'blk'), 'dp'), parts along dimension 0
- grad_up_left: float32 [128, 2048], P(('group', 'blk'), 'dp'), parts along dimension 0
- grad_up_right: float32 [128, 3584], P(('group', 'blk'), 'dp'), parts along dimension 0
- grad_down_left: float32 [128, 3584], P(('group', 'blk'), 'dp'), parts along dimension 0
- grad_down_right: float32 [128, 2048], P(('group', 'blk'), 'dp'), parts along dimension 0
There are 2 independent parts, one for each index of `group`. A program takes and returns all parts, laid end to end along the dimension named above; an argument that names none is the same for every part. Nothing has to cross between parts.
Inputs may be any that keep to these rules, and one draw needn't show every extreme that they name: block_order names each block exactly once.
All inputs are finite; a program needn't handle non-finite values.
Results may differ from a plain program's by a relative error of at most 0.0043.
Values may be sent and summed in bfloat16 or wider, within the bound.
No kernel may reach another device: no remote copies, remote signals or barrier semaphores. Data moves between devices by JAX's collectives and lax.ppermute only.
A program may use at most 128 MiB of HBM per device.

v0:
```python
import jax
import jax.numpy as jnp
from jax import lax
from jax.sharding import PartitionSpec as P

NB = 64
RANK = 16
BIN = 128
BHID = 224


def arrange(values, order):
    rows = values.shape[0]
    grid = values.reshape(rows, -1, NB)
    return jnp.take(grid, order, axis=2)


def settle(returned, inverse, blocks):
    rows = returned.shape[0]
    return jnp.take(returned, inverse, axis=2).reshape(rows, blocks, RANK)


def on_device(
    activations,
    teacher_out,
    block_order,
    gate_left,
    gate_right,
    up_left,
    up_right,
    down_left,
    down_right,
):
    f32 = jnp.float32
    bf16 = jnp.bfloat16
    whole = (
        lax.all_gather(gate_left, "dp", axis=1, tiled=True),
        lax.all_gather(gate_right, "dp", axis=1, tiled=True),
        lax.all_gather(up_left, "dp", axis=1, tiled=True),
        lax.all_gather(up_right, "dp", axis=1, tiled=True),
        lax.all_gather(down_left, "dp", axis=1, tiled=True),
        lax.all_gather(down_right, "dp", axis=1, tiled=True),
    )
    blocks = whole[0].shape[0]
    left_gate = whole[0].reshape(blocks, BIN, RANK)
    right_gate = whole[1].reshape(blocks, RANK, BHID)
    left_up = whole[2].reshape(blocks, BIN, RANK)
    right_up = whole[3].reshape(blocks, RANK, BHID)
    left_down = whole[4].reshape(blocks, BHID, RANK)
    right_down = whole[5].reshape(blocks, RANK, BIN)
    rows = activations.shape[0]
    feats = activations.reshape(rows, blocks, BIN)
    inverse = jnp.argsort(block_order)
    gate_inner = jnp.einsum("tjb,jbc->tjc", feats, left_gate, preferred_element_type=f32).astype(
        bf16
    )
    up_inner = jnp.einsum("tjb,jbc->tjc", feats, left_up, preferred_element_type=f32).astype(bf16)
    sent = (
        lax.all_to_all(
            arrange(gate_inner, block_order), "blk", split_axis=2, concat_axis=1, tiled=True
        ),
        lax.all_to_all(
            arrange(up_inner, block_order), "blk", split_axis=2, concat_axis=1, tiled=True
        ),
    )
    gate_mixed = jnp.transpose(sent[0], (0, 2, 1))
    up_mixed = jnp.transpose(sent[1], (0, 2, 1))
    gate = jnp.einsum("tka,kao->tko", gate_mixed, right_gate, preferred_element_type=f32)
    upper = jnp.einsum("tka,kao->tko", up_mixed, right_up, preferred_element_type=f32)
    sig = jax.nn.sigmoid(gate)
    act = gate * sig
    hidden = (act * upper).astype(bf16)
    down_inner = jnp.einsum("tjo,joc->tjc", hidden, left_down, preferred_element_type=f32).astype(
        bf16
    )
    sent_down = lax.all_to_all(
        arrange(down_inner, block_order), "blk", split_axis=2, concat_axis=1, tiled=True
    )
    down_mixed = jnp.transpose(sent_down, (0, 2, 1))
    student = jnp.einsum("tka,kab->tkb", down_mixed, right_down, preferred_element_type=f32)
    scale = float(rows * lax.axis_size("dp")) ** (-0.5)
    delta = ((student - teacher_out.reshape(rows, blocks, BIN).astype(f32)) * scale).astype(bf16)
    grad_rd = jnp.einsum("tka,tkb->kab", down_mixed, delta, preferred_element_type=f32)
    down_back = jnp.einsum("tkb,kab->tka", delta, right_down, preferred_element_type=f32).astype(
        bf16
    )
    back_down = lax.all_to_all(
        jnp.transpose(down_back, (0, 2, 1)), "blk", split_axis=1, concat_axis=2, tiled=True
    )
    down_return = settle(back_down, inverse, blocks)
    grad_ld = jnp.einsum("tjo,tjc->joc", hidden, down_return, preferred_element_type=f32)
    dhidden = jnp.einsum("tjc,joc->tjo", down_return, left_down, preferred_element_type=f32)
    dgate = (dhidden * upper * sig * (1.0 + gate * (1.0 - sig))).astype(bf16)
    dup = (dhidden * act).astype(bf16)
    grad_rg = jnp.einsum("tka,tko->kao", gate_mixed, dgate, preferred_element_type=f32)
    grad_ru = jnp.einsum("tka,tko->kao", up_mixed, dup, preferred_element_type=f32)
    gate_back = jnp.einsum("tko,kao->tka", dgate, right_gate, preferred_element_type=f32).astype(
        bf16
    )
    up_back = jnp.einsum("tko,kao->tka", dup, right_up, preferred_element_type=f32).astype(bf16)
    back_pair = (
        lax.all_to_all(
            jnp.transpose(gate_back, (0, 2, 1)), "blk", split_axis=1, concat_axis=2, tiled=True
        ),
        lax.all_to_all(
            jnp.transpose(up_back, (0, 2, 1)), "blk", split_axis=1, concat_axis=2, tiled=True
        ),
    )
    gate_return = settle(back_pair[0], inverse, blocks)
    up_return = settle(back_pair[1], inverse, blocks)
    grad_lg = jnp.einsum("tjb,tjc->jbc", feats, gate_return, preferred_element_type=f32)
    grad_lu = jnp.einsum("tjb,tjc->jbc", feats, up_return, preferred_element_type=f32)
    result = (
        lax.psum_scatter(grad_lg.reshape(blocks, -1), "dp", scatter_dimension=1, tiled=True),
        lax.psum_scatter(grad_rg.reshape(blocks, -1), "dp", scatter_dimension=1, tiled=True),
        lax.psum_scatter(grad_lu.reshape(blocks, -1), "dp", scatter_dimension=1, tiled=True),
        lax.psum_scatter(grad_ru.reshape(blocks, -1), "dp", scatter_dimension=1, tiled=True),
        lax.psum_scatter(grad_ld.reshape(blocks, -1), "dp", scatter_dimension=1, tiled=True),
        lax.psum_scatter(grad_rd.reshape(blocks, -1), "dp", scatter_dimension=1, tiled=True),
    )
    return (result[0], result[1], result[2], result[3], result[4], result[5])


def solution(mesh):
    in_specs = (
        P(("group", "dp"), "blk"),
        P(("group", "dp"), "blk"),
        P(),
        P("blk", "dp"),
        P("blk", "dp"),
        P("blk", "dp"),
        P("blk", "dp"),
        P("blk", "dp"),
        P("blk", "dp"),
    )
    out_specs = (
        P(("group", "blk"), "dp"),
        P(("group", "blk"), "dp"),
        P(("group", "blk"), "dp"),
        P(("group", "blk"), "dp"),
        P(("group", "blk"), "dp"),
        P(("group", "blk"), "dp"),
    )
    return jax.shard_map(
        on_device, mesh=mesh, in_specs=in_specs, out_specs=out_specs, check_vma=False
    )
```

profile of v0, /device:TPU:0, one launch (start us, length us, event | category | flops | bytes accessed | tf_op | source)
XLA Modules:
  0.0 689.7 jit_solution(9703821397321889254)
XLA Ops:
  8.7 32.6 %all_gather.18 = bf16[32,2048]{1,0:T(8,128)(2,1)S(1)} all-gather(bf16[32,256]{1,0:T(8,128)(2,1)} %param.14), channel_id=1, replica_groups=mesh['group'=2,'dp'=8,'blk'=2] {'dp'}, dimensions={1}, use_global_device_ids=true | all-gather | bytes 147456 | tf_op jit(solution)/shard_map/all_gather | solution.py:37
  41.2 30.7 %all_gather.20 = bf16[32,2048]{1,0:T(8,128)(2,1)S(1)} all-gather(bf16[32,256]{1,0:T(8,128)(2,1)} %param.16), channel_id=1, replica_groups=mesh['group'=2,'dp'=8,'blk'=2] {'dp'}, dimensions={1}, use_global_device_ids=true | all-gather | bytes 147456 | tf_op jit(solution)/shard_map/all_gather | solution.py:39
  77.3 3.4 all-to-all-start
  80.8 30.8 %all-gather = bf16[8,448,32]{1,2,0:T(8,128)(2,1)S(1)} all-gather(bf16[1,448,32]{1,2,0:T(8,128)(2,1)S(1)} %bitcast.251), channel_id=1, replica_groups=mesh['group'=2,'dp'=8,'blk'=2] {'dp'}, dimensions={0}, use_global_device_ids=true | all-gather | bytes 258048 | tf_op jit(solution)/shard_map/all_gather | solution.py:38
  112.4 30.7 %all-gather.1 = bf16[8,448,32]{1,2,0:T(8,128)(2,1)S(1)} all-gather(bf16[1,448,32]{1,2,0:T(8,128)(2,1)S(1)} %bitcast.252), channel_id=1, replica_groups=mesh['group'=2,'dp'=8,'blk'=2] {'dp'}, dimensions={0}, use_global_device_ids=true | all-gather | bytes 258048 | tf_op jit(solution)/shard_map/all_gather | solution.py:40
  144.7 30.8 %all-gather.2 = bf16[8,448,32]{1,2,0:T(8,128)(2,1)S(1)} all-gather(bf16[1,448,32]{1,2,0:T(8,128)(2,1)S(1)} %bitcast.253), channel_id=1, replica_groups=mesh['group'=2,'dp'=8,'blk'=2] {'dp'}, dimensions={0}, use_global_device_ids=true | all-gather | bytes 258048 | tf_op jit(solution)/shard_map/all_gather | solution.py:41
  179.7 3.4 all-to-all-start.1
  183.2 4.1 fusion.47
  187.3 6.3 fusion.4
  197.6 3.4 all-to-all-start.2
  201.1 30.7 %all_gather.23 = bf16[32,2048]{1,0:T(8,128)(2,1)S(1)} all-gather(bf16[32,256]{1,0:T(8,128)(2,1)S(1)} %copy-done.15), channel_id=1, replica_groups=mesh['group'=2,'dp'=8,'blk'=2] {'dp'}, dimensions={1}, use_global_device_ids=true | all-gather | bytes 147456 | tf_op jit(solution)/shard_map/all_gather | solution.py:42
  231.8 4.1 copy.147
  235.9 4.3 copy.148
  246.1 3.4 all-to-all-start.3
  252.6 8.8 %fusion.3 = (bf16[256,32,224]{0,2,1:T(8,128)(2,1)}, bf16[256,32,224]{0,2,1:T(8,128)(2,1)S(1)}) fusion(f32[32,256,224]{1,2,0:T(8,128)} %fusion.47, f32[32,256,224]{1,2,0:T(8,128)} %get-tuple-element.40, bf16[256,32,16]{0,2,1:T(8,128)(2,1)S(1)} %bitcast.231, bf16[32,224,16]{1,2,0:T(8,128)(2,1)} %copy.144), kind=kOutput, calls=%fused_computation.11 | convolution fusion | flops 82575360 | bytes 22511616 | tf_op jit(solution)/shard_map/tjc,joc->tjo/dot_general | solution.py:92
  264.5 3.4 all-to-all-start.4
  271.4 4.1 all-to-all-start.5
  288.7 3.2 fusion.41
  302.2 44.0 %reduce-scatter.11.cloned.1.call-done = f32[32,256]{0,1:T(8,128)} async-done(((f32[32,2048]{0,1:T(8,128)}), f32[32,256]{0,1:T(8,128)}) %reduce-scatter.11.cloned.1.call-update) | async-done | bytes 32784 | tf_op jit(solution)/shard_map/reduce_scatter | solution.py:114
  347.8 64.6 %reduce-scatter.13.cloned.1.call-done = f32[32,256]{0,1:T(8,128)} async-done(((f32[32,2048]{0,1:T(8,128)}), f32[32,256]{0,1:T(8,128)}) %reduce-scatter.13.cloned.1.call-update) | async-done | bytes 32784 | tf_op jit(solution)/shard_map/reduce_scatter | solution.py:116
  414.0 67.1 %reduce-scatter.19.cloned.1.call-done = f32[448,32]{1,0:T(8,128)} async-done(((f32[3584,32]{1,0:T(8,128)}), f32[448,32]{1,0:T(8,128)}) %reduce-scatter.19.cloned.1.call-update) | async-done | bytes 57360
  482.7 67.3 %reduce-scatter.21.cloned.1.call-done = f32[448,32]{1,0:T(8,128)} async-done(((f32[3584,32]{1,0:T(8,128)}), f32[448,32]{1,0:T(8,128)}) %reduce-scatter.21.cloned.1.call-update) | async-done | bytes 57360
  551.7 66.6 %reduce-scatter.15.cloned.1.call-done = f32[32,448]{0,1:T(8,128)} async-done(((f32[32,3584]{0,1:T(8,128)}), f32[32,448]{0,1:T(8,128)}) %reduce-scatter.15.cloned.1.call-update) | async-done | bytes 57360 | tf_op jit(solution)/shard_map/reduce_scatter | solution.py:118
  619.9 63.0 %reduce-scatter.17.cloned.1.call-done = f32[32,256]{1,0:T(8,128)} async-done(((f32[32,2048]{1,0:T(8,128)}), f32[32,256]{1,0:T(8,128)}) %reduce-scatter.17.cloned.1.call-update) | async-done | bytes 32784 | tf_op jit(solution)/shard_map/reduce_scatter | solution.py:119
  (123 shorter events, 64.3 us)
Async XLA Ops:
  7.2 65.6 %copy-start = (bf16[256,4096]{1,0:T(8,128)(2,1)S(1)}, bf16[256,4096]{1,0:T(8,128)(2,1)}, u32[]{:S(2)}) copy-start(bf16[256,4096]{1,0:T(8,128)(2,1)} %param.11) | copy-start | bytes 6291460
  73.8 7.0 %copy-start.12 = (bf16[32,448]{1,0:T(8,128)(2,1)S(1)}, bf16[32,448]{1,0:T(8,128)(2,1)}, u32[]{:S(2)}) copy-start(bf16[32,448]{1,0:T(8,128)(2,1)} %param.15) | copy-start | bytes 86020
  75.0 37.4 %copy-start.13 = (bf16[32,448]{1,0:T(8,128)(2,1)S(1)}, bf16[32,448]{1,0:T(8,128)(2,1)}, u32[]{:S(2)}) copy-start(bf16[32,448]{1,0:T(8,128)(2,1)} %param.17) | copy-start | bytes 86020
  75.2 69.5 %copy-start.14 = (bf16[32,448]{1,0:T(8,128)(2,1)S(1)}, bf16[32,448]{1,0:T(8,128)(2,1)}, u32[]{:S(2)}) copy-start(bf16[32,448]{1,0:T(8,128)(2,1)} %param.18) | copy-start | bytes 86020
  77.3 102.4 %all-to-all-start = ((bf16[256,8,64]{0,1,2:T(8,128)(2,1)}), bf16[256,8,64]{0,1,2:T(8,128)(2,1)S(1)}, u32[]{:S(2)}, u32[]{:S(2)}) async-start(bf16[256,8,64]{0,1,2:T(8,128)(2,1)} %get-tuple-element.37), calls=%async_computation | async-start | bytes 524288 | tf_op jit(solution)/shard_map/all_to_all | solution.py:59
  179.7 7.6 %all-to-all-start.1 = ((bf16[256,8,64]{0,1,2:T(8,128)(2,1)}), bf16[256,8,64]{0,1,2:T(8,128)(2,1)S(1)}, u32[]{:S(2)}, u32[]{:S(2)}) async-start(bf16[256,8,64]{0,1,2:T(8,128)(2,1)} %get-tuple-element.38), calls=%async_computation.1 | async-start | bytes 524288 | tf_op jit(solution)/shard_map/all_to_all | solution.py:62
  187.3 6.3 copy-start.4
  187.3 8.1 %copy-start.10 = (bf16[32,224,16]{1,2,0:T(8,128)(2,1)S(1)}, bf16[32,224,16]{1,2,0:T(8,128)(2,1)}, u32[]{:S(2)}) copy-start(bf16[32,224,16]{1,2,0:T(8,128)(2,1)} %copy.144) | copy-start | bytes 688132
  193.6 7.5 %copy-start.15 = (bf16[32,256]{1,0:T(8,128)(2,1)S(1)}, bf16[32,256]{1,0:T(8,128)(2,1)}, u32[]{:S(2)}) copy-start(bf16[32,256]{1,0:T(8,128)(2,1)} %param.19) | copy-start | bytes 49156
  197.6 42.6 %all-to-all-start.2 = ((bf16[256,8,64]{0,1,2:T(8,128)(2,1)}), bf16[256,8,64]{0,1,2:T(8,128)(2,1)S(1)}, u32[]{:S(2)}, u32[]{:S(2)}) async-start(bf16[256,8,64]{0,1,2:T(8,128)(2,1)} %select_bitcast_fusion.3), calls=%async_computation.2 | async-start | bytes 524288 | tf_op jit(solution)/shard_map/all_to_all | solution.py:76
  240.2 9.3 %copy-start.16 = (s32[64]{0:T(128)S(1)}, s32[64]{0:T(128)}, u32[]{:S(2)}) copy-start(s32[64]{0:T(128)} %param.13) | copy-start | bytes 772
  246.1 5.5 all-to-all-start.3
  252.6 8.8 %copy-start.6 = (bf16[256,8,64]{0,2,1:T(8,128)(2,1)}, bf16[256,8,64]{0,2,1:T(8,128)(2,1)S(1)}, u32[]{:S(2)}) copy-start(bf16[256,8,64]{0,2,1:T(8,128)(2,1)S(1)} %copy.152) | copy-start | bytes 786436
  261.4 6.6 copy-start.9
  264.5 6.9 all-to-all-start.4
  271.4 5.8 all-to-all-start.5
  275.5 70.7 %reduce-scatter.11.cloned.1.call-start = ((), (), s32[]{:S(2)}) async-start(), calls=%async_computation.12 | async-start | bytes 1179648 | tf_op jit(solution)/shard_map/reduce_scatter | solution.py:114
  281.6 130.8 %reduce-scatter.13.cloned.1.call-start = ((), (), s32[]{:S(2)}) async-start(), calls=%async_computation.13 | async-start | bytes 1179648 | tf_op jit(solution)/shard_map/reduce_scatter | solution.py:116
  283.6 5.2 copy-start.5
  283.6 197.5 %reduce-scatter.19.cloned.1.call-start = ((), (), s32[]{:S(2)}) async-start(), calls=%async_computation.16 | async-start | bytes 2064384
  288.7 5.2 copy-start.7
  288.7 261.3 %reduce-scatter.21.cloned.1.call-start = ((), (), s32[]{:S(2)}) async-start(), calls=%async_computation.17 | async-start | bytes 2064384
  293.8 324.4 %reduce-scatter.15.cloned.1.call-start = ((), (), s32[]{:S(2)}) async-start(), calls=%async_computation.14 | async-start | bytes 2064384 | tf_op jit(solution)/shard_map/reduce_scatter | solution.py:118
  299.3 383.6 %reduce-scatter.17.cloned.1.call-start = ((), (), s32[]{:S(2)}) async-start(), calls=%async_computation.15 | async-start | bytes 294912 | tf_op jit(solution)/shard_map/reduce_scatter | solution.py:119
  (5 other events, 11.0 us)
Sparse Core Ops, SparseCore 0:
  281.8 64.4 reduce-scatter.10
  350.0 62.3 reduce-scatter.12
  415.9 65.1 reduce-scatter.18
  484.8 65.1 reduce-scatter.20
  553.3 64.8 reduce-scatter.14
  622.4 60.4 reduce-scatter.16
where the time goes:
time: 691 us; the launch traced here: 690 us
  waiting for transfers between devices  373 us (54%)
  blocking collectives  186 us (27%)
  local copies, waits for them, and re-layouts  47.4 us (7%)
  matrix products  40.1 us (6%)
  starting transfers between devices  21.5 us (3%)
  between operations  14.6 us (2%)
    unnamed x8, waiting for transfers between devices  134 us
    reduce_scatter x1, waiting for transfers between devices, on_device(): lax.psum_scatter(grad_ld.reshape(blocks, -1), 'dp', scatter_dimension=1,...  66.6 us
    reduce_scatter x1, waiting for transfers between devices, on_device(): lax.psum_scatter(grad_lu.reshape(blocks, -1), 'dp', scatter_dimension=1,...  64.6 us
    reduce_scatter x1, waiting for transfers between devices, on_device(): lax.psum_scatter(grad_rd.reshape(blocks, -1), 'dp', scatter_dimension=1,...  63 us
    reduce_scatter x1, waiting for transfers between devices, on_device(): lax.psum_scatter(grad_lg.reshape(blocks, -1), 'dp', scatter_dimension=1,...  44 us
    all_gather x1, blocking collectives, on_device(): lax.all_gather(gate_left, 'dp', axis=1, tiled=True)  32.6 us
    all_gather x1, blocking collectives, on_device(): lax.all_gather(down_left, 'dp', axis=1, tiled=True)  30.8 us
    all_gather x1, blocking collectives, on_device(): lax.all_gather(gate_right, 'dp', axis=1, tiled=True)  30.8 us
  transfers between devices with their start and end apart: 12, of which 7 were waited for; matrix products, arithmetic and copies ran while one was open for 8% of the time, Pallas kernels for 0%

commit v1 on v0

v1 whole, which is shorter than its diff:
```python
import functools

import jax
import jax.numpy as jnp
from jax import lax
from jax.experimental import pallas as pl
from jax.experimental.pallas import tpu as pltpu
from jax.sharding import PartitionSpec as P

NB = 64
HALF = 32
RANK = 16
BIN = 128
BHID = 224
WIDE = 256
CHUNKS = 8
ROWS = 560
f32 = jnp.float32
bf16 = jnp.bfloat16

R_AT = 128
RD_AT = 384
LD_AT = 448


def pack(lg, rg, lu, ru, ld, rd):
    left = jnp.stack([lg, lu]).reshape(2, HALF, 16, 2, 8)
    left = jnp.transpose(left, (2, 4, 3, 0, 1)).reshape(128, 128)
    right = jnp.stack([rg, ru]).reshape(2, HALF, 2, BHID)
    right = jnp.pad(right, ((0, 0), (0, 0), (0, 0), (0, WIDE - BHID)))
    right = right.reshape(2, HALF, 2, 2, 128)
    right = jnp.transpose(right, (3, 0, 2, 1, 4)).reshape(256, 128)
    rdown = jnp.transpose(rd.reshape(HALF, 2, 128), (1, 0, 2)).reshape(64, 128)
    ldown = jnp.transpose(ld.reshape(HALF, 28, 4, 4), (1, 3, 2, 0)).reshape(112, 128)
    return jnp.concatenate([left, right, rdown, ldown], axis=0)


def unpack(packed):
    left = packed[:R_AT].reshape(16, 8, 2, 2, HALF)
    left = jnp.transpose(left, (3, 4, 0, 2, 1)).reshape(2, HALF, 256)
    right = packed[R_AT:RD_AT].reshape(2, 2, 2, HALF, 128)
    right = jnp.transpose(right, (1, 3, 2, 0, 4)).reshape(2, HALF, 2, WIDE)
    right = right[..., :BHID].reshape(2, HALF, 448)
    rdown = jnp.transpose(packed[RD_AT:LD_AT].reshape(2, HALF, 128), (1, 0, 2)).reshape(HALF, 256)
    ldown = packed[LD_AT:].reshape(28, 4, 4, HALF)
    ldown = jnp.transpose(ldown, (3, 0, 2, 1)).reshape(HALF, 448)
    return left[0], right[0], left[1], right[1], ldown, rdown


def nn(a, b):
    return jnp.dot(a, b, preferred_element_type=f32)


def nt(a, b):
    return lax.dot_general(a, b, (((1,), (1,)), ((), ())), preferred_element_type=f32)


def rounded(v):
    return v.astype(bf16).astype(f32)


def wide(pair, row, stride):
    return jnp.concatenate([v[pl.ds(row, RANK, stride=stride), :] for v in pair], axis=1).astype(bf16)


def widen(pair, row, stride, value):
    pair[0][pl.ds(row, RANK, stride=stride), :] = value[:, :128]
    pair[1][pl.ds(row, RANK, stride=stride), :] = value[:, 128:]


def body(scale, where, order, *refs):
    weights = refs[:16]
    x_ref, y_ref, out_ref = refs[16:19]
    (s_l, r_lo, r_hi, s_rd, d_lo, d_hi, inner, down, ret, act_s, slope_s, hid_s, stage) = refs[19:]
    s_r = (r_lo, r_hi)
    s_ld = (d_lo, d_hi)
    toks = x_ref.shape[0]
    me = where[0]
    side = where[1]

    for own in range(2):
        blk = side if own == 0 else 1 - side
        for r in range(CHUNKS):
            g = weights[own * CHUNKS + r]
            d = me ^ r
            for gu in range(2):
                for al in range(2):
                    row = pl.multiple_of((2 * d + al) * 128 + gu * NB + blk * HALF, HALF)
                    for half in range(2):
                        at = R_AT + half * 128 + gu * 64 + al * HALF
                        s_r[half][pl.ds(row, HALF), :] = g[pl.ds(at, HALF), :].astype(f32)
            for al in range(2):
                row = pl.multiple_of((2 * d + al) * NB + blk * HALF, HALF)
                s_rd[pl.ds(row, HALF), :] = g[pl.ds(RD_AT + al * HALF, HALF), :].astype(f32)
            stage[pl.ds(pl.multiple_of(d * 128, 128), 128), :] = g[pl.ds(0, 128), :].astype(f32)
            stage[pl.ds(pl.multiple_of(1024 + d * 112, 16), 112), :] = g[pl.ds(LD_AT, 112), :].astype(f32)
        for c8 in range(8):
            t = stage[pl.ds(c8, 128, stride=8), :].T
            for ch in range(2):
                for gu in range(2):
                    row = pl.multiple_of((ch * 8 + c8) * 128 + gu * NB + blk * HALF, HALF)
                    s_l[pl.ds(row, HALF), :] = t[(ch * 2 + gu) * HALF : (ch * 2 + gu + 1) * HALF]
        for c4 in range(4):
            t0 = stage[pl.ds(1024 + c4, 128, stride=4), :].T
            t1 = stage[pl.ds(1024 + 512 + c4, 96, stride=4), :]
            t1 = jnp.concatenate([t1, jnp.zeros((32, 128), f32)], axis=0).T
            for cq in range(4):
                row = pl.multiple_of((cq * 4 + c4) * NB + blk * HALF, HALF)
                d_lo[pl.ds(row, HALF), :] = t0[cq * HALF : (cq + 1) * HALF]
                d_hi[pl.ds(row, HALF), :] = t1[cq * HALF : (cq + 1) * HALF]

    def lanes(j, width=BIN):
        return pl.ds(pl.multiple_of(j * width, width), width)

    def first(j, _):
        wg = s_l[pl.ds(j, RANK, stride=128), :]
        wu = s_l[pl.ds(j + NB, RANK, stride=128), :]
        w = jnp.concatenate([wg, wu], axis=0).astype(bf16)
        got = rounded(nt(w, x_ref[:, lanes(j)]))
        at = pl.multiple_of(j * RANK, RANK)
        inner[pl.ds(at, RANK), :] = got[:RANK]
        inner[pl.ds(1024 + at, RANK), :] = got[RANK:]
        return 0

    lax.fori_loop(0, NB, first, 0, unroll=4)

    def mixed_of(m):
        return jnp.concatenate(
            [inner[pl.ds(m, RANK, stride=NB), :], inner[pl.ds(1024 + m, RANK, stride=NB), :]], axis=0
        )

    zeros = jnp.zeros((RANK, WIDE), bf16)

    def second(k, _):
        m = order[k]
        mixed = mixed_of(m).T.astype(bf16)
        wg = wide(s_r, k, 128)
        wu = wide(s_r, k + NB, 128)
        gate = nn(mixed, jnp.concatenate([wg, zeros], axis=0))
        upper = nn(mixed, jnp.concatenate([zeros, wu], axis=0))
        sig = 1.0 / (1.0 + jnp.exp(-gate))
        act = gate * sig
        hidden = (act * upper).astype(bf16)
        act_s[k] = act
        slope_s[k] = upper * sig * (1.0 + gate * (1.0 - sig))
        hid_s[k] = hidden
        wl = wide(s_ld, k, NB)
        down[pl.ds(pl.multiple_of(k * RANK, RANK), RANK), :] = rounded(nt(wl, hidden))
        return 0

    lax.fori_loop(0, NB, second, 0, unroll=2)

    def third(k, _):
        m = order[k]
        dm = down[pl.ds(m, RANK, stride=NB), :]
        wr = s_rd[pl.ds(k, RANK, stride=NB), :].astype(bf16)
        student = nn(dm.T.astype(bf16), wr)
        delta = ((student - y_ref[:, lanes(k)].astype(f32)) * scale).astype(bf16)
        back = rounded(nt(wr, delta))
        s_rd[pl.ds(k, RANK, stride=NB), :] = nn(dm.astype(bf16), delta)
        ret[pl.ds(m, RANK, stride=NB), :] = back
        return 0

    lax.fori_loop(0, NB, third, 0, unroll=2)

    def fourth(j, _):
        m = order[j]
        dr = ret[pl.ds(pl.multiple_of(j * RANK, RANK), RANK), :]
        wl = wide(s_ld, j, NB)
        dhidden = nn(dr.T.astype(bf16), wl)
        widen(s_ld, j, NB, nn(dr.astype(bf16), hid_s[j]))
        dgate = (dhidden * slope_s[j]).astype(bf16)
        dup = (dhidden * act_s[j]).astype(bf16)
        gm = inner[pl.ds(m, RANK, stride=NB), :].astype(bf16)
        um = inner[pl.ds(1024 + m, RANK, stride=NB), :].astype(bf16)
        wg = wide(s_r, j, 128)
        wu = wide(s_r, j + NB, 128)
        inner[pl.ds(m, RANK, stride=NB), :] = rounded(nt(wg, dgate))
        inner[pl.ds(1024 + m, RANK, stride=NB), :] = rounded(nt(wu, dup))
        widen(s_r, j, 128, nn(gm, dgate))
        widen(s_r, j + NB, 128, nn(um, dup))
        return 0

    lax.fori_loop(0, NB, fourth, 0, unroll=2)

    def fifth(j, _):
        at = pl.multiple_of(j * RANK, RANK)
        back = jnp.concatenate([inner[pl.ds(at, RANK), :], inner[pl.ds(1024 + at, RANK), :]], axis=0)
        grads = nn(back.astype(bf16), x_ref[:, lanes(j)])
        s_l[pl.ds(j, RANK, stride=128), :] = grads[:RANK]
        s_l[pl.ds(j + NB, RANK, stride=128), :] = grads[RANK:]
        return 0

    lax.fori_loop(0, NB, fifth, 0, unroll=4)

    for blk in range(2):
        for c8 in range(8):
            parts = []
            for ch in range(2):
                for gu in range(2):
                    row = (ch * 8 + c8) * 128 + gu * NB + blk * HALF
                    parts.append(s_l[pl.ds(row, HALF), :])
            stage[pl.ds(c8, 128, stride=8), :] = jnp.concatenate(parts, axis=0).T
        for c4 in range(4):
            p0, p1 = [], []
            for cq in range(4):
                row = (cq * 4 + c4) * NB + blk * HALF
                p0.append(d_lo[pl.ds(row, HALF), :])
                p1.append(d_hi[pl.ds(row, HALF), :])
            stage[pl.ds(1024 + c4, 128, stride=4), :] = jnp.concatenate(p0, axis=0).T
            stage[pl.ds(1024 + 512 + c4, 96, stride=4), :] = jnp.concatenate(p1, axis=0).T[:96]
        for d in range(CHUNKS):
            out_ref[blk, d, pl.ds(0, 128), :] = stage[pl.ds(d * 128, 128), :].astype(bf16)
            out_ref[blk, d, pl.ds(LD_AT, 112), :] = stage[pl.ds(1024 + d * 112, 112), :].astype(bf16)
            for gu in range(2):
                for al in range(2):
                    row = (2 * d + al) * 128 + gu * NB + blk * HALF
                    for half in range(2):
                        at = R_AT + half * 128 + gu * 64 + al * HALF
                        out_ref[blk, d, pl.ds(at, HALF), :] = s_r[half][pl.ds(row, HALF), :].astype(bf16)
            for al in range(2):
                row = (2 * d + al) * NB + blk * HALF
                out_ref[blk, d, pl.ds(RD_AT + al * HALF, HALF), :] = s_rd[pl.ds(row, HALF), :].astype(bf16)


def layer(scale, where, order, weights, x, y):
    toks = x.shape[0]
    vmem = pl.BlockSpec(memory_space=pltpu.VMEM)
    smem = pl.BlockSpec(memory_space=pltpu.SMEM)
    return pl.pallas_call(
        functools.partial(body, scale),
        out_shape=jax.ShapeDtypeStruct((2, CHUNKS, ROWS, 128), bf16),
        in_specs=[smem, smem] + [vmem] * 18,
        out_specs=vmem,
        scratch_shapes=[
            pltpu.VMEM((RANK * 128, BIN), f32),
            pltpu.VMEM((RANK * 128, 128), f32),
            pltpu.VMEM((RANK * 128, 128), f32),
            pltpu.VMEM((RANK * NB, BIN), f32),
            pltpu.VMEM((RANK * NB, 128), f32),
            pltpu.VMEM((RANK * NB, 128), f32),
            pltpu.VMEM((2 * NB * RANK, toks), f32),
            pltpu.VMEM((NB * RANK, toks), f32),
            pltpu.VMEM((NB * RANK, toks), f32),
            pltpu.VMEM((NB, toks, WIDE), f32),
            pltpu.VMEM((NB, toks, WIDE), f32),
            pltpu.VMEM((NB, toks, WIDE), bf16),
            pltpu.VMEM((1024 + 896, 128), f32),
        ],
        compiler_params=pltpu.CompilerParams(vmem_limit_bytes=56 * 2**20),
    )(where, order, *weights, x, y)


def swap(v, axis, bit, size):
    return lax.ppermute(v, axis, [(i, i ^ bit) for i in range(size)])


def at(v, i):
    return lax.dynamic_index_in_dim(v, i, 0, keepdims=False)


def tokens_of(v, side):
    half = v.shape[0] // 2
    own = lax.dynamic_slice_in_dim(v, side * half, half, 0)
    sent = lax.dynamic_slice_in_dim(v, (1 - side) * half, half, 0)
    got = swap(sent, "blk", 1, 2)
    first = jnp.where(side == 0, own, got)
    second = jnp.where(side == 0, got, own)
    return jnp.concatenate([first, second], axis=1)


def on_device(activations, teacher_out, block_order, *factors):
    n = lax.axis_size("dp")
    me = lax.axis_index("dp")
    side = lax.axis_index("blk")
    scale = float(activations.shape[0] * n) ** (-0.5)
    x = tokens_of(activations, side)
    y = tokens_of(teacher_out, side)
    if n == CHUNKS:
        mine = pack(*factors)
        along = [mine] + [swap(mine, "dp", 2 * s, n) for s in range(1, 4)]
        own = []
        for piece in along:
            own += [piece, swap(piece, "dp", 1, n)]
        where = jnp.stack([me, side]).astype(jnp.int32)
    else:
        whole = [lax.all_gather(v, "dp", axis=1, tiled=True) for v in factors]
        cut = [jnp.moveaxis(v.reshape(HALF, CHUNKS, -1), 1, 0) for v in whole]
        packed = jax.vmap(pack)(*cut)
        own = [packed[d] for d in range(CHUNKS)]
        where = jnp.stack([jnp.zeros_like(side), side]).astype(jnp.int32)
    other = swap(jnp.stack(own), "blk", 1, 2)
    grads = layer(scale, where, block_order, own + [other[d] for d in range(CHUNKS)], x, y)
    total = at(grads, side).astype(f32) + swap(at(grads, 1 - side), "blk", 1, 2).astype(f32)
    if n == CHUNKS:
        total = total.astype(bf16).reshape(4, 2, ROWS, 128)
        xs, zs = me % 2, me // 2
        pick = functools.partial(lax.dynamic_index_in_dim, axis=1, keepdims=False)
        line = pick(total, xs).astype(f32) + swap(pick(total, 1 - xs), "dp", 1, n).astype(f32)
        line = line.astype(bf16)
        result = at(line, zs).astype(f32)
        for s in range(1, 4):
            result = result + swap(at(line, zs ^ s), "dp", 2 * s, n).astype(f32)
        return unpack(result)
    parts = jax.vmap(unpack)(total)
    parts = [jnp.moveaxis(v, 0, 1).reshape(HALF, -1) for v in parts]
    return tuple(lax.psum_scatter(v, "dp", scatter_dimension=1, tiled=True) for v in parts)


def solution(mesh):
    rows = P(("group", "dp"), "blk")
    factor = P("blk", "dp")
    grad = P(("group", "blk"), "dp")
    return jax.shard_map(
        on_device,
        mesh=mesh,
        in_specs=(rows, rows, P()) + (factor,) * 6,
        out_specs=(grad,) * 6,
        check_vma=False,
    )
```

time: 691 us -> 144 us (0.21)
  waiting for transfers between devices: 373 us -> 34.7 us
  blocking collectives: 186 us -> 0 us
  Pallas kernels: 0 us -> 65.8 us
  matrix products: 40.1 us -> 0 us
  local copies, waits for them, and re-layouts: 47.4 us -> 18.8 us
  between operations: 14.6 us -> 1.08 us
    reduce_scatter x4 -> x0, waiting for transfers between devices: 238 us -> none  [the longest x1 66.6 us: on_device(): lax.psum_scatter(grad_ld.reshape(blocks, -1), 'dp', scatter_dimension=1,...]
    all_gather x6 -> x0, blocking collectives: 186 us -> none  [the longest x1 32.6 us: on_device(): lax.all_gather(gate_left, 'dp', axis=1, tiled=True)]
    unnamed x8 -> x0, waiting for transfers between devices: 134 us -> none
    pallas_call x0 -> x1, Pallas kernels: none -> 65.8 us  [layer(): pl.pallas_call(functools.partial(body, scale), out_shape=jax.ShapeDtypeSt...]
    dot_general x16 -> x0, matrix products: 40.1 us -> none  [the longest x1 8.77 us: on_device(): jnp.einsum('tjc,joc->tjo', down_return, left_down, preferred_element_type...]
    ppermute x0 -> x15, waiting for transfers between devices: none -> 34.7 us  [swap(): return lax.ppermute(v, axis, [(i, i ^ bit) for i in range(size)])]
    all_to_all x6 -> x0, starting transfers between devices: 21.3 us -> none  [the longest x1 4.09 us: on_device(): lax.all_to_all(jnp.transpose(up_back, (0, 2, 1)), 'blk', split_axis=1, co...]
    unnamed x48 -> x39, local copies, waits for them, and re-layouts: 24.7 us -> 8.14 us
  transfers between devices with their start and end apart: 12 -> 15, of which waited for: 7 -> 7; matrix products, arithmetic and copies ran while one was open for 8% -> 8% of each run, Pallas kernels for 0% -> 0%
where the time goes in v1:
time: 144 us
  Pallas kernels  65.8 us (46%)
  waiting for transfers between devices  34.7 us (24%)
  local copies, waits for them, and re-layouts  18.8 us (13%)
  starting transfers between devices  16 us (11%)
  other arithmetic  7.47 us (5%)
    pallas_call x1, Pallas kernels, layer(): pl.pallas_call(functools.partial(body, scale), out_shape=jax.ShapeDtypeSt...  65.8 us
    ppermute x15, waiting for transfers between devices, swap(): return lax.ppermute(v, axis, [(i, i ^ bit) for i in range(size)])  34.7 us
    ppermute x15, starting transfers between devices, swap(): return lax.ppermute(v, axis, [(i, i ^ bit) for i in range(size)])  16 us
    unnamed x39, local copies, waits for them, and re-layouts  8.14 us
    dynamic_slice x2, local copies, waits for them, and re-layouts, tokens_of(): sent = lax.dynamic_slice_in_dim(v, (1 - side) * half, half, 0)  3.34 us
    concatenate x2, other arithmetic, tokens_of(): return jnp.concatenate([first, second], axis=1)  3.09 us
  transfers between devices with their start and end apart: 15, of which 7 were waited for; matrix products, arithmetic and copies ran while one was open for 8% of the time, Pallas kernels for 0%

profile of v1, /device:TPU:0, one launch (start us, length us, event | category | flops | bytes accessed | tf_op | source)
XLA Modules:
  0.0 143.8 jit_solution(8438592449879238917)
XLA Ops:
  5.5 3.0 %collective-permute-start = (bf16[560,128]{1,0:T(8,128)(2,1)S(1)}, bf16[560,128]{1,0:T(8,128)(2,1)S(1)}, u32[]{:S(2)}, u32[]{:S(2)}) collective-permute-start(bf16[560,128]{1,0:T(8,128)(2,1)S(1)} %pad_maximum_fusion.2.refs_0_), channel_id=1, source_target_pairs={{0,2},{2,0},{4,6},{6,4},{8,10},{10,8},{12,14},{14,12},{1,3},{3,1},... | collective-permute-start | bytes 430088 | tf_op jit(solution)/shard_map/ppermute | solution.py:255
  8.5 1.6 %collective-permute-start.1 = (bf16[560,128]{1,0:T(8,128)(2,1)S(1)}, bf16[560,128]{1,0:T(8,128)(2,1)}, u32[]{:S(2)}, u32[]{:S(2)}) collective-permute-start(bf16[560,128]{1,0:T(8,128)(2,1)S(1)} %pad_maximum_fusion.2.refs_0_), channel_id=1, source_target_pairs={{0,4},{2,6},{4,0},{6,2},{8,12},{10,14},{12,8},{14,10},{1,5},{3,7},... | collective-permute-start | bytes 430088 | tf_op jit(solution)/shard_map/ppermute | solution.py:255
  10.0 2.6 %collective-permute-start.3 = (bf16[560,128]{1,0:T(8,128)(2,1)S(1)}, bf16[560,128]{1,0:T(8,128)(2,1)}, u32[]{:S(2)}, u32[]{:S(2)}) collective-permute-start(bf16[560,128]{1,0:T(8,128)(2,1)S(1)} %pad_maximum_fusion.2.refs_0_), channel_id=1, source_target_pairs={{0,8},{2,10},{4,12},{6,14},{8,0},{10,2},{12,4},{14,6},{1,9},{3,11}... | collective-permute-start | bytes 430088 | tf_op jit(solution)/shard_map/ppermute | solution.py:255
  12.8 2.3 %constant_dynamic-slice_fusion.1 = bf16[128,4096]{1,0:T(8,128)(2,1)} fusion(bf16[256,4096]{1,0:T(8,128)(2,1)} %param.9, s32[]{:T(128)S(6)} %select_n.68), kind=kLoop, calls=%fused_computation.43 | loop fusion | bytes 2097156 | tf_op jit(solution)/shard_map/dynamic_slice | solution.py:265
  15.1 1.1 constant_dynamic-slice_fusion
  18.6 5.1 %collective-permute-done.3.refs_4_ = bf16[560,128]{1,0:T(8,128)(2,1)} collective-permute-done((bf16[560,128]{1,0:T(8,128)(2,1)S(1)}, bf16[560,128]{1,0:T(8,128)(2,1)}, u32[]{:S(2)}, u32[]{:S(2)}) %collective-permute-start.3) | collective-permute-done | bytes 143392 | tf_op jit(solution)/shard_map/ppermute | solution.py:255
  24.2 1.5 %collective-permute-start.6 = (bf16[560,128]{1,0:T(8,128)(2,1)}, bf16[560,128]{1,0:T(8,128)(2,1)S(1)}, u32[]{:S(2)}, u32[]{:S(2)}) collective-permute-start(bf16[560,128]{1,0:T(8,128)(2,1)} %collective-permute-done.5.refs_6_), channel_id=1, source_target_pairs={{0,2},{2,0},{4,6},{6,4},{8,10},{10,8},{12,14},{14,12},{1,3},{3,1},... | collective-permute-start | bytes 430088 | tf_op jit(solution)/shard_map/ppermute | solution.py:255
  25.8 0.9 bitcast_dynamic-update-slice_fusion.5
  26.7 1.0 bitcast_dynamic-update-slice_fusion.3
  27.7 1.3 collective-permute-done.4.refs_5_
  29.0 1.0 bitcast_dynamic-update-slice_fusion.1
  30.7 1.1 broadcast_select_fusion.1
  31.8 1.5 %pad_maximum_fusion.refs_16_ = bf16[128,8192]{1,0:T(8,128)(2,1)} fusion(bf16[128,4096]{1,0:T(8,128)(2,1)S(1)} %get-tuple-element.37, bf16[128,4096]{1,0:T(8,128)(2,1)S(1)} %get-tuple-element.38), kind=kLoop, calls=%fused_computation.2 | loop fusion | flops 4194304 | bytes 4194304 | tf_op jit(solution)/shard_map/concatenate | solution.py:269
  33.3 1.6 %pad_maximum_fusion.1.refs_17_ = bf16[128,8192]{1,0:T(8,128)(2,1)} fusion(bf16[128,4096]{1,0:T(8,128)(2,1)S(1)} %get-tuple-element.19, bf16[128,4096]{1,0:T(8,128)(2,1)S(1)} %get-tuple-element.18), kind=kLoop, calls=%fused_computation.3 | loop fusion | flops 4194304 | bytes 4194304 | tf_op jit(solution)/shard_map/concatenate | solution.py:269
  34.9 1.1 slice_bitcast_fusion
  36.0 65.8 %shard_map.136 = bf16[2,8,560,128]{3,2,1,0:T(8,128)(2,1)} custom-call(s32[2]{0:T(128)} %pad_add_fusion.where, s32[64]{0:T(128)} %order.1, bf16[560,128]{1,0:T(8,128)(2,1)} %copy-done.5, bf16[560,128]{1,0:T(8,128)(2,1)} %copy-done.6, bf16[560,128]{1,0:T(8,128)(2,1)} %collective-permute-done.1.refs_2_, bf16[560,128]{1,0:T(8,128)(2,1)} %copy-done.7, ...), custom_call_target="tpu_custom_call" | custom-call | tf_op jit(solution)/shard_map/pallas_call | solution.py:230
  101.8 1.5 %dynamic-slice_bitcast_fusion = bf16[8,560,128]{2,1,0:T(8,128)(2,1)S(1)} fusion(bf16[2,8,560,128]{3,2,1,0:T(8,128)(2,1)} %shard_map.136, s32[]{:T(128)S(6)} %select_n.74), kind=kLoop, calls=%fused_computation.6 | loop fusion | bytes 2293764 | tf_op jit(solution)/shard_map/jit(dynamic_index_in_dim)/squeeze | solution.py:259
  103.8 2.6 %collective-permute-done.10 = bf16[8,560,128]{2,1,0:T(8,128)(2,1)} collective-permute-done((bf16[8,560,128]{2,1,0:T(8,128)(2,1)S(1)}, bf16[8,560,128]{2,1,0:T(8,128)(2,1)}, u32[]{:S(2)}, u32[]{:S(2)}) %collective-permute-start.10) | collective-permute-done | bytes 1146912 | tf_op jit(solution)/shard_map/ppermute | solution.py:255
  106.4 1.6 %fusion = bf16[8,560,128]{2,1,0:T(8,128)(2,1)S(1)} fusion(bf16[8,560,128]{2,1,0:T(8,128)(2,1)} %collective-permute-done.10, bf16[2,8,560,128]{3,2,1,0:T(8,128)(2,1)S(1)} %copy-done.1, s32[]{:T(128)S(6)} %select_n.73), kind=kLoop, calls=%fused_computation.1 | loop fusion | flops 2293760 | bytes 3440644 | tf_op jit(solution)/shard_map/convert_element_type | solution.py:296
  108.6 14.7 %collective-permute-done.11 = bf16[4,560,128]{2,1,0:T(8,128)(2,1)S(1)} collective-permute-done((bf16[4,560,128]{2,1,0:T(8,128)(2,1)S(1)}, bf16[4,560,128]{2,1,0:T(8,128)(2,1)S(1)}, u32[]{:S(2)}, u32[]{:S(2)}) %collective-permute-start.11) | collective-permute-done | bytes 573472 | tf_op jit(solution)/shard_map/ppermute | solution.py:255
  123.5 1.0 collective-permute-start.12
  124.5 3.1 %collective-permute-start.13 = (bf16[560,128]{1,0:T(8,128)(2,1)S(1)}, bf16[560,128]{1,0:T(8,128)(2,1)S(1)}, u32[]{:S(2)}, u32[]{:S(2)}) collective-permute-start(bf16[560,128]{1,0:T(8,128)(2,1)S(1)} %get-tuple-element.32), channel_id=1, source_target_pairs={{0,8},{2,10},{4,12},{6,14},{8,0},{10,2},{12,4},{14,6},{1,9},{3,11}... | collective-permute-start | bytes 430088 | tf_op jit(solution)/shard_map/ppermute | solution.py:255
  128.0 2.8 %collective-permute-done.12 = bf16[560,128]{1,0:T(8,128)(2,1)S(1)} collective-permute-done((bf16[560,128]{1,0:T(8,128)(2,1)S(1)}, bf16[560,128]{1,0:T(8,128)(2,1)S(1)}, u32[]{:S(2)}, u32[]{:S(2)}) %collective-permute-start.12) | collective-permute-done | bytes 143392 | tf_op jit(solution)/shard_map/ppermute | solution.py:255
  130.8 7.6 %collective-permute-done.13 = bf16[560,128]{1,0:T(8,128)(2,1)S(1)} collective-permute-done((bf16[560,128]{1,0:T(8,128)(2,1)S(1)}, bf16[560,128]{1,0:T(8,128)(2,1)S(1)}, u32[]{:S(2)}, u32[]{:S(2)}) %collective-permute-start.13) | collective-permute-done | bytes 143392 | tf_op jit(solution)/shard_map/ppermute | solution.py:255
  (92 shorter events, 15.6 us)
Async XLA Ops:
  0.6 4.2 %copy-start = (bf16[32,256]{1,0:T(8,128)(2,1)S(1)}, bf16[32,256]{1,0:T(8,128)(2,1)}, u32[]{:S(2)}) copy-start(bf16[32,256]{1,0:T(8,128)(2,1)} %param.17) | copy-start | bytes 49156
  0.6 3.8 %copy-start.12 = (bf16[32,448]{1,0:T(8,128)(2,1)S(1)}, bf16[32,448]{1,0:T(8,128)(2,1)}, u32[]{:S(2)}) copy-start(bf16[32,448]{1,0:T(8,128)(2,1)} %param.16) | copy-start | bytes 86020
  5.4 9.7 %copy-start.2 = (bf16[256,4096]{1,0:T(8,128)(2,1)S(1)}, bf16[256,4096]{1,0:T(8,128)(2,1)}, u32[]{:S(2)}) copy-start(bf16[256,4096]{1,0:T(8,128)(2,1)} %param.10) | copy-start | bytes 6291460
  5.4 10.8 %copy-start.5 = (bf16[560,128]{1,0:T(8,128)(2,1)}, bf16[560,128]{1,0:T(8,128)(2,1)S(1)}, u32[]{:S(2)}) copy-start(bf16[560,128]{1,0:T(8,128)(2,1)S(1)} %pad_maximum_fusion.2.refs_0_) | copy-start | bytes 430084
  5.5 12.2 %collective-permute-start = (bf16[560,128]{1,0:T(8,128)(2,1)S(1)}, bf16[560,128]{1,0:T(8,128)(2,1)S(1)}, u32[]{:S(2)}, u32[]{:S(2)}) collective-permute-start(bf16[560,128]{1,0:T(8,128)(2,1)S(1)} %pad_maximum_fusion.2.refs_0_), channel_id=1, source_target_pairs={{0,2},{2,0},{4,6},{6,4},{8,10},{10,8},{12,14},{14,12},{1,3},{3,1},... | collective-permute-start | bytes 430088 | tf_op jit(solution)/shard_map/ppermute | solution.py:255
  8.5 9.8 %collective-permute-start.1 = (bf16[560,128]{1,0:T(8,128)(2,1)S(1)}, bf16[560,128]{1,0:T(8,128)(2,1)}, u32[]{:S(2)}, u32[]{:S(2)}) collective-permute-start(bf16[560,128]{1,0:T(8,128)(2,1)S(1)} %pad_maximum_fusion.2.refs_0_), channel_id=1, source_target_pairs={{0,4},{2,6},{4,0},{6,2},{8,12},{10,14},{12,8},{14,10},{1,5},{3,7},... | collective-permute-start | bytes 430088 | tf_op jit(solution)/shard_map/ppermute | solution.py:255
  10.0 13.7 %collective-permute-start.3 = (bf16[560,128]{1,0:T(8,128)(2,1)S(1)}, bf16[560,128]{1,0:T(8,128)(2,1)}, u32[]{:S(2)}, u32[]{:S(2)}) collective-permute-start(bf16[560,128]{1,0:T(8,128)(2,1)S(1)} %pad_maximum_fusion.2.refs_0_), channel_id=1, source_target_pairs={{0,8},{2,10},{4,12},{6,14},{8,0},{10,2},{12,4},{14,6},{1,9},{3,11}... | collective-permute-start | bytes 430088 | tf_op jit(solution)/shard_map/ppermute | solution.py:255
  12.6 11.6 %collective-permute-start.5 = (bf16[560,128]{1,0:T(8,128)(2,1)S(1)}, bf16[560,128]{1,0:T(8,128)(2,1)}, u32[]{:S(2)}, u32[]{:S(2)}) collective-permute-start(bf16[560,128]{1,0:T(8,128)(2,1)S(1)} %pad_maximum_fusion.2.refs_0_), channel_id=1, source_target_pairs={{0,12},{2,14},{4,8},{6,10},{8,4},{10,6},{12,0},{14,2},{1,13},{3,15... | collective-permute-start | bytes 430088 | tf_op jit(solution)/shard_map/ppermute | solution.py:255
  15.1 15.5 %collective-permute-start.8 = (bf16[128,4096]{1,0:T(8,128)(2,1)}, bf16[128,4096]{1,0:T(8,128)(2,1)S(1)}, u32[]{:S(2)}, u32[]{:S(2)}) collective-permute-start(bf16[128,4096]{1,0:T(8,128)(2,1)} %constant_dynamic-slice_fusion.1), channel_id=1, source_target_pairs={{0,1},{1,0},{2,3},{3,2},{4,5},{5,4},{6,7},{7,6},{8,9},{9,8},{10,11... | collective-permute-start | bytes 3145736 | tf_op jit(solution)/shard_map/ppermute | solution.py:255
  16.8 13.9 %copy-start.3 = (bf16[256,4096]{1,0:T(8,128)(2,1)S(1)}, bf16[256,4096]{1,0:T(8,128)(2,1)}, u32[]{:S(2)}) copy-start(bf16[256,4096]{1,0:T(8,128)(2,1)} %param.9) | copy-start | bytes 6291460
  17.7 14.0 %copy-start.6 = (bf16[560,128]{1,0:T(8,128)(2,1)}, bf16[560,128]{1,0:T(8,128)(2,1)S(1)}, u32[]{:S(2)}) copy-start(bf16[560,128]{1,0:T(8,128)(2,1)S(1)} %collective-permute-done.refs_1_) | copy-start | bytes 430084
  17.7 13.0 %collective-permute-start.9 = (bf16[128,4096]{1,0:T(8,128)(2,1)}, bf16[128,4096]{1,0:T(8,128)(2,1)S(1)}, u32[]{:S(2)}, u32[]{:S(2)}) collective-permute-start(bf16[128,4096]{1,0:T(8,128)(2,1)} %constant_dynamic-slice_fusion), channel_id=1, source_target_pairs={{0,1},{1,0},{2,3},{3,2},{4,5},{5,4},{6,7},{7,6},{8,9},{9,8},{10,11... | collective-permute-start | bytes 3145736 | tf_op jit(solution)/shard_map/ppermute | solution.py:255
  18.3 8.4 %collective-permute-start.2 = (bf16[560,128]{1,0:T(8,128)(2,1)}, bf16[560,128]{1,0:T(8,128)(2,1)S(1)}, u32[]{:S(2)}, u32[]{:S(2)}) collective-permute-start(bf16[560,128]{1,0:T(8,128)(2,1)} %collective-permute-done.1.refs_2_), channel_id=1, source_target_pairs={{0,2},{2,0},{4,6},{6,4},{8,10},{10,8},{12,14},{14,12},{1,3},{3,1},... | collective-permute-start | bytes 430088 | tf_op jit(solution)/shard_map/ppermute | solution.py:255
  23.7 5.3 %collective-permute-start.4 = (bf16[560,128]{1,0:T(8,128)(2,1)}, bf16[560,128]{1,0:T(8,128)(2,1)S(1)}, u32[]{:S(2)}, u32[]{:S(2)}) collective-permute-start(bf16[560,128]{1,0:T(8,128)(2,1)} %collective-permute-done.3.refs_4_), channel_id=1, source_target_pairs={{0,2},{2,0},{4,6},{6,4},{8,10},{10,8},{12,14},{14,12},{1,3},{3,1},... | collective-permute-start | bytes 430088 | tf_op jit(solution)/shard_map/ppermute | solution.py:255
  24.2 6.3 %collective-permute-start.6 = (bf16[560,128]{1,0:T(8,128)(2,1)}, bf16[560,128]{1,0:T(8,128)(2,1)S(1)}, u32[]{:S(2)}, u32[]{:S(2)}) collective-permute-start(bf16[560,128]{1,0:T(8,128)(2,1)} %collective-permute-done.5.refs_6_), channel_id=1, source_target_pairs={{0,2},{2,0},{4,6},{6,4},{8,10},{10,8},{12,14},{14,12},{1,3},{3,1},... | collective-permute-start | bytes 430088 | tf_op jit(solution)/shard_map/ppermute | solution.py:255
  26.7 5.1 %copy-start.7 = (bf16[560,128]{1,0:T(8,128)(2,1)}, bf16[560,128]{1,0:T(8,128)(2,1)S(1)}, u32[]{:S(2)}) copy-start(bf16[560,128]{1,0:T(8,128)(2,1)S(1)} %collective-permute-done.2.refs_3_) | copy-start | bytes 430084
  29.0 2.8 %copy-start.8 = (bf16[560,128]{1,0:T(8,128)(2,1)}, bf16[560,128]{1,0:T(8,128)(2,1)S(1)}, u32[]{:S(2)}) copy-start(bf16[560,128]{1,0:T(8,128)(2,1)S(1)} %collective-permute-done.4.refs_5_) | copy-start | bytes 430084
  30.6 4.3 %collective-permute-start.7 = (bf16[8,560,128]{2,1,0:T(8,128)(2,1)S(1)}, bf16[8,560,128]{2,1,0:T(8,128)(2,1)S(1)}, u32[]{:S(2)}, u32[]{:S(2)}) collective-permute-start(bf16[8,560,128]{2,1,0:T(8,128)(2,1)S(1)} %bitcast_dynamic-update-slice_fusion), channel_id=1, source_target_pairs={{0,1},{1,0},{2,3},{3,2},{4,5},{5,4},{6,7},{7,6},{8,9},{9,8},{10,11... | collective-permute-start | bytes 3440648 | tf_op jit(solution)/shard_map/ppermute | solution.py:255
  101.8 4.6 %copy-start.1 = (bf16[2,8,560,128]{3,2,1,0:T(8,128)(2,1)S(1)}, bf16[2,8,560,128]{3,2,1,0:T(8,128)(2,1)}, u32[]{:S(2)}) copy-start(bf16[2,8,560,128]{3,2,1,0:T(8,128)(2,1)} %shard_map.136) | copy-start | bytes 6881284
  103.3 3.1 %collective-permute-start.10 = (bf16[8,560,128]{2,1,0:T(8,128)(2,1)S(1)}, bf16[8,560,128]{2,1,0:T(8,128)(2,1)}, u32[]{:S(2)}, u32[]{:S(2)}) collective-permute-start(bf16[8,560,128]{2,1,0:T(8,128)(2,1)S(1)} %dynamic-slice_bitcast_fusion), channel_id=1, source_target_pairs={{0,1},{1,0},{2,3},{3,2},{4,5},{5,4},{6,7},{7,6},{8,9},{9,8},{10,11... | collective-permute-start | bytes 3440648 | tf_op jit(solution)/shard_map/ppermute | solution.py:255
  108.0 15.3 %collective-permute-start.11 = (bf16[4,560,128]{2,1,0:T(8,128)(2,1)S(1)}, bf16[4,560,128]{2,1,0:T(8,128)(2,1)S(1)}, u32[]{:S(2)}, u32[]{:S(2)}) collective-permute-start(bf16[4,560,128]{2,1,0:T(8,128)(2,1)S(1)} %dynamic-slice_bitcast_fusion.1), channel_id=1, source_target_pairs={{0,2},{2,0},{4,6},{6,4},{8,10},{10,8},{12,14},{14,12},{1,3},{3,1},... | collective-permute-start | bytes 1720328 | tf_op jit(solution)/shard_map/ppermute | solution.py:255
  123.5 7.3 %collective-permute-start.12 = (bf16[560,128]{1,0:T(8,128)(2,1)S(1)}, bf16[560,128]{1,0:T(8,128)(2,1)S(1)}, u32[]{:S(2)}, u32[]{:S(2)}) collective-permute-start(bf16[560,128]{1,0:T(8,128)(2,1)S(1)} %get-tuple-element.30), channel_id=1, source_target_pairs={{0,4},{2,6},{4,0},{6,2},{8,12},{10,14},{12,8},{14,10},{1,5},{3,7},... | collective-permute-start | bytes 430088 | tf_op jit(solution)/shard_map/ppermute | solution.py:255
  124.5 13.9 %collective-permute-start.13 = (bf16[560,128]{1,0:T(8,128)(2,1)S(1)}, bf16[560,128]{1,0:T(8,128)(2,1)S(1)}, u32[]{:S(2)}, u32[]{:S(2)}) collective-permute-start(bf16[560,128]{1,0:T(8,128)(2,1)S(1)} %get-tuple-element.32), channel_id=1, source_target_pairs={{0,8},{2,10},{4,12},{6,14},{8,0},{10,2},{12,4},{14,6},{1,9},{3,11}... | collective-permute-start | bytes 430088 | tf_op jit(solution)/shard_map/ppermute | solution.py:255
  127.6 10.8 %collective-permute-start.14 = (bf16[560,128]{1,0:T(8,128)(2,1)S(1)}, bf16[560,128]{1,0:T(8,128)(2,1)S(1)}, u32[]{:S(2)}, u32[]{:S(2)}) collective-permute-start(bf16[560,128]{1,0:T(8,128)(2,1)S(1)} %get-tuple-element.31), channel_id=1, source_target_pairs={{0,12},{2,14},{4,8},{6,10},{8,4},{10,6},{12,0},{14,2},{1,13},{3,15... | collective-permute-start | bytes 430088 | tf_op jit(solution)/shard_map/ppermute | solution.py:255
  (5 other events, 7.0 us)

commit v2 on v1

--- a/solution.py
+++ b/solution.py
@@ -14,6 +14,7 @@
 BHID = 224
 WIDE = 256
 CHUNKS = 8
+GROUP = 8
 ROWS = 560
 f32 = jnp.float32
 bf16 = jnp.bfloat16
@@ -71,9 +72,13 @@
 def body(scale, where, order, *refs):
     weights = refs[:16]
     x_ref, y_ref, out_ref = refs[16:19]
-    (s_l, r_lo, r_hi, s_rd, d_lo, d_hi, inner, down, ret, act_s, slope_s, hid_s, stage) = refs[19:]
+    (s_l, r_lo, r_hi, s_rd, d_lo, d_hi, g_l, q_lo, q_hi, g_rd, e_lo, e_hi,
+     inner, back, down, ret, act_s, slope_s, hid_s, stage,
+     t_l, t_r, t_rd, t_ld) = refs[19:]
     s_r = (r_lo, r_hi)
     s_ld = (d_lo, d_hi)
+    g_r = (q_lo, q_hi)
+    g_ld = (e_lo, e_hi)
     toks = x_ref.shape[0]
     me = where[0]
     side = where[1]
@@ -112,86 +117,118 @@
     def lanes(j, width=BIN):
         return pl.ds(pl.multiple_of(j * width, width), width)
 
-    def first(j, _):
-        wg = s_l[pl.ds(j, RANK, stride=128), :]
-        wu = s_l[pl.ds(j + NB, RANK, stride=128), :]
-        w = jnp.concatenate([wg, wu], axis=0).astype(bf16)
-        got = rounded(nt(w, x_ref[:, lanes(j)]))
-        at = pl.multiple_of(j * RANK, RANK)
-        inner[pl.ds(at, RANK), :] = got[:RANK]
-        inner[pl.ds(1024 + at, RANK), :] = got[RANK:]
-        return 0
-
-    lax.fori_loop(0, NB, first, 0, unroll=4)
-
-    def mixed_of(m):
+    def rows(j, height=RANK):
+        return pl.ds(pl.multiple_of(j * height, height), height)
+
+    slot = lax.broadcasted_iota(jnp.int32, (1, 128), 1) // RANK
+    masks = [jnp.where(slot == u, 1.0, 0.0).astype(bf16) for u in range(GROUP)]
+
+    def stacked(ref, start, stride, g):
         return jnp.concatenate(
-            [inner[pl.ds(m, RANK, stride=NB), :], inner[pl.ds(1024 + m, RANK, stride=NB), :]], axis=0
+            [ref[pl.ds(start + g * GROUP + u, RANK, stride=stride), :] for u in range(GROUP)], axis=0
         )
 
-    zeros = jnp.zeros((RANK, WIDE), bf16)
-
-    def second(k, _):
-        m = order[k]
-        mixed = mixed_of(m).T.astype(bf16)
-        wg = wide(s_r, k, 128)
-        wu = wide(s_r, k + NB, 128)
-        gate = nn(mixed, jnp.concatenate([wg, zeros], axis=0))
-        upper = nn(mixed, jnp.concatenate([zeros, wu], axis=0))
-        sig = 1.0 / (1.0 + jnp.exp(-gate))
-        act = gate * sig
-        hidden = (act * upper).astype(bf16)
-        act_s[k] = act
-        slope_s[k] = upper * sig * (1.0 + gate * (1.0 - sig))
-        hid_s[k] = hidden
-        wl = wide(s_ld, k, NB)
-        down[pl.ds(pl.multiple_of(k * RANK, RANK), RANK), :] = rounded(nt(wl, hidden))
-        return 0
-
-    lax.fori_loop(0, NB, second, 0, unroll=2)
-
-    def third(k, _):
-        m = order[k]
-        dm = down[pl.ds(m, RANK, stride=NB), :]
-        wr = s_rd[pl.ds(k, RANK, stride=NB), :].astype(bf16)
-        student = nn(dm.T.astype(bf16), wr)
-        delta = ((student - y_ref[:, lanes(k)].astype(f32)) * scale).astype(bf16)
-        back = rounded(nt(wr, delta))
-        s_rd[pl.ds(k, RANK, stride=NB), :] = nn(dm.astype(bf16), delta)
-        ret[pl.ds(m, RANK, stride=NB), :] = back
-        return 0
-
-    lax.fori_loop(0, NB, third, 0, unroll=2)
-
-    def fourth(j, _):
-        m = order[j]
-        dr = ret[pl.ds(pl.multiple_of(j * RANK, RANK), RANK), :]
-        wl = wide(s_ld, j, NB)
-        dhidden = nn(dr.T.astype(bf16), wl)
-        widen(s_ld, j, NB, nn(dr.astype(bf16), hid_s[j]))
-        dgate = (dhidden * slope_s[j]).astype(bf16)
-        dup = (dhidden * act_s[j]).astype(bf16)
-        gm = inner[pl.ds(m, RANK, stride=NB), :].astype(bf16)
-        um = inner[pl.ds(1024 + m, RANK, stride=NB), :].astype(bf16)
-        wg = wide(s_r, j, 128)
-        wu = wide(s_r, j + NB, 128)
-        inner[pl.ds(m, RANK, stride=NB), :] = rounded(nt(wg, dgate))
-        inner[pl.ds(1024 + m, RANK, stride=NB), :] = rounded(nt(wu, dup))
-        widen(s_r, j, 128, nn(gm, dgate))
-        widen(s_r, j + NB, 128, nn(um, dup))
-        return 0
-
-    lax.fori_loop(0, NB, fourth, 0, unroll=2)
-
-    def fifth(j, _):
-        at = pl.multiple_of(j * RANK, RANK)
-        back = jnp.concatenate([inner[pl.ds(at, RANK), :], inner[pl.ds(1024 + at, RANK), :]], axis=0)
-        grads = nn(back.astype(bf16), x_ref[:, lanes(j)])
-        s_l[pl.ds(j, RANK, stride=128), :] = grads[:RANK]
-        s_l[pl.ds(j + NB, RANK, stride=128), :] = grads[RANK:]
-        return 0
-
-    lax.fori_loop(0, NB, fifth, 0, unroll=4)
+    def turn(g, _):
+        for gu in range(2):
+            t_l[gu, g] = stacked(s_l, gu * NB, 128, g).T.astype(bf16)
+            for h in range(2):
+                t_r[gu, g, pl.ds(h * 128, 128), :] = stacked(s_r[h], gu * NB, 128, g).T.astype(bf16)
+        for h in range(2):
+            t_ld[g, pl.ds(h * 128, 128), :] = stacked(s_ld[h], 0, NB, g).T.astype(bf16)
+        t_rd[g] = stacked(s_rd, 0, NB, g).T.astype(bf16)
+        return 0
+
+    lax.fori_loop(0, NB // GROUP, turn, 0)
+
+    def blocks(g):
+        return [(u, g * GROUP + u) for u in range(GROUP)]
+
+    def first(g, _):
+        for gu in range(2):
+            total = jnp.zeros((toks, 128), f32)
+            for u, j in blocks(g):
+                total += nn(x_ref[:, lanes(j)], t_l[gu, g] * masks[u])
+            inner[rows(gu * GROUP + g, 128), :] = rounded(total.T)
+        return 0
+
+    lax.fori_loop(0, NB // GROUP, first, 0)
+
+    def second(g, _):
+        turned = []
+        for gu in range(2):
+            mixed = [inner[pl.ds(gu * 1024 + order[k], RANK, stride=NB), :] for u, k in blocks(g)]
+            turned.append(jnp.concatenate(mixed, axis=0).T.astype(bf16))
+        for u, k in blocks(g):
+            at = u * RANK
+            act_s[k] = nn(turned[0][:, at : at + RANK], wide(s_r, k, 128))
+            slope_s[k] = nn(turned[1][:, at : at + RANK], wide(s_r, k + NB, 128))
+        for u, k in blocks(g):
+            gate, upper = act_s[k], slope_s[k]
+            sig = 0.5 * jnp.tanh(0.5 * gate) + 0.5
+            act = gate * sig
+            act_s[k] = act
+            slope_s[k] = upper * (sig + act * (1.0 - sig))
+            hid_s[k] = (act * upper).astype(bf16)
+        total = jnp.zeros((toks, 128), f32)
+        for u, k in blocks(g):
+            total += nn(hid_s[k], t_ld[g] * masks[u])
+        down[rows(g, 128), :] = rounded(total.T)
+        return 0
+
+    lax.fori_loop(0, NB // GROUP, second, 0)
+
+    def third(g, _):
+        dms = [down[pl.ds(order[k], RANK, stride=NB), :] for u, k in blocks(g)]
+        turned = jnp.concatenate(dms, axis=0).T.astype(bf16)
+        deltas = []
+        for u, k in blocks(g):
+            wr = s_rd[pl.ds(k, RANK, stride=NB), :].astype(bf16)
+            student = nn(turned[:, u * RANK : (u + 1) * RANK], wr)
+            deltas.append(((student - y_ref[:, lanes(k)].astype(f32)) * scale).astype(bf16))
+        total = jnp.zeros((toks, 128), f32)
+        for u, k in blocks(g):
+            total += nn(deltas[u], t_rd[g] * masks[u])
+        for u, k in blocks(g):
+            g_rd[pl.ds(k, RANK, stride=NB), :] = nn(dms[u].astype(bf16), deltas[u])
+        total = rounded(total.T)
+        for u, k in blocks(g):
+            ret[pl.ds(order[k], RANK, stride=NB), :] = total[u * RANK : (u + 1) * RANK]
+        return 0
+
+    lax.fori_loop(0, NB // GROUP, third, 0)
+
+    def fourth(g, _):
+        returned = ret[rows(g, 128), :]
+        turned = returned.T.astype(bf16)
+        for u, j in blocks(g):
+            widen(g_ld, j, NB, nn(returned[u * RANK : (u + 1) * RANK].astype(bf16), hid_s[j]))
+        sent = []
+        for u, j in blocks(g):
+            dhidden = nn(turned[:, u * RANK : (u + 1) * RANK], wide(s_ld, j, NB))
+            sent.append(((dhidden * slope_s[j]).astype(bf16), (dhidden * act_s[j]).astype(bf16)))
+        for gu in range(2):
+            total = jnp.zeros((toks, 128), f32)
+            for u, j in blocks(g):
+                total += nn(sent[u][gu], t_r[gu, g] * masks[u])
+            total = rounded(total.T)
+            for u, j in blocks(g):
+                back[pl.ds(gu * 1024 + order[j], RANK, stride=NB), :] = total[u * RANK : (u + 1) * RANK]
+            for u, j in blocks(g):
+                mixed = inner[pl.ds(gu * 1024 + order[j], RANK, stride=NB), :].astype(bf16)
+                widen(g_r, j + gu * NB, 128, nn(mixed, sent[u][gu]))
+        return 0
+
+    lax.fori_loop(0, NB // GROUP, fourth, 0)
+
+    def fifth(g, _):
+        for u, j in blocks(g):
+            both = jnp.concatenate([back[rows(j), :], back[rows(j + NB), :]], axis=0)
+            grads = nn(both.astype(bf16), x_ref[:, lanes(j)])
+            g_l[pl.ds(j, RANK, stride=128), :] = grads[:RANK]
+            g_l[pl.ds(j + NB, RANK, stride=128), :] = grads[RANK:]
+        return 0
+
+    lax.fori_loop(0, NB // GROUP, fifth, 0)
 
     for blk in range(2):
         for c8 in range(8):
@@ -199,14 +236,14 @@
             for ch in range(2):
                 for gu in range(2):
                     row = (ch * 8 + c8) * 128 + gu * NB + blk * HALF
-                    parts.append(s_l[pl.ds(row, HALF), :])
+                    parts.append(g_l[pl.ds(row, HALF), :])
             stage[pl.ds(c8, 128, stride=8), :] = jnp.concatenate(parts, axis=0).T
         for c4 in range(4):
             p0, p1 = [], []
             for cq in range(4):
                 row = (cq * 4 + c4) * NB + blk * HALF
-                p0.append(d_lo[pl.ds(row, HALF), :])
-                p1.append(d_hi[pl.ds(row, HALF), :])
+                p0.append(e_lo[pl.ds(row, HALF), :])
+                p1.append(e_hi[pl.ds(row, HALF), :])
             stage[pl.ds(1024 + c4, 128, stride=4), :] = jnp.concatenate(p0, axis=0).T
             stage[pl.ds(1024 + 512 + c4, 96, stride=4), :] = jnp.concatenate(p1, axis=0).T[:96]
         for d in range(CHUNKS):
@@ -217,10 +254,10 @@
                     row = (2 * d + al) * 128 + gu * NB + blk * HALF
                     for half in range(2):
                         at = R_AT + half * 128 + gu * 64 + al * HALF
-                        out_ref[blk, d, pl.ds(at, HALF), :] = s_r[half][pl.ds(row, HALF), :].astype(bf16)
+                        out_ref[blk, d, pl.ds(at, HALF), :] = g_r[half][pl.ds(row, HALF), :].astype(bf16)
             for al in range(2):
                 row = (2 * d + al) * NB + blk * HALF
-                out_ref[blk, d, pl.ds(RD_AT + al * HALF, HALF), :] = s_rd[pl.ds(row, HALF), :].astype(bf16)
+                out_ref[blk, d, pl.ds(RD_AT + al * HALF, HALF), :] = g_rd[pl.ds(row, HALF), :].astype(bf16)
 
 
 def layer(scale, where, order, weights, x, y):
@@ -239,6 +276,13 @@
             pltpu.VMEM((RANK * NB, BIN), f32),
             pltpu.VMEM((RANK * NB, 128), f32),
             pltpu.VMEM((RANK * NB, 128), f32),
+            pltpu.VMEM((RANK * 128, BIN), f32),
+            pltpu.VMEM((RANK * 128, 128), f32),
+            pltpu.VMEM((RANK * 128, 128), f32),
+            pltpu.VMEM((RANK * NB, BIN), f32),
+            pltpu.VMEM((RANK * NB, 128), f32),
+            pltpu.VMEM((RANK * NB, 128), f32),
+            pltpu.VMEM((2 * NB * RANK, toks), f32),
             pltpu.VMEM((2 * NB * RANK, toks), f32),
             pltpu.VMEM((NB * RANK, toks), f32),
             pltpu.VMEM((NB * RANK, toks), f32),
@@ -246,6 +290,10 @@
             pltpu.VMEM((NB, toks, WIDE), f32),
             pltpu.VMEM((NB, toks, WIDE), bf16),
             pltpu.VMEM((1024 + 896, 128), f32),
+            pltpu.VMEM((2, NB // GROUP, BIN, 128), bf16),
+            pltpu.VMEM((2, NB // GROUP, WIDE, 128), bf16),
+            pltpu.VMEM((NB // GROUP, BIN, 128), bf16),
+            pltpu.VMEM((NB // GROUP, WIDE, 128), bf16),
         ],
         compiler_params=pltpu.CompilerParams(vmem_limit_bytes=56 * 2**20),
     )(where, order, *weights, x, y)

time: 144 us -> 116 us (0.81)
  Pallas kernels: 65.8 us -> 37.8 us
    pallas_call x1, Pallas kernels: 65.8 us -> 37.8 us  [layer(): pl.pallas_call(functools.partial(body, scale), out_shape=jax.ShapeDtypeSt...]
  transfers between devices with their start and end apart: 15 -> 15, of which waited for: 7 -> 7; matrix products, arithmetic and copies ran while one was open for 8% -> 10% of each run, Pallas kernels for 0% -> 0%
where the time goes in v2:
time: 116 us
  Pallas kernels  37.8 us (33%)
  waiting for transfers between devices  34.7 us (30%)
  local copies, waits for them, and re-layouts  18.8 us (16%)
  starting transfers between devices  16 us (14%)
  other arithmetic  7.47 us (6%)
    pallas_call x1, Pallas kernels, layer(): pl.pallas_call(functools.partial(body, scale), out_shape=jax.ShapeDtypeSt...  37.8 us
    ppermute x15, waiting for transfers between devices, swap(): return lax.ppermute(v, axis, [(i, i ^ bit) for i in range(size)])  34.7 us
    ppermute x15, starting transfers between devices, swap(): return lax.ppermute(v, axis, [(i, i ^ bit) for i in range(size)])  16 us
    unnamed x39, local copies, waits for them, and re-layouts  8.14 us
    dynamic_slice x2, local copies, waits for them, and re-layouts, tokens_of(): sent = lax.dynamic_slice_in_dim(v, (1 - side) * half, half, 0)  3.34 us
    concatenate x2, other arithmetic, tokens_of(): return jnp.concatenate([first, second], axis=1)  3.09 us
  transfers between devices with their start and end apart: 15, of which 7 were waited for; matrix products, arithmetic and copies ran while one was open for 10% of the time, Pallas kernels for 0%

profile of v2, /device:TPU:0, one launch (start us, length us, event | category | flops | bytes accessed | tf_op | source)
XLA Modules:
  0.0 115.8 jit_solution(9448808029518617120)
XLA Ops:
  5.5 3.0 %collective-permute-start = (bf16[560,128]{1,0:T(8,128)(2,1)S(1)}, bf16[560,128]{1,0:T(8,128)(2,1)S(1)}, u32[]{:S(2)}, u32[]{:S(2)}) collective-permute-start(bf16[560,128]{1,0:T(8,128)(2,1)S(1)} %pad_maximum_fusion.2.refs_0_), channel_id=1, source_target_pairs={{0,2},{2,0},{4,6},{6,4},{8,10},{10,8},{12,14},{14,12},{1,3},{3,1},... | collective-permute-start | bytes 430088 | tf_op jit(solution)/shard_map/ppermute | solution.py:303
  8.5 1.6 %collective-permute-start.1 = (bf16[560,128]{1,0:T(8,128)(2,1)S(1)}, bf16[560,128]{1,0:T(8,128)(2,1)}, u32[]{:S(2)}, u32[]{:S(2)}) collective-permute-start(bf16[560,128]{1,0:T(8,128)(2,1)S(1)} %pad_maximum_fusion.2.refs_0_), channel_id=1, source_target_pairs={{0,4},{2,6},{4,0},{6,2},{8,12},{10,14},{12,8},{14,10},{1,5},{3,7},... | collective-permute-start | bytes 430088 | tf_op jit(solution)/shard_map/ppermute | solution.py:303
  10.0 2.6 %collective-permute-start.3 = (bf16[560,128]{1,0:T(8,128)(2,1)S(1)}, bf16[560,128]{1,0:T(8,128)(2,1)}, u32[]{:S(2)}, u32[]{:S(2)}) collective-permute-start(bf16[560,128]{1,0:T(8,128)(2,1)S(1)} %pad_maximum_fusion.2.refs_0_), channel_id=1, source_target_pairs={{0,8},{2,10},{4,12},{6,14},{8,0},{10,2},{12,4},{14,6},{1,9},{3,11}... | collective-permute-start | bytes 430088 | tf_op jit(solution)/shard_map/ppermute | solution.py:303
  12.8 2.3 %constant_dynamic-slice_fusion.1 = bf16[128,4096]{1,0:T(8,128)(2,1)} fusion(bf16[256,4096]{1,0:T(8,128)(2,1)} %param.9, s32[]{:T(128)S(6)} %select_n.68), kind=kLoop, calls=%fused_computation.43 | loop fusion | bytes 2097156 | tf_op jit(solution)/shard_map/dynamic_slice | solution.py:313
  15.1 1.1 constant_dynamic-slice_fusion
  18.6 5.1 %collective-permute-done.3.refs_4_ = bf16[560,128]{1,0:T(8,128)(2,1)} collective-permute-done((bf16[560,128]{1,0:T(8,128)(2,1)S(1)}, bf16[560,128]{1,0:T(8,128)(2,1)}, u32[]{:S(2)}, u32[]{:S(2)}) %collective-permute-start.3) | collective-permute-done | bytes 143392 | tf_op jit(solution)/shard_map/ppermute | solution.py:303
  24.2 1.5 %collective-permute-start.6 = (bf16[560,128]{1,0:T(8,128)(2,1)}, bf16[560,128]{1,0:T(8,128)(2,1)S(1)}, u32[]{:S(2)}, u32[]{:S(2)}) collective-permute-start(bf16[560,128]{1,0:T(8,128)(2,1)} %collective-permute-done.5.refs_6_), channel_id=1, source_target_pairs={{0,2},{2,0},{4,6},{6,4},{8,10},{10,8},{12,14},{14,12},{1,3},{3,1},... | collective-permute-start | bytes 430088 | tf_op jit(solution)/shard_map/ppermute | solution.py:303
  25.8 0.9 bitcast_dynamic-update-slice_fusion.5
  26.7 1.0 bitcast_dynamic-update-slice_fusion.3
  27.7 1.3 %collective-permute-done.4.refs_5_ = bf16[560,128]{1,0:T(8,128)(2,1)S(1)} collective-permute-done((bf16[560,128]{1,0:T(8,128)(2,1)}, bf16[560,128]{1,0:T(8,128)(2,1)S(1)}, u32[]{:S(2)}, u32[]{:S(2)}) %collective-permute-start.4) | collective-permute-done | bytes 143392 | tf_op jit(solution)/shard_map/ppermute | solution.py:303
  29.0 1.0 bitcast_dynamic-update-slice_fusion.1
  30.7 1.1 broadcast_select_fusion.1
  31.8 1.5 %pad_maximum_fusion.refs_16_ = bf16[128,8192]{1,0:T(8,128)(2,1)} fusion(bf16[128,4096]{1,0:T(8,128)(2,1)S(1)} %get-tuple-element.37, bf16[128,4096]{1,0:T(8,128)(2,1)S(1)} %get-tuple-element.38), kind=kLoop, calls=%fused_computation.2 | loop fusion | flops 4194304 | bytes 4194304 | tf_op jit(solution)/shard_map/concatenate | solution.py:317
  33.3 1.6 %pad_maximum_fusion.1.refs_17_ = bf16[128,8192]{1,0:T(8,128)(2,1)} fusion(bf16[128,4096]{1,0:T(8,128)(2,1)S(1)} %get-tuple-element.19, bf16[128,4096]{1,0:T(8,128)(2,1)S(1)} %get-tuple-element.18), kind=kLoop, calls=%fused_computation.3 | loop fusion | flops 4194304 | bytes 4194304 | tf_op jit(solution)/shard_map/concatenate | solution.py:317
  34.9 1.1 slice_bitcast_fusion
  36.0 37.8 %shard_map.136 = bf16[2,8,560,128]{3,2,1,0:T(8,128)(2,1)} custom-call(s32[2]{0:T(128)} %pad_add_fusion.where, s32[64]{0:T(128)} %order.1, bf16[560,128]{1,0:T(8,128)(2,1)} %copy-done.5, bf16[560,128]{1,0:T(8,128)(2,1)} %copy-done.6, bf16[560,128]{1,0:T(8,128)(2,1)} %collective-permute-done.1.refs_2_, bf16[560,128]{1,0:T(8,128)(2,1)} %copy-done.7, ...), custom_call_target="tpu_custom_call" | custom-call | tf_op jit(solution)/shard_map/pallas_call | solution.py:267
  73.8 1.5 %dynamic-slice_bitcast_fusion = bf16[8,560,128]{2,1,0:T(8,128)(2,1)S(1)} fusion(bf16[2,8,560,128]{3,2,1,0:T(8,128)(2,1)} %shard_map.136, s32[]{:T(128)S(6)} %select_n.74), kind=kLoop, calls=%fused_computation.6 | loop fusion | bytes 2293764 | tf_op jit(solution)/shard_map/jit(dynamic_index_in_dim)/squeeze | solution.py:307
  75.8 2.6 %collective-permute-done.10 = bf16[8,560,128]{2,1,0:T(8,128)(2,1)} collective-permute-done((bf16[8,560,128]{2,1,0:T(8,128)(2,1)S(1)}, bf16[8,560,128]{2,1,0:T(8,128)(2,1)}, u32[]{:S(2)}, u32[]{:S(2)}) %collective-permute-start.10) | collective-permute-done | bytes 1146912 | tf_op jit(solution)/shard_map/ppermute | solution.py:303
  78.4 1.6 %fusion = bf16[8,560,128]{2,1,0:T(8,128)(2,1)S(1)} fusion(bf16[8,560,128]{2,1,0:T(8,128)(2,1)} %collective-permute-done.10, bf16[2,8,560,128]{3,2,1,0:T(8,128)(2,1)S(1)} %copy-done.1, s32[]{:T(128)S(6)} %select_n.73), kind=kLoop, calls=%fused_computation.1 | loop fusion | flops 2293760 | bytes 3440644 | tf_op jit(solution)/shard_map/convert_element_type | solution.py:344
  80.6 14.7 %collective-permute-done.11 = bf16[4,560,128]{2,1,0:T(8,128)(2,1)S(1)} collective-permute-done((bf16[4,560,128]{2,1,0:T(8,128)(2,1)S(1)}, bf16[4,560,128]{2,1,0:T(8,128)(2,1)S(1)}, u32[]{:S(2)}, u32[]{:S(2)}) %collective-permute-start.11) | collective-permute-done | bytes 573472 | tf_op jit(solution)/shard_map/ppermute | solution.py:303
  95.5 1.0 collective-permute-start.12
  96.5 3.1 %collective-permute-start.13 = (bf16[560,128]{1,0:T(8,128)(2,1)S(1)}, bf16[560,128]{1,0:T(8,128)(2,1)S(1)}, u32[]{:S(2)}, u32[]{:S(2)}) collective-permute-start(bf16[560,128]{1,0:T(8,128)(2,1)S(1)} %get-tuple-element.32), channel_id=1, source_target_pairs={{0,8},{2,10},{4,12},{6,14},{8,0},{10,2},{12,4},{14,6},{1,9},{3,11}... | collective-permute-start | bytes 430088 | tf_op jit(solution)/shard_map/ppermute | solution.py:303
  100.0 2.8 %collective-permute-done.12 = bf16[560,128]{1,0:T(8,128)(2,1)S(1)} collective-permute-done((bf16[560,128]{1,0:T(8,128)(2,1)S(1)}, bf16[560,128]{1,0:T(8,128)(2,1)S(1)}, u32[]{:S(2)}, u32[]{:S(2)}) %collective-permute-start.12) | collective-permute-done | bytes 143392 | tf_op jit(solution)/shard_map/ppermute | solution.py:303
  102.8 7.6 %collective-permute-done.13 = bf16[560,128]{1,0:T(8,128)(2,1)S(1)} collective-permute-done((bf16[560,128]{1,0:T(8,128)(2,1)S(1)}, bf16[560,128]{1,0:T(8,128)(2,1)S(1)}, u32[]{:S(2)}, u32[]{:S(2)}) %collective-permute-start.13) | collective-permute-done | bytes 143392 | tf_op jit(solution)/shard_map/ppermute | solution.py:303
  (92 shorter events, 15.6 us)
Async XLA Ops:
  0.6 4.2 %copy-start = (bf16[32,256]{1,0:T(8,128)(2,1)S(1)}, bf16[32,256]{1,0:T(8,128)(2,1)}, u32[]{:S(2)}) copy-start(bf16[32,256]{1,0:T(8,128)(2,1)} %param.17) | copy-start | bytes 49156
  0.6 3.8 %copy-start.12 = (bf16[32,448]{1,0:T(8,128)(2,1)S(1)}, bf16[32,448]{1,0:T(8,128)(2,1)}, u32[]{:S(2)}) copy-start(bf16[32,448]{1,0:T(8,128)(2,1)} %param.16) | copy-start | bytes 86020
  5.4 9.7 %copy-start.2 = (bf16[256,4096]{1,0:T(8,128)(2,1)S(1)}, bf16[256,4096]{1,0:T(8,128)(2,1)}, u32[]{:S(2)}) copy-start(bf16[256,4096]{1,0:T(8,128)(2,1)} %param.10) | copy-start | bytes 6291460
  5.4 10.8 %copy-start.5 = (bf16[560,128]{1,0:T(8,128)(2,1)}, bf16[560,128]{1,0:T(8,128)(2,1)S(1)}, u32[]{:S(2)}) copy-start(bf16[560,128]{1,0:T(8,128)(2,1)S(1)} %pad_maximum_fusion.2.refs_0_) | copy-start | bytes 430084
  5.5 12.2 %collective-permute-start = (bf16[560,128]{1,0:T(8,128)(2,1)S(1)}, bf16[560,128]{1,0:T(8,128)(2,1)S(1)}, u32[]{:S(2)}, u32[]{:S(2)}) collective-permute-start(bf16[560,128]{1,0:T(8,128)(2,1)S(1)} %pad_maximum_fusion.2.refs_0_), channel_id=1, source_target_pairs={{0,2},{2,0},{4,6},{6,4},{8,10},{10,8},{12,14},{14,12},{1,3},{3,1},... | collective-permute-start | bytes 430088 | tf_op jit(solution)/shard_map/ppermute | solution.py:303
  8.5 9.8 %collective-permute-start.1 = (bf16[560,128]{1,0:T(8,128)(2,1)S(1)}, bf16[560,128]{1,0:T(8,128)(2,1)}, u32[]{:S(2)}, u32[]{:S(2)}) collective-permute-start(bf16[560,128]{1,0:T(8,128)(2,1)S(1)} %pad_maximum_fusion.2.refs_0_), channel_id=1, source_target_pairs={{0,4},{2,6},{4,0},{6,2},{8,12},{10,14},{12,8},{14,10},{1,5},{3,7},... | collective-permute-start | bytes 430088 | tf_op jit(solution)/shard_map/ppermute | solution.py:303
  10.0 13.7 %collective-permute-start.3 = (bf16[560,128]{1,0:T(8,128)(2,1)S(1)}, bf16[560,128]{1,0:T(8,128)(2,1)}, u32[]{:S(2)}, u32[]{:S(2)}) collective-permute-start(bf16[560,128]{1,0:T(8,128)(2,1)S(1)} %pad_maximum_fusion.2.refs_0_), channel_id=1, source_target_pairs={{0,8},{2,10},{4,12},{6,14},{8,0},{10,2},{12,4},{14,6},{1,9},{3,11}... | collective-permute-start | bytes 430088 | tf_op jit(solution)/shard_map/ppermute | solution.py:303
  12.6 11.6 %collective-permute-start.5 = (bf16[560,128]{1,0:T(8,128)(2,1)S(1)}, bf16[560,128]{1,0:T(8,128)(2,1)}, u32[]{:S(2)}, u32[]{:S(2)}) collective-permute-start(bf16[560,128]{1,0:T(8,128)(2,1)S(1)} %pad_maximum_fusion.2.refs_0_), channel_id=1, source_target_pairs={{0,12},{2,14},{4,8},{6,10},{8,4},{10,6},{12,0},{14,2},{1,13},{3,15... | collective-permute-start | bytes 430088 | tf_op jit(solution)/shard_map/ppermute | solution.py:303
  15.1 15.5 %collective-permute-start.8 = (bf16[128,4096]{1,0:T(8,128)(2,1)}, bf16[128,4096]{1,0:T(8,128)(2,1)S(1)}, u32[]{:S(2)}, u32[]{:S(2)}) collective-permute-start(bf16[128,4096]{1,0:T(8,128)(2,1)} %constant_dynamic-slice_fusion.1), channel_id=1, source_target_pairs={{0,1},{1,0},{2,3},{3,2},{4,5},{5,4},{6,7},{7,6},{8,9},{9,8},{10,11... | collective-permute-start | bytes 3145736 | tf_op jit(solution)/shard_map/ppermute | solution.py:303
  16.8 13.9 %copy-start.3 = (bf16[256,4096]{1,0:T(8,128)(2,1)S(1)}, bf16[256,4096]{1,0:T(8,128)(2,1)}, u32[]{:S(2)}) copy-start(bf16[256,4096]{1,0:T(8,128)(2,1)} %param.9) | copy-start | bytes 6291460
  17.7 14.0 %copy-start.6 = (bf16[560,128]{1,0:T(8,128)(2,1)}, bf16[560,128]{1,0:T(8,128)(2,1)S(1)}, u32[]{:S(2)}) copy-start(bf16[560,128]{1,0:T(8,128)(2,1)S(1)} %collective-permute-done.refs_1_) | copy-start | bytes 430084
  17.7 13.0 %collective-permute-start.9 = (bf16[128,4096]{1,0:T(8,128)(2,1)}, bf16[128,4096]{1,0:T(8,128)(2,1)S(1)}, u32[]{:S(2)}, u32[]{:S(2)}) collective-permute-start(bf16[128,4096]{1,0:T(8,128)(2,1)} %constant_dynamic-slice_fusion), channel_id=1, source_target_pairs={{0,1},{1,0},{2,3},{3,2},{4,5},{5,4},{6,7},{7,6},{8,9},{9,8},{10,11... | collective-permute-start | bytes 3145736 | tf_op jit(solution)/shard_map/ppermute | solution.py:303
  18.3 8.4 %collective-permute-start.2 = (bf16[560,128]{1,0:T(8,128)(2,1)}, bf16[560,128]{1,0:T(8,128)(2,1)S(1)}, u32[]{:S(2)}, u32[]{:S(2)}) collective-permute-start(bf16[560,128]{1,0:T(8,128)(2,1)} %collective-permute-done.1.refs_2_), channel_id=1, source_target_pairs={{0,2},{2,0},{4,6},{6,4},{8,10},{10,8},{12,14},{14,12},{1,3},{3,1},... | collective-permute-start | bytes 430088 | tf_op jit(solution)/shard_map/ppermute | solution.py:303
  23.7 5.3 %collective-permute-start.4 = (bf16[560,128]{1,0:T(8,128)(2,1)}, bf16[560,128]{1,0:T(8,128)(2,1)S(1)}, u32[]{:S(2)}, u32[]{:S(2)}) collective-permute-start(bf16[560,128]{1,0:T(8,128)(2,1)} %collective-permute-done.3.refs_4_), channel_id=1, source_target_pairs={{0,2},{2,0},{4,6},{6,4},{8,10},{10,8},{12,14},{14,12},{1,3},{3,1},... | collective-permute-start | bytes 430088 | tf_op jit(solution)/shard_map/ppermute | solution.py:303
  24.2 6.3 %collective-permute-start.6 = (bf16[560,128]{1,0:T(8,128)(2,1)}, bf16[560,128]{1,0:T(8,128)(2,1)S(1)}, u32[]{:S(2)}, u32[]{:S(2)}) collective-permute-start(bf16[560,128]{1,0:T(8,128)(2,1)} %collective-permute-done.5.refs_6_), channel_id=1, source_target_pairs={{0,2},{2,0},{4,6},{6,4},{8,10},{10,8},{12,14},{14,12},{1,3},{3,1},... | collective-permute-start | bytes 430088 | tf_op jit(solution)/shard_map/ppermute | solution.py:303
  26.7 5.1 %copy-start.7 = (bf16[560,128]{1,0:T(8,128)(2,1)}, bf16[560,128]{1,0:T(8,128)(2,1)S(1)}, u32[]{:S(2)}) copy-start(bf16[560,128]{1,0:T(8,128)(2,1)S(1)} %collective-permute-done.2.refs_3_) | copy-start | bytes 430084
  29.0 2.8 %copy-start.8 = (bf16[560,128]{1,0:T(8,128)(2,1)}, bf16[560,128]{1,0:T(8,128)(2,1)S(1)}, u32[]{:S(2)}) copy-start(bf16[560,128]{1,0:T(8,128)(2,1)S(1)} %collective-permute-done.4.refs_5_) | copy-start | bytes 430084
  30.6 4.3 %collective-permute-start.7 = (bf16[8,560,128]{2,1,0:T(8,128)(2,1)S(1)}, bf16[8,560,128]{2,1,0:T(8,128)(2,1)S(1)}, u32[]{:S(2)}, u32[]{:S(2)}) collective-permute-start(bf16[8,560,128]{2,1,0:T(8,128)(2,1)S(1)} %bitcast_dynamic-update-slice_fusion), channel_id=1, source_target_pairs={{0,1},{1,0},{2,3},{3,2},{4,5},{5,4},{6,7},{7,6},{8,9},{9,8},{10,11... | collective-permute-start | bytes 3440648 | tf_op jit(solution)/shard_map/ppermute | solution.py:303
  73.8 4.6 %copy-start.1 = (bf16[2,8,560,128]{3,2,1,0:T(8,128)(2,1)S(1)}, bf16[2,8,560,128]{3,2,1,0:T(8,128)(2,1)}, u32[]{:S(2)}) copy-start(bf16[2,8,560,128]{3,2,1,0:T(8,128)(2,1)} %shard_map.136) | copy-start | bytes 6881284
  75.3 3.1 %collective-permute-start.10 = (bf16[8,560,128]{2,1,0:T(8,128)(2,1)S(1)}, bf16[8,560,128]{2,1,0:T(8,128)(2,1)}, u32[]{:S(2)}, u32[]{:S(2)}) collective-permute-start(bf16[8,560,128]{2,1,0:T(8,128)(2,1)S(1)} %dynamic-slice_bitcast_fusion), channel_id=1, source_target_pairs={{0,1},{1,0},{2,3},{3,2},{4,5},{5,4},{6,7},{7,6},{8,9},{9,8},{10,11... | collective-permute-start | bytes 3440648 | tf_op jit(solution)/shard_map/ppermute | solution.py:303
  80.0 15.3 %collective-permute-start.11 = (bf16[4,560,128]{2,1,0:T(8,128)(2,1)S(1)}, bf16[4,560,128]{2,1,0:T(8,128)(2,1)S(1)}, u32[]{:S(2)}, u32[]{:S(2)}) collective-permute-start(bf16[4,560,128]{2,1,0:T(8,128)(2,1)S(1)} %dynamic-slice_bitcast_fusion.1), channel_id=1, source_target_pairs={{0,2},{2,0},{4,6},{6,4},{8,10},{10,8},{12,14},{14,12},{1,3},{3,1},... | collective-permute-start | bytes 1720328 | tf_op jit(solution)/shard_map/ppermute | solution.py:303
  95.5 7.3 %collective-permute-start.12 = (bf16[560,128]{1,0:T(8,128)(2,1)S(1)}, bf16[560,128]{1,0:T(8,128)(2,1)S(1)}, u32[]{:S(2)}, u32[]{:S(2)}) collective-permute-start(bf16[560,128]{1,0:T(8,128)(2,1)S(1)} %get-tuple-element.30), channel_id=1, source_target_pairs={{0,4},{2,6},{4,0},{6,2},{8,12},{10,14},{12,8},{14,10},{1,5},{3,7},... | collective-permute-start | bytes 430088 | tf_op jit(solution)/shard_map/ppermute | solution.py:303
  96.5 13.9 %collective-permute-start.13 = (bf16[560,128]{1,0:T(8,128)(2,1)S(1)}, bf16[560,128]{1,0:T(8,128)(2,1)S(1)}, u32[]{:S(2)}, u32[]{:S(2)}) collective-permute-start(bf16[560,128]{1,0:T(8,128)(2,1)S(1)} %get-tuple-element.32), channel_id=1, source_target_pairs={{0,8},{2,10},{4,12},{6,14},{8,0},{10,2},{12,4},{14,6},{1,9},{3,11}... | collective-permute-start | bytes 430088 | tf_op jit(solution)/shard_map/ppermute | solution.py:303
  99.6 10.8 %collective-permute-start.14 = (bf16[560,128]{1,0:T(8,128)(2,1)S(1)}, bf16[560,128]{1,0:T(8,128)(2,1)S(1)}, u32[]{:S(2)}, u32[]{:S(2)}) collective-permute-start(bf16[560,128]{1,0:T(8,128)(2,1)S(1)} %get-tuple-element.31), channel_id=1, source_target_pairs={{0,12},{2,14},{4,8},{6,10},{8,4},{10,6},{12,0},{14,2},{1,13},{3,15... | collective-permute-start | bytes 430088 | tf_op jit(solution)/shard_map/ppermute | solution.py:303
  (5 other events, 7.0 us)

commit v3 on v0

v3 whole, which is shorter than its diff:
```python
import functools

import jax
import jax.numpy as jnp
from jax import lax
from jax.experimental import pallas as pl
from jax.experimental.pallas import tpu as pltpu
from jax.sharding import PartitionSpec as P

NB = 64
HALF = 32
RANK = 16
BIN = 128
BHID = 224
WIDE = 256
CHUNKS = 8
GROUP = 8
GROUPS = NB // GROUP
f32 = jnp.float32
bf16 = jnp.bfloat16

FIRST = 128
REST = 448
RD_AT = 256
LD_AT = 320
RIGHT = 256
DOWN = 192


def pack(lg, rg, lu, ru, ld, rd):
    left = jnp.stack([lg, lu]).reshape(2, 4, 8, 16, 16)
    left = jnp.transpose(left, (0, 1, 3, 2, 4)).reshape(FIRST, 128)
    right = jnp.stack([rg, ru]).reshape(2, HALF, 2, 8, 28)
    right = jnp.pad(right, ((0, 0),) * 4 + ((0, 4),)).reshape(2, HALF, 2, 2, 128)
    right = jnp.transpose(right, (3, 0, 2, 1, 4)).reshape(256, 128)
    rdown = jnp.transpose(rd.reshape(HALF, 2, 128), (1, 0, 2)).reshape(64, 128)
    ldown = jnp.transpose(ld.reshape(4, 8, 28, 16), (0, 2, 1, 3)).reshape(4, 28, 128)
    ldown = jnp.pad(ldown, ((0, 0), (0, 4), (0, 0))).reshape(128, 128)
    return left, jnp.concatenate([right, rdown, ldown], axis=0)


def unpack(first, rest):
    left = jnp.transpose(first.reshape(2, 4, 16, 8, 16), (0, 1, 3, 2, 4)).reshape(2, HALF, 256)
    right = jnp.transpose(rest[:RD_AT].reshape(2, 2, 2, HALF, 128), (1, 3, 2, 0, 4))
    right = right.reshape(2, HALF, 2, 8, 32)[..., :28].reshape(2, HALF, 448)
    rdown = jnp.transpose(rest[RD_AT:LD_AT].reshape(2, HALF, 128), (1, 0, 2)).reshape(HALF, 256)
    ldown = rest[LD_AT:].reshape(4, 32, 8, 16)[:, :28]
    ldown = jnp.transpose(ldown, (0, 2, 1, 3)).reshape(HALF, 448)
    return left[0], right[0], left[1], right[1], ldown, rdown


def turn_blocks(v):
    whole = v.reshape(-1, 8, 128)
    row = lax.broadcasted_iota(jnp.int32, (1, 8, 128), 1)
    lane = lax.broadcasted_iota(jnp.int32, (1, 8, 128), 2) // RANK
    out = whole
    for s in range(1, 8):
        moved = pltpu.roll(pltpu.roll(whole, s, 1), 128 - RANK * s, 2)
        out = jnp.where((row - lane - s) % 8 == 0, moved, out)
    return out


def spaced(v):
    gap = jnp.zeros((v.shape[0], 4), f32)
    parts = []
    for q in range(8):
        parts += [v[:, 28 * q : 28 * q + 28], gap]
    return jnp.concatenate(parts, axis=1)


def prepare_body(where, *refs):
    shards, (x, y, packed, x_out, y_out), (lg, rg, lu, ru, ld, rd) = refs[:6], refs[6:11], refs[11:17]
    sems, shard_sems = refs[17:]
    half = x_out.shape[0]
    off = pl.multiple_of((1 - where[1]) * half, half)
    loads = [
        pltpu.make_async_copy(shard, ref, shard_sems.at[i])
        for i, (shard, ref) in enumerate(zip(shards, refs[11:17]))
    ]
    copies = [
        pltpu.make_async_copy(x.at[pl.ds(off, half), :], x_out, sems.at[0]),
        pltpu.make_async_copy(y.at[pl.ds(off, half), :], y_out, sems.at[1]),
    ]
    for copy in loads + copies:
        copy.start()
    for copy in loads:
        copy.wait()
    for gu, ref in enumerate([lg, lu]):
        v = ref[...].astype(f32)
        lo, hi = turn_blocks(v[:, :128]), turn_blocks(v[:, 128:])
        for g in range(4):
            both = jnp.concatenate([lo[g], hi[g]], axis=0)
            packed[pl.ds((gu * 4 + g) * 16, 16), :] = both.astype(bf16)
    for gu, ref in enumerate([rg, ru]):
        v = ref[...].astype(f32)
        for al in range(2):
            part = spaced(v[:, al * BHID : (al + 1) * BHID]).astype(bf16)
            for h in range(2):
                at = FIRST + h * 128 + gu * 64 + al * HALF
                packed[pl.ds(at, HALF), :] = part[:, h * 128 : (h + 1) * 128]
    for al in range(2):
        packed[pl.ds(FIRST + RD_AT + al * HALF, HALF), :] = rd[:, pl.ds(al * 128, 128)]
    v = ld[...].astype(f32)
    v = jnp.concatenate([v, jnp.zeros((HALF, 64), f32)], axis=1)
    quarters = [turn_blocks(v[:, q * 128 : (q + 1) * 128]) for q in range(4)]
    for g in range(4):
        part = jnp.concatenate([q[g] for q in quarters], axis=0).astype(bf16)
        packed[pl.ds(FIRST + LD_AT + g * 32, 32), :] = part
    for copy in copies:
        copy.wait()


def finish_body(first, rights, downs, lg, rg, lu, ru, ld, rd):
    def total(pieces, start, height):
        return sum(p[pl.ds(start, height), :].astype(f32) for p in pieces)

    left = total(first, 0, FIRST)
    for gu, ref in enumerate([lg, lu]):
        v = left[gu * 64 : (gu + 1) * 64].reshape(4, 2, 8, 128)
        for h in range(2):
            ref[:, pl.ds(h * 128, 128)] = turn_blocks(v[:, h]).reshape(HALF, 128)
    right = total(rights, 0, RIGHT)
    for gu, ref in enumerate([rg, ru]):
        parts = []
        for al in range(2):
            for q in range(8):
                at = (q // 4) * 128 + gu * 64 + al * HALF
                parts.append(right[at : at + HALF, 32 * (q % 4) : 32 * (q % 4) + 28])
        ref[...] = jnp.concatenate(parts, axis=1)
    down = total(downs, 0, 64)
    for al in range(2):
        rd[:, pl.ds(al * 128, 128)] = down[al * HALF : (al + 1) * HALF]
    v = total(downs, 64, 128).reshape(4, 4, 8, 128)
    parts = [turn_blocks(v[:, q]).reshape(HALF, 128) for q in range(4)]
    ld[...] = jnp.concatenate(parts, axis=1)[:, :448]


def nn(a, b):
    return jnp.dot(a, b, preferred_element_type=f32)


def rounded(v):
    return v.astype(bf16).astype(f32)


def rows(j, height=RANK):
    return pl.ds(pl.multiple_of(j * height, height), height)


def lanes(j, width=BIN):
    return pl.ds(pl.multiple_of(j * width, width), width)


def spread(v, masks):
    return jnp.concatenate([v * mask for mask in masks], axis=0)


def chosen(out, toks):
    slot = lax.broadcasted_iota(jnp.int32, (toks, 128), 1) // RANK
    total = out[:toks]
    for u in range(1, GROUP):
        total = jnp.where(slot == u, out[u * toks : (u + 1) * toks], total)
    return total


def crossed_pair(a, b):
    return jnp.concatenate(
        [jnp.concatenate([a, jnp.zeros_like(b)], axis=1), jnp.concatenate([jnp.zeros_like(a), b], axis=1)], axis=0
    )


def unit_masks():
    slot = lax.broadcasted_iota(jnp.int32, (1, 128), 1) // RANK
    return [jnp.where(slot == u, 1.0, 0.0).astype(bf16) for u in range(GROUP)]


def chunk_of(me, r):
    return me ^ (2 * (r % 4)) ^ (r // 4)


def inner_body(other, where, along, across, x, inner, t_l, xs, sem):
    me, side = where[0], where[1]
    toks = xs.shape[0]
    off = 0 if other else pl.multiple_of(side * toks, toks)
    copy = pltpu.make_async_copy(x.at[pl.ds(off, toks), :], xs, sem)
    copy.start()
    masks = [jnp.concatenate([mask, mask], axis=1) for mask in unit_masks()]
    for r in range(CHUNKS):
        piece = (along, across)[r // 4]
        for gg in range(8):
            t_l[gg, rows(chunk_of(me, r)), :] = piece[r % 4, pl.ds(gg * 16, 16), :]
    copy.wait()

    def step(i, _):
        both = jnp.concatenate([t_l[i], t_l[4 + i]], axis=1)
        total = jnp.zeros((toks, 256), f32)
        for p in range(GROUP // 2):
            w = jnp.concatenate([both * masks[2 * p + h] for h in range(2)], axis=0)
            total += nn(xs[:, lanes(i * GROUP // 2 + p, 256)], w)
        for gu in range(2):
            inner[gu, rows(i, 128), :] = rounded(total[:, gu * 128 : (gu + 1) * 128].T)
        return 0

    lax.fori_loop(0, 4, step, 0)


def by_parity(ref, m):
    return jnp.concatenate(
        [ref[pl.ds(m, 8, stride=2 * NB), :], ref[pl.ds(m + NB, 8, stride=2 * NB), :]], axis=0
    ).astype(bf16)


def middle_body(
    scale, where, order, own_a, own_b, oth_a, oth_b, inner_own, inner_oth, y, y_got, keep, send,
    inner, ret, t_r, n_ld, act_own, act_oth, slope_own, slope_oth,
    ys, sems, r_lo, r_hi, s_rd, n_r, n_rd, t_rd, t_ld, g_out, down, hid_s,
):
    me, side = where[0], where[1]
    toks = ys.shape[1]
    copies = [
        pltpu.make_async_copy(y.at[pl.ds(pl.multiple_of(side * toks, toks), toks), :], ys.at[0], sems.at[0]),
        pltpu.make_async_copy(y_got, ys.at[1], sems.at[1]),
    ]
    for copy in copies:
        copy.start()
    masks = unit_masks()
    s_r = (r_lo, r_hi)
    for gu in range(2):
        for b, part in enumerate([inner_own, inner_oth]):
            inner[rows(gu * 2 + (side ^ b), 512), :] = part[gu]

    for b, pieces in enumerate([(own_a, own_b), (oth_a, oth_b)]):
        blk = side ^ b
        for r in range(CHUNKS):
            d = chunk_of(me, r)
            ref, at = pieces[r // 4], r % 4
            for gu in range(2):
                for al in range(2):
                    row = pl.multiple_of((2 * d + al) * 128 + gu * NB + blk * HALF, HALF)
                    for half in range(2):
                        src = FIRST + half * 128 + gu * 64 + al * HALF
                        s_r[half][pl.ds(row, HALF), :] = ref[at, pl.ds(src, HALF), :].astype(f32)
            for al in range(2):
                row = pl.multiple_of((2 * d + al) * NB + blk * HALF, HALF)
                s_rd[pl.ds(row, HALF), :] = ref[at, pl.ds(FIRST + RD_AT + al * HALF, HALF), :].astype(f32)
            for g in range(4):
                t_ld[blk * 4 + g, rows(d, 32), :] = ref[at, pl.ds(FIRST + LD_AT + g * 32, 32), :]

    def stacked(ref, start, stride, g):
        return jnp.concatenate(
            [ref[pl.ds(start + g * GROUP + u, RANK, stride=stride), :] for u in range(GROUP)], axis=0
        )

    def turn(g, _):
        for gu in range(2):
            for h in range(2):
                flat = stacked(s_r[h], gu * NB, 128, g)
                n_r[gu, g, :, pl.ds(h * 128, 128)] = flat.astype(bf16)
                t_r[gu, g, pl.ds(h * 128, 128), :] = flat.T.astype(bf16)
        for h in range(2):
            part = t_ld[g, pl.ds(h * 128, 128), :].astype(f32).T
            n_ld[g, :, pl.ds(h * 128, 128)] = part.astype(bf16)
        flat = stacked(s_rd, 0, NB, g)
        n_rd[g] = flat.astype(bf16)
        t_rd[g] = flat.T.astype(bf16)
        return 0

    lax.fori_loop(0, GROUPS, turn, 0)

    def blocks(g):
        return [(u, g * GROUP + u) for u in range(GROUP)]

    def second(i, _, b):
        g = (side ^ b) * 4 + i
        act_s, slope_s = ((act_own, slope_own), (act_oth, slope_oth))[b]
        turned = []
        for gu in range(2):
            mixed = [inner[pl.ds(gu * 1024 + order[k], RANK, stride=NB), :] for u, k in blocks(g)]
            turned.append(jnp.concatenate(mixed, axis=0).T.astype(bf16))
        span = pl.ds(pl.multiple_of(i * GROUP, GROUP), GROUP)
        act_s[span] = nn(spread(turned[0], masks), n_r[0, g]).reshape(GROUP, toks, WIDE)
        slope_s[span] = nn(spread(turned[1], masks), n_r[1, g]).reshape(GROUP, toks, WIDE)
        for u, k in blocks(g):
            local = i * GROUP + u
            gate, upper = act_s[local], slope_s[local]
            sig = 0.5 * jnp.tanh(0.5 * gate) + 0.5
            act = gate * sig
            act_s[local] = act
            slope_s[local] = upper * (sig + act * (1.0 - sig))
            hid_s[k] = (act * upper).astype(bf16)
        hidden = hid_s[pl.ds(pl.multiple_of(g * GROUP, GROUP), GROUP)].reshape(GROUP * toks, WIDE)
        total = chosen(nn(hidden, t_ld[g]), toks)
        down[rows(g, 128), :] = rounded(total.T)
        return 0

    for b in range(2):
        lax.fori_loop(0, 4, functools.partial(second, b=b), 0)

    def put(b, base, value):
        for al in range(2):
            g_out[b, pl.ds(base + al * HALF, 8, stride=DOWN), :] = value[al * 8 : (al + 1) * 8]

    for b in range(2):
        copies[b].wait()

        def third(i, _, b=b):
            g = (side ^ b) * 4 + i
            dms = [down[pl.ds(order[k], RANK, stride=NB), :] for u, k in blocks(g)]
            turned = jnp.concatenate(dms, axis=0).T.astype(bf16)
            student = nn(spread(turned, masks), n_rd[g])
            deltas = []
            for u, k in blocks(g):
                target = ys[b, :, lanes(i * GROUP + u)].astype(f32)
                part = student[u * toks : (u + 1) * toks]
                deltas.append(((part - target) * scale).astype(bf16))
            total = chosen(nn(jnp.concatenate(deltas, axis=0), t_rd[g]), toks)
            parity = [by_parity(down, order[k]) for u, k in blocks(g)]
            for q in range(2):
                d = deltas[4 * q : 4 * q + 4]
                m = parity[4 * q : 4 * q + 4]
                grads = nn(
                    crossed_pair(jnp.concatenate(m[:2], axis=0), jnp.concatenate(m[2:], axis=0)),
                    jnp.concatenate([jnp.concatenate(d[:2], axis=1), jnp.concatenate(d[2:], axis=1)], axis=0),
                )
                for e in range(4):
                    part = grads[e * RANK : (e + 1) * RANK, (e % 2) * 128 : (e % 2 + 1) * 128]
                    put(b, i * GROUP + 4 * q + e, part)
            total = rounded(total.T)
            for u, k in blocks(g):
                ret[pl.ds(order[k], RANK, stride=NB), :] = total[u * RANK : (u + 1) * RANK]
            return 0

        lax.fori_loop(0, 4, third, 0)

    def inward(i, _, b):
        g = (side ^ b) * 4 + i
        returned = ret[rows(g, 128), :].astype(bf16)
        grads = []
        for p in range(GROUP // 2):
            pair = [returned[u * RANK : (u + 1) * RANK] for u in (2 * p, 2 * p + 1)]
            both = hid_s[pl.ds(g * GROUP + 2 * p, 2)].reshape(2 * toks, WIDE)
            grads.append(nn(crossed_pair(*pair), both))
        grads = jnp.concatenate(grads, axis=0)
        for h in range(2):
            part = grads[:, h * 128 : (h + 1) * 128].T
            for q in range(4):
                at = (h * 4 + q) * DOWN + 64 + i * 32
                g_out[b, pl.ds(pl.multiple_of(at, 32), 32), :] = part[q * 32 : (q + 1) * 32]
        return 0

    for b in range(2):
        lax.fori_loop(0, 4, functools.partial(inward, b=b), 0)

    for b, out in enumerate([keep, send]):
        for r in range(CHUNKS):
            out[r] = g_out[b, rows(chunk_of(me, r), DOWN), :].astype(bf16)


def right_body(b, where, order, inner, ret, t_r, n_ld, act_s, slope_s, *refs):
    if b == 0:
        before, grads_out, back, g_out = refs
        back[...] = before[...]
    else:
        grads_out, back, g_out = refs
    me, side = where[0], where[1]
    toks = inner.shape[1]
    masks = unit_masks()

    def step(i, _):
        g = (side ^ b) * 4 + i
        blocks = [(u, g * GROUP + u) for u in range(GROUP)]
        turned = ret[rows(g, 128), :].T.astype(bf16)
        dhidden = nn(spread(turned, masks), n_ld[g])
        sent = ([], [])
        for u, j in blocks:
            local, part = i * GROUP + u, dhidden[u * toks : (u + 1) * toks]
            sent[0].append((part * slope_s[local]).astype(bf16))
            sent[1].append((part * act_s[local]).astype(bf16))
        for gu in range(2):
            total = rounded(chosen(nn(jnp.concatenate(sent[gu], axis=0), t_r[gu, g]), toks).T)
            for u, j in blocks:
                back[pl.ds(gu * 1024 + order[j], RANK, stride=NB), :] = total[u * RANK : (u + 1) * RANK]
        for u, j in blocks:
            mixed = [by_parity(inner, gu * 1024 + order[j]) for gu in range(2)]
            grad = nn(crossed_pair(*mixed), jnp.concatenate([sent[0][u], sent[1][u]], axis=0))
            for gu in range(2):
                for h in range(2):
                    base = h * 128 + gu * 64 + i * GROUP + u
                    for al in range(2):
                        g_out[pl.ds(base + al * HALF, 8, stride=RIGHT), :] = grad[
                            gu * RANK + al * 8 : gu * RANK + (al + 1) * 8, h * 128 : (h + 1) * 128
                        ]
        return 0

    lax.fori_loop(0, 4, step, 0)
    for r in range(CHUNKS):
        grads_out[r] = g_out[rows(chunk_of(me, r), RIGHT), :].astype(bf16)


def left_body(where, back, x, x_got, keep, send, turned, xs, sems):
    me, side = where[0], where[1]
    toks = xs.shape[1]
    copies = [
        pltpu.make_async_copy(x.at[pl.ds(pl.multiple_of(side * toks, toks), toks), :], xs.at[0], sems.at[0]),
        pltpu.make_async_copy(x_got, xs.at[1], sems.at[1]),
    ]
    for copy in copies:
        copy.start()
    for b, out in enumerate([keep, send]):
        copies[b].wait()

        def step(i, _, b=b):
            parts = ([], [])
            for q in range(2):
                both = []
                for u in range(4 * q, 4 * q + 4):
                    j = ((side ^ b) * 4 + i) * GROUP + u
                    both += [back[rows(j), :], back[rows(j + NB), :]]
                both = jnp.concatenate(both, axis=0).astype(bf16)
                at = i * 4 + 2 * q
                x4 = jnp.concatenate([xs[b, :, lanes(at, 256)], xs[b, :, lanes(at + 1, 256)]], axis=0)
                grads = nn(crossed_pair(both[:64], both[64:]), x4)
                for e in range(4):
                    for gu in range(2):
                        top = (e * 2 + gu) * RANK
                        parts[gu].append(grads[top : top + RANK, (e % 2) * 128 : (e % 2 + 1) * 128])
            for gu in range(2):
                turned[rows(gu * 4 + i, 128), :] = jnp.concatenate(parts[gu], axis=0).T.astype(bf16)
            return 0

        lax.fori_loop(0, 4, step, 0)
        for r in range(CHUNKS):
            d = chunk_of(me, r)
            for gg in range(8):
                at = pl.multiple_of(gg * 128 + d * 16, 16)
                out[r, pl.ds(gg * 16, 16), :] = turned[pl.ds(at, 16), :]


VMEM = pl.BlockSpec(memory_space=pltpu.VMEM)
SMEM = pl.BlockSpec(memory_space=pltpu.SMEM)


ANY = pl.BlockSpec(memory_space=pl.ANY)
HBM = pl.BlockSpec(memory_space=pltpu.HBM)
VMEM_MIDDLE = 20 * 2**20
VMEM_RIGHT = 10 * 2**20


def prepare_call(where, factors, x, y):
    sent = jax.ShapeDtypeStruct((x.shape[0] // 2, x.shape[1]), bf16)
    return pl.pallas_call(
        prepare_body,
        out_shape=(jax.ShapeDtypeStruct((FIRST + REST, 128), bf16), sent, sent),
        in_specs=[SMEM] + [HBM] * 8,
        out_specs=(VMEM, VMEM, VMEM),
        scratch_shapes=[pltpu.VMEM(v.shape, bf16) for v in factors]
        + [pltpu.SemaphoreType.DMA((2,)), pltpu.SemaphoreType.DMA((6,))],
        compiler_params=pltpu.CompilerParams(vmem_limit_bytes=60 * 2**20),
    )(where, *factors, x, y)


def finish_call(first, rights, downs):
    cut, count = len(first), len(first) + len(rights) + len(downs)
    turn = cut + len(rights)
    shapes = [256, 448, 256, 448, 448, 256]
    return pl.pallas_call(
        lambda *refs: finish_body(refs[:cut], refs[cut:turn], refs[turn:count], *refs[count:]),
        out_shape=tuple(jax.ShapeDtypeStruct((HALF, c), f32) for c in shapes),
        in_specs=[VMEM] * count,
        out_specs=(VMEM,) * 6,
        compiler_params=pltpu.CompilerParams(vmem_limit_bytes=16 * 2**20),
    )(*first, *rights, *downs)


def inner_call(other, where, along, across, x, toks):
    front = pl.BlockSpec((4, FIRST, 128), lambda i: (0, 0, 0))
    return pl.pallas_call(
        functools.partial(inner_body, other),
        grid=(1,),
        out_shape=jax.ShapeDtypeStruct((2, NB * RANK // 2, toks), f32),
        in_specs=[SMEM, front, front, ANY],
        out_specs=VMEM,
        scratch_shapes=[
            pltpu.VMEM((8, BIN, 128), bf16),
            pltpu.VMEM((toks, x.shape[1]), bf16),
            pltpu.SemaphoreType.DMA,
        ],
        compiler_params=pltpu.CompilerParams(vmem_limit_bytes=16 * 2**20),
        cost_estimate=pl.CostEstimate(flops=10**9, bytes_accessed=10**7, transcendentals=0),
    )(where, along, across, x)


def middle_call(scale, where, order, pieces, inner, y, y_got):
    toks = y_got.shape[0]
    down = jax.ShapeDtypeStruct((CHUNKS, DOWN, 128), bf16)
    kept = jax.ShapeDtypeStruct((HALF, toks, WIDE), f32)
    return pl.pallas_call(
        functools.partial(middle_body, scale),
        out_shape=(
            down,
            down,
            jax.ShapeDtypeStruct((2 * NB * RANK, toks), f32),
            jax.ShapeDtypeStruct((NB * RANK, toks), f32),
            jax.ShapeDtypeStruct((2, GROUPS, WIDE, 128), bf16),
            jax.ShapeDtypeStruct((GROUPS, 128, WIDE), bf16),
            kept,
            kept,
            kept,
            kept,
        ),
        in_specs=[SMEM, SMEM] + [VMEM] * 6 + [ANY] * 2,
        out_specs=(VMEM,) * 10,
        scratch_shapes=[
            pltpu.VMEM((2,) + y_got.shape, bf16),
            pltpu.SemaphoreType.DMA((2,)),
            pltpu.VMEM((RANK * 128, 128), f32),
            pltpu.VMEM((RANK * 128, 128), f32),
            pltpu.VMEM((RANK * NB, 128), f32),
            pltpu.VMEM((2, GROUPS, 128, WIDE), bf16),
            pltpu.VMEM((GROUPS, 128, BIN), bf16),
            pltpu.VMEM((GROUPS, BIN, 128), bf16),
            pltpu.VMEM((GROUPS, WIDE, 128), bf16),
            pltpu.VMEM((2, CHUNKS * DOWN, 128), f32),
            pltpu.VMEM((NB * RANK, toks), f32),
            pltpu.VMEM((NB, toks, WIDE), bf16),
        ],
        compiler_params=pltpu.CompilerParams(vmem_limit_bytes=VMEM_MIDDLE),
        cost_estimate=pl.CostEstimate(flops=5 * 10**9, bytes_accessed=4 * 10**7, transcendentals=0),
    )(where, order, *pieces, *inner, y, y_got)


def right_call(b, where, order, *arrays):
    toks = arrays[0].shape[1]
    return pl.pallas_call(
        functools.partial(right_body, b),
        out_shape=(
            jax.ShapeDtypeStruct((CHUNKS, RIGHT, 128), bf16),
            jax.ShapeDtypeStruct((2 * NB * RANK, toks), f32),
        ),
        in_specs=[SMEM, SMEM] + [VMEM] * len(arrays),
        out_specs=(VMEM, VMEM),
        scratch_shapes=[pltpu.VMEM((CHUNKS * RIGHT, 128), f32)],
        compiler_params=pltpu.CompilerParams(vmem_limit_bytes=VMEM_RIGHT),
        cost_estimate=pl.CostEstimate(flops=5 * 10**9, bytes_accessed=2 * 10**7, transcendentals=0),
    )(where, order, *arrays)


def left_call(where, back, x, x_got):
    grads = jax.ShapeDtypeStruct((CHUNKS, FIRST, 128), bf16)
    return pl.pallas_call(
        left_body,
        out_shape=(grads, grads),
        in_specs=[SMEM, VMEM, ANY, ANY],
        out_specs=(VMEM, VMEM),
        scratch_shapes=[
            pltpu.VMEM((8 * 128, 128), bf16),
            pltpu.VMEM((2,) + x_got.shape, bf16),
            pltpu.SemaphoreType.DMA((2,)),
        ],
        compiler_params=pltpu.CompilerParams(vmem_limit_bytes=16 * 2**20),
        cost_estimate=pl.CostEstimate(flops=10**9, bytes_accessed=10**7, transcendentals=0),
    )(where, back, x, x_got)


def swap(v, axis, bit, size):
    return lax.ppermute(v, axis, [(i, i ^ bit) for i in range(size)])


def sibling(v):
    return swap(v, "blk", 1, 2)


def gathered(mine, n):
    along = [mine] + [swap(mine, "dp", 2 * s, n) for s in range(1, 4)]
    across = [swap(v, "dp", 1, n) for v in along]
    along, across = jnp.stack(along), jnp.stack(across)
    return along, across, sibling(along), sibling(across)


def add(a, b):
    return (a.astype(f32) + b.astype(f32)).astype(bf16)


def tie(value, *others):
    return lax.optimization_barrier((value,) + others)[0]


def along_z(line, n):
    return [swap(line[s], "dp", 2 * s, n) for s in range(1, 4)]


def by_z_then_x(keep, got, n):
    both = add(keep, got)
    both = both.reshape((2, 4) + both.shape[1:])
    pair = both[:, 0].astype(f32)
    for s in range(1, 4):
        pair = pair + swap(both[:, s], "dp", 2 * s, n).astype(f32)
    pair = pair.astype(bf16)
    return [pair[0], swap(pair[1], "dp", 1, n)]


def on_device(activations, teacher_out, block_order, *factors):
    n = lax.axis_size("dp")
    me = lax.axis_index("dp")
    side = lax.axis_index("blk")
    toks = activations.shape[0] // 2
    scale = float(activations.shape[0] * n) ** (-0.5)
    direct = n == CHUNKS
    if direct:
        where = jnp.stack([me, side]).astype(jnp.int32)
        mine, x_sent, y_sent = prepare_call(where, factors, activations, teacher_out)
        pieces = gathered(mine, n)
    else:
        where = jnp.stack([jnp.zeros_like(side), side]).astype(jnp.int32)
        whole = [lax.all_gather(v, "dp", axis=1, tiled=True) for v in factors]
        cut = [jnp.moveaxis(v.reshape(HALF, CHUNKS, -1), 1, 0) for v in whole]
        packed = jnp.concatenate(jax.vmap(pack)(*cut), axis=1)
        pieces = (packed[0::2], packed[1::2], sibling(packed[0::2]), sibling(packed[1::2]))
        x_sent, y_sent = [
            lax.dynamic_slice_in_dim(v, (1 - side) * toks, toks, 0) for v in (activations, teacher_out)
        ]
    x_got, y_got = sibling(x_sent), sibling(y_sent)
    inner = (
        inner_call(False, where, pieces[0], pieces[1], activations, toks),
        inner_call(True, where, pieces[2], pieces[3], x_got, toks),
    )
    keep, send, *state = middle_call(scale, where, block_order, pieces, inner, teacher_out, y_got)
    shared, (act_own, act_oth, slope_own, slope_oth) = state[:4], state[4:]
    got = sibling(send)
    right_send, back = right_call(1, where, block_order, *shared, act_oth, slope_oth)
    right_got = sibling(right_send)
    if direct:
        away = add(keep[4:], got[4:])
        here = add(keep[:4], got[:4])
        crossed = swap(away, "dp", 1, n)
        back = tie(back, away, here)
    right_keep, back = right_call(0, where, block_order, *shared, act_own, slope_own, back)
    if direct:
        right_away = add(right_keep[4:], right_got[4:])
        right_here = add(right_keep[:4], right_got[:4])
        right_crossed = swap(right_away, "dp", 1, n)
        line = add(here, crossed)
        down = [line[0]] + along_z(line, n)
        back = tie(back, right_away, line)
    left_keep, left_send = left_call(where, back, activations, x_got)
    left_got = sibling(left_send)
    if direct:
        right_line = add(right_here, right_crossed)
        right = [right_line[0]] + along_z(right_line, n)
        left = by_z_then_x(left_keep, left_got, n)
        return finish_call(left, right, down)
    rest = (jnp.concatenate([right_keep, keep], axis=1), jnp.concatenate([right_got, got], axis=1))
    sums = []
    rest = [jnp.concatenate(v, axis=1) for v in ((right_keep, keep), (right_send, send))]
    for own, away in ((left_keep, left_got), rest):
        total = own.astype(f32) + away.astype(f32)
        sums.append(jnp.stack([total[:4], total[4:]], axis=1).reshape(total.shape))
    parts = jax.vmap(unpack)(*sums)
    parts = [jnp.moveaxis(v, 0, 1).reshape(HALF, -1) for v in parts]
    return tuple(lax.psum_scatter(v, "dp", scatter_dimension=1, tiled=True) for v in parts)


def solution(mesh):
    tokens = P(("group", "dp"), "blk")
    factor = P("blk", "dp")
    grad = P(("group", "blk"), "dp")
    return jax.shard_map(
        on_device,
        mesh=mesh,
        in_specs=(tokens, tokens, P()) + (factor,) * 6,
        out_specs=(grad,) * 6,
        check_vma=False,
    )
```

time: 691 us -> 96.5 us (0.14)
  waiting for transfers between devices: 373 us -> 27.4 us
  blocking collectives: 186 us -> 0 us
  local copies, waits for them, and re-layouts: 47.4 us -> 0.07 us
  matrix products: 40.1 us -> 0 us
  Pallas kernels: 0 us -> 39.3 us
  between operations: 14.6 us -> 0.89 us
    reduce_scatter x4 -> x0, waiting for transfers between devices: 238 us -> none  [the longest x1 66.6 us: on_device(): lax.psum_scatter(grad_ld.reshape(blocks, -1), 'dp', scatter_dimension=1,...]
    all_gather x6 -> x0, blocking collectives: 186 us -> none  [the longest x1 32.6 us: on_device(): lax.all_gather(gate_left, 'dp', axis=1, tiled=True)]
    unnamed x8 -> x0, waiting for transfers between devices: 134 us -> none
    dot_general x16 -> x0, matrix products: 40.1 us -> none  [the longest x1 8.77 us: on_device(): jnp.einsum('tjc,joc->tjo', down_return, left_down, preferred_element_type...]
    pallas_call x0 -> x8, Pallas kernels: none -> 39.3 us  [the longest x1 17.8 us: middle_call(): pl.pallas_call(functools.partial(middle_body, scale), out_shape=(down, do...]
    ppermute x0 -> x26, waiting for transfers between devices: none -> 27.4 us  [swap(): return lax.ppermute(v, axis, [(i, i ^ bit) for i in range(size)])]
    ppermute x0 -> x26, starting transfers between devices: none -> 26.4 us  [swap(): return lax.ppermute(v, axis, [(i, i ^ bit) for i in range(size)])]
    unnamed x48 -> x8, local copies, waits for them, and re-layouts: 24.7 us -> 0.02 us
  transfers between devices with their start and end apart: 12 -> 26, of which waited for: 7 -> 12; matrix products, arithmetic and copies ran while one was open for 8% -> 1% of each run, Pallas kernels for 0% -> 14%
where the time goes in v3:
time: 96.5 us; the launch traced here: 96.2 us
  Pallas kernels  39.3 us (41%)
  waiting for transfers between devices  27.4 us (28%)
  starting transfers between devices  26.4 us (27%)
  other arithmetic  2.07 us (2%)
    ppermute x26, waiting for transfers between devices, swap(): return lax.ppermute(v, axis, [(i, i ^ bit) for i in range(size)])  27.4 us
    ppermute x26, starting transfers between devices, swap(): return lax.ppermute(v, axis, [(i, i ^ bit) for i in range(size)])  26.4 us
    pallas_call x1, Pallas kernels, middle_call(): pl.pallas_call(functools.partial(middle_body, scale), out_shape=(down, do...  17.8 us
    pallas_call x2, Pallas kernels, right_call(): pl.pallas_call(functools.partial(right_body, b), out_shape=(jax.ShapeDtyp...  9.66 us
    pallas_call x1, Pallas kernels, prepare_call(): pl.pallas_call(prepare_body, out_shape=(jax.ShapeDtypeStruct((FIRST + RES...  3.9 us
    pallas_call x2, Pallas kernels, inner_call(): pl.pallas_call(functools.partial(inner_body, other), grid=(1,), out_shape...  3.79 us
    pallas_call x1, Pallas kernels, left_call(): pl.pallas_call(left_body, out_shape=(grads, grads), in_specs=[SMEM, VMEM,...  3.11 us
  transfers between devices with their start and end apart: 26, of which 12 were waited for; matrix products, arithmetic and copies ran while one was open for 1% of the time, Pallas kernels for 14%

profile of v3, /device:TPU:0, one launch (start us, length us, event | category | flops | bytes accessed | tf_op | source)
XLA Modules:
  0.0 96.2 jit_solution(72723865056951085)
XLA Ops:
  1.2 3.9 %shard_map.136 = (bf16[576,128]{1,0:T(8,128)(2,1)}, bf16[128,4096]{1,0:T(8,128)(2,1)}, bf16[128,4096]{1,0:T(8,128)(2,1)}) custom-call(s32[2]{0:T(128)} %pad_add_fusion.where, bf16[32,256]{1,0:T(8,128)(2,1)} %refs_0_.1, bf16[32,448]{1,0:T(8,128)(2,1)} %refs_1_.1, bf16[32,256]{1,0:T(8,128)(2,1)} %refs_2_.1, bf16[32,448]{1,0:T(8,128)(2,1)} %refs_3_.1, ...), custom_call_target="tpu_custom_call" | custom-call | tf_op jit(solution)/shard_map/pallas_call | solution.py:451
  5.1 3.0 %collective-permute-start.3 = (bf16[576,128]{1,0:T(8,128)(2,1)}, bf16[576,128]{1,0:T(8,128)(2,1)S(1)}, u32[]{:S(2)}, u32[]{:S(2)}) collective-permute-start(bf16[576,128]{1,0:T(8,128)(2,1)} %get-tuple-element.27), channel_id=1, source_target_pairs={{0,2},{2,0},{4,6},{6,4},{8,10},{10,8},{12,14},{14,12},{1,3},{3,1},... | collective-permute-start | bytes 442376 | tf_op jit(solution)/shard_map/ppermute | solution.py:566
  8.2 3.6 %collective-permute-start.2 = (bf16[576,128]{1,0:T(8,128)(2,1)}, bf16[576,128]{1,0:T(8,128)(2,1)S(1)}, u32[]{:S(2)}, u32[]{:S(2)}) collective-permute-start(bf16[576,128]{1,0:T(8,128)(2,1)} %get-tuple-element.27), channel_id=1, source_target_pairs={{0,12},{2,14},{4,8},{6,10},{8,4},{10,6},{12,0},{14,2},{1,13},{3,15... | collective-permute-start | bytes 442376 | tf_op jit(solution)/shard_map/ppermute | solution.py:566
  12.5 4.4 %collective-permute-done.2 = bf16[576,128]{1,0:T(8,128)(2,1)S(1)} collective-permute-done((bf16[576,128]{1,0:T(8,128)(2,1)}, bf16[576,128]{1,0:T(8,128)(2,1)S(1)}, u32[]{:S(2)}, u32[]{:S(2)}) %collective-permute-start.2) | collective-permute-done | bytes 147488 | tf_op jit(solution)/shard_map/ppermute | solution.py:566
  17.3 7.8 %collective-permute-done.1 = bf16[576,128]{1,0:T(8,128)(2,1)S(1)} collective-permute-done((bf16[576,128]{1,0:T(8,128)(2,1)}, bf16[576,128]{1,0:T(8,128)(2,1)S(1)}, u32[]{:S(2)}, u32[]{:S(2)}) %collective-permute-start.1) | collective-permute-done | bytes 147488 | tf_op jit(solution)/shard_map/ppermute | solution.py:566
  25.7 1.5 %collective-permute-start.4 = (bf16[576,128]{1,0:T(8,128)(2,1)S(1)}, bf16[576,128]{1,0:T(8,128)(2,1)S(1)}, u32[]{:S(2)}, u32[]{:S(2)}) collective-permute-start(bf16[576,128]{1,0:T(8,128)(2,1)S(1)} %collective-permute-done), channel_id=1, source_target_pairs={{0,2},{2,0},{4,6},{6,4},{8,10},{10,8},{12,14},{14,12},{1,3},{3,1},... | collective-permute-start | bytes 442376 | tf_op jit(solution)/shard_map/ppermute | solution.py:566
  28.2 3.6 %collective-permute-done.5 = bf16[576,128]{1,0:T(8,128)(2,1)S(1)} collective-permute-done((bf16[576,128]{1,0:T(8,128)(2,1)S(1)}, bf16[576,128]{1,0:T(8,128)(2,1)S(1)}, u32[]{:S(2)}, u32[]{:S(2)}) %collective-permute-start.5) | collective-permute-done | bytes 147488 | tf_op jit(solution)/shard_map/ppermute | solution.py:566
  31.9 1.9 %collective-permute-done.4 = bf16[576,128]{1,0:T(8,128)(2,1)S(1)} collective-permute-done((bf16[576,128]{1,0:T(8,128)(2,1)S(1)}, bf16[576,128]{1,0:T(8,128)(2,1)S(1)}, u32[]{:S(2)}, u32[]{:S(2)}) %collective-permute-start.4) | collective-permute-done | bytes 147488 | tf_op jit(solution)/shard_map/ppermute | solution.py:566
  33.9 1.9 %shard_map.137.inner_own = f32[2,512,128]{2,1,0:T(8,128)S(1)} custom-call(s32[2]{0:T(128)S(1)} %copy-done.2, bf16[4,576,128]{2,1,0:T(8,128)(2,1)S(1)} %pad_maximum_fusion.along.own_a, bf16[4,576,128]{2,1,0:T(8,128)(2,1)S(1)} %pad_maximum_fusion.1.across.own_b, bf16[256,4096]{1,0:T(8,128)(2,1)S(1)} %copy-done), custom_call_target="tpu_custom_call" | custom-call | flops 1000000000 | bytes 10000000 | tf_op jit(solution)/shard_map/pallas_call | solution.py:477
  35.9 1.9 %shard_map.138.inner_oth = f32[2,512,128]{2,1,0:T(8,128)S(1)} custom-call(s32[2]{0:T(128)S(1)} %copy-done.2, bf16[4,576,128]{2,1,0:T(8,128)(2,1)S(1)} %collective-permute-done.7.along.oth_a, bf16[4,576,128]{2,1,0:T(8,128)(2,1)S(1)} %collective-permute-done.8.across.oth_b, bf16[128,4096]{1,0:T(8,128)(2,1)S(1)} %collective-permute-done.9.x.x_got), custom_call_target="tpu_custom_call" | custom-call | flops 1000000000 | bytes 10000000 | tf_op jit(solution)/shard_map/pallas_call | solution.py:477
  37.8 17.8 %shard_map.139 = (bf16[8,192,128]{2,1,0:T(8,128)(2,1)S(1)}, bf16[8,192,128]{2,1,0:T(8,128)(2,1)S(1)}, f32[2048,128]{1,0:T(8,128)S(1)}, f32[1024,128]{1,0:T(8,128...) custom-call(s32[2]{0:T(128)S(1)} %copy-done.2, ...), custom_call_target="tpu_custom_call" | custom-call | flops 5000000000 | bytes 40000000 | tf_op jit(solution)/shard_map/pallas_call | solution.py:497
  56.2 1.3 %collective-permute-done.11 = bf16[8,192,128]{2,1,0:T(8,128)(2,1)S(1)} collective-permute-done((bf16[8,192,128]{2,1,0:T(8,128)(2,1)S(1)}, bf16[8,192,128]{2,1,0:T(8,128)(2,1)S(1)}, u32[]{:S(2)}, u32[]{:S(2)}) %collective-permute-start.11) | collective-permute-done | bytes 393248 | tf_op jit(solution)/shard_map/ppermute | solution.py:566
  58.2 4.8 %shard_map.140 = (bf16[8,256,128]{2,1,0:T(8,128)(2,1)S(1)}, f32[2048,128]{1,0:T(8,128)S(1)}) custom-call(s32[2]{0:T(128)S(1)} %copy-done.2, s32[64]{0:T(128)S(1)} %copy-done.3, f32[2048,128]{1,0:T(8,128)S(1)} %get-tuple-element.30.inner, f32[1024,128]{1,0:T(8,128)S(1)} %get-tuple-element.31.ret, bf16[2,8,256,128]{3,2,1,0:T(8,128)(2,1)S(1)} %get-tuple-element.32.t_r, ...), custom_call_target="tpu_custom_call" | custom-call | flops 5000000000 | bytes 20000000 | tf_op jit(solution)/shard_map/pallas_call | solution.py:534
  63.1 1.7 %collective-permute-done.13 = bf16[4,192,128]{2,1,0:T(8,128)(2,1)S(1)} collective-permute-done((bf16[4,192,128]{2,1,0:T(8,128)(2,1)S(1)}, bf16[4,192,128]{2,1,0:T(8,128)(2,1)S(1)}, u32[]{:S(2)}, u32[]{:S(2)}) %collective-permute-start.13) | collective-permute-done | bytes 196640 | tf_op jit(solution)/shard_map/ppermute | solution.py:566
  64.9 4.8 %shard_map.141 = (bf16[8,256,128]{2,1,0:T(8,128)(2,1)S(1)}, f32[2048,128]{1,0:T(8,128)S(1)}) custom-call(s32[2]{0:T(128)S(1)} %copy-done.2, s32[64]{0:T(128)S(1)} %copy-done.3, f32[2048,128]{1,0:T(8,128)S(1)} %get-tuple-element.30.inner, f32[1024,128]{1,0:T(8,128)S(1)} %get-tuple-element.31.ret, bf16[2,8,256,128]{3,2,1,0:T(8,128)(2,1)S(1)} %get-tuple-element.32.t_r, ...), custom_call_target="tpu_custom_call" | custom-call | flops 5000000000 | bytes 20000000 | tf_op jit(solution)/shard_map/pallas_call | solution.py:534
  69.9 3.1 %shard_map.142 = (bf16[8,128,128]{2,1,0:T(8,128)(2,1)S(1)}, bf16[8,128,128]{2,1,0:T(8,128)(2,1)S(1)}) custom-call(s32[2]{0:T(128)S(1)} %copy-done.2, f32[2048,128]{1,0:T(8,128)S(1)} %get-tuple-element.45.back, bf16[256,4096]{1,0:T(8,128)(2,1)S(1)} %copy-done, bf16[128,4096]{1,0:T(8,128)(2,1)S(1)} %collective-permute-done.9.x.x_got), custom_call_target="tpu_custom_call" | custom-call | flops 1000000000 | bytes 10000000 | tf_op jit(solution)/shard_map/pallas_call | solution.py:550
  73.7 2.6 %collective-permute-start.25 = (bf16[192,128]{1,0:T(8,128)(2,1)S(1)}, bf16[192,128]{1,0:T(8,128)(2,1)S(1)}, u32[]{:S(2)}, u32[]{:S(2)}) collective-permute-start(bf16[192,128]{1,0:T(8,128)(2,1)S(1)} %get-tuple-element.57), channel_id=1, source_target_pairs={{0,12},{2,14},{4,8},{6,10},{8,4},{10,6},{12,0},{14,2},{1,13},{3,15... | collective-permute-start | bytes 147464 | tf_op jit(solution)/shard_map/ppermute | solution.py:566
  76.3 2.0 %collective-permute-start.15 = (bf16[2,128,128]{2,1,0:T(8,128)(2,1)S(1)}, bf16[2,128,128]{2,1,0:T(8,128)(2,1)S(1)}, u32[]{:S(2)}, u32[]{:S(2)}) collective-permute-start(bf16[2,128,128]{2,1,0:T(8,128)(2,1)S(1)} %get-tuple-element.54), channel_id=1, source_target_pairs={{0,4},{2,6},{4,0},{6,2},{8,12},{10,14},{12,8},{14,10},{1,5},{3,7},... | collective-permute-start | bytes 196616 | tf_op jit(solution)/shard_map/ppermute | solution.py:566
  78.3 1.1 %collective-permute-start.16 = (bf16[2,128,128]{2,1,0:T(8,128)(2,1)S(1)}, bf16[2,128,128]{2,1,0:T(8,128)(2,1)S(1)}, u32[]{:S(2)}, u32[]{:S(2)}) collective-permute-start(bf16[2,128,128]{2,1,0:T(8,128)(2,1)S(1)} %get-tuple-element.55), channel_id=1, source_target_pairs={{0,8},{2,10},{4,12},{6,14},{8,0},{10,2},{12,4},{14,6},{1,9},{3,11}... | collective-permute-start | bytes 196616 | tf_op jit(solution)/shard_map/ppermute | solution.py:566
  79.4 2.4 %collective-permute-done.19 = bf16[4,256,128]{2,1,0:T(8,128)(2,1)S(1)} collective-permute-done((bf16[4,256,128]{2,1,0:T(8,128)(2,1)S(1)}, bf16[4,256,128]{2,1,0:T(8,128)(2,1)S(1)}, u32[]{:S(2)}, u32[]{:S(2)}) %collective-permute-start.19) | collective-permute-done | bytes 262176 | tf_op jit(solution)/shard_map/ppermute | solution.py:566
  81.8 2.5 %collective-permute-start.17 = (bf16[2,128,128]{2,1,0:T(8,128)(2,1)S(1)}, bf16[2,128,128]{2,1,0:T(8,128)(2,1)S(1)}, u32[]{:S(2)}, u32[]{:S(2)}) collective-permute-start(bf16[2,128,128]{2,1,0:T(8,128)(2,1)S(1)} %get-tuple-element.56), channel_id=1, source_target_pairs={{0,12},{2,14},{4,8},{6,10},{8,4},{10,6},{12,0},{14,2},{1,13},{3,15... | collective-permute-start | bytes 196616 | tf_op jit(solution)/shard_map/ppermute | solution.py:566
  84.5 2.5 %collective-permute-start.22 = (bf16[256,128]{1,0:T(8,128)(2,1)S(1)}, bf16[256,128]{1,0:T(8,128)(2,1)S(1)}, u32[]{:S(2)}, u32[]{:S(2)}) collective-permute-start(bf16[256,128]{1,0:T(8,128)(2,1)S(1)} %get-tuple-element.50), channel_id=1, source_target_pairs={{0,12},{2,14},{4,8},{6,10},{8,4},{10,6},{12,0},{14,2},{1,13},{3,15... | collective-permute-start | bytes 196616 | tf_op jit(solution)/shard_map/ppermute | solution.py:566
  88.5 2.7 %collective-permute-start.20 = (bf16[256,128]{1,0:T(8,128)(2,1)S(1)}, bf16[256,128]{1,0:T(8,128)(2,1)S(1)}, u32[]{:S(2)}, u32[]{:S(2)}) collective-permute-start(bf16[256,128]{1,0:T(8,128)(2,1)S(1)} %get-tuple-element.52), channel_id=1, source_target_pairs={{0,4},{2,6},{4,0},{6,2},{8,12},{10,14},{12,8},{14,10},{1,5},{3,7},... | collective-permute-start | bytes 196616 | tf_op jit(solution)/shard_map/ppermute | solution.py:566
  91.8 2.0 %collective-permute-done.21.refs_4_ = bf16[256,128]{1,0:T(8,128)(2,1)S(1)} collective-permute-done((bf16[256,128]{1,0:T(8,128)(2,1)S(1)}, bf16[256,128]{1,0:T(8,128)(2,1)S(1)}, u32[]{:S(2)}, u32[]{:S(2)}) %collective-permute-start.21) | collective-permute-done | bytes 65568 | tf_op jit(solution)/shard_map/ppermute | solution.py:566
  (57 shorter events, 10.6 us)
Async XLA Ops:
  5.1 7.4 %collective-permute-start.3 = (bf16[576,128]{1,0:T(8,128)(2,1)}, bf16[576,128]{1,0:T(8,128)(2,1)S(1)}, u32[]{:S(2)}, u32[]{:S(2)}) collective-permute-start(bf16[576,128]{1,0:T(8,128)(2,1)} %get-tuple-element.27), channel_id=1, source_target_pairs={{0,2},{2,0},{4,6},{6,4},{8,10},{10,8},{12,14},{14,12},{1,3},{3,1},... | collective-permute-start | bytes 442376 | tf_op jit(solution)/shard_map/ppermute | solution.py:566
  8.1 27.8 %collective-permute-start.9 = (bf16[128,4096]{1,0:T(8,128)(2,1)}, bf16[128,4096]{1,0:T(8,128)(2,1)S(1)}, u32[]{:S(2)}, u32[]{:S(2)}) collective-permute-start(bf16[128,4096]{1,0:T(8,128)(2,1)} %get-tuple-element.28), channel_id=1, source_target_pairs={{0,1},{1,0},{2,3},{3,2},{4,5},{5,4},{6,7},{7,6},{8,9},{9,8},{10,11... | collective-permute-start | bytes 3145736 | tf_op jit(solution)/shard_map/ppermute | solution.py:566
  8.2 8.7 %collective-permute-start.2 = (bf16[576,128]{1,0:T(8,128)(2,1)}, bf16[576,128]{1,0:T(8,128)(2,1)S(1)}, u32[]{:S(2)}, u32[]{:S(2)}) collective-permute-start(bf16[576,128]{1,0:T(8,128)(2,1)} %get-tuple-element.27), channel_id=1, source_target_pairs={{0,12},{2,14},{4,8},{6,10},{8,4},{10,6},{12,0},{14,2},{1,13},{3,15... | collective-permute-start | bytes 442376 | tf_op jit(solution)/shard_map/ppermute | solution.py:566
  11.8 13.4 %collective-permute-start.1 = (bf16[576,128]{1,0:T(8,128)(2,1)}, bf16[576,128]{1,0:T(8,128)(2,1)S(1)}, u32[]{:S(2)}, u32[]{:S(2)}) collective-permute-start(bf16[576,128]{1,0:T(8,128)(2,1)} %get-tuple-element.27), channel_id=1, source_target_pairs={{0,8},{2,10},{4,12},{6,14},{8,0},{10,2},{12,4},{14,6},{1,9},{3,11}... | collective-permute-start | bytes 442376 | tf_op jit(solution)/shard_map/ppermute | solution.py:566
  11.8 13.9 %collective-permute-start = (bf16[576,128]{1,0:T(8,128)(2,1)}, bf16[576,128]{1,0:T(8,128)(2,1)S(1)}, u32[]{:S(2)}, u32[]{:S(2)}) collective-permute-start(bf16[576,128]{1,0:T(8,128)(2,1)} %get-tuple-element.27), channel_id=1, source_target_pairs={{0,4},{2,6},{4,0},{6,2},{8,12},{10,14},{12,8},{14,10},{1,5},{3,7},... | collective-permute-start | bytes 442376 | tf_op jit(solution)/shard_map/ppermute | solution.py:566
  12.5 25.3 %collective-permute-start.10 = (bf16[128,4096]{1,0:T(8,128)(2,1)}, bf16[128,4096]{1,0:T(8,128)(2,1)S(1)}, u32[]{:S(2)}, u32[]{:S(2)}) collective-permute-start(bf16[128,4096]{1,0:T(8,128)(2,1)} %get-tuple-element.29), channel_id=1, source_target_pairs={{0,1},{1,0},{2,3},{3,2},{4,5},{5,4},{6,7},{7,6},{8,9},{9,8},{10,11... | collective-permute-start | bytes 3145736 | tf_op jit(solution)/shard_map/ppermute | solution.py:566
  16.9 11.2 %collective-permute-start.6 = (bf16[576,128]{1,0:T(8,128)(2,1)S(1)}, bf16[576,128]{1,0:T(8,128)(2,1)S(1)}, u32[]{:S(2)}, u32[]{:S(2)}) collective-permute-start(bf16[576,128]{1,0:T(8,128)(2,1)S(1)} %collective-permute-done.2), channel_id=1, source_target_pairs={{0,2},{2,0},{4,6},{6,4},{8,10},{10,8},{12,14},{14,12},{1,3},{3,1},... | collective-permute-start | bytes 442376 | tf_op jit(solution)/shard_map/ppermute | solution.py:566
  25.1 6.8 %collective-permute-start.5 = (bf16[576,128]{1,0:T(8,128)(2,1)S(1)}, bf16[576,128]{1,0:T(8,128)(2,1)S(1)}, u32[]{:S(2)}, u32[]{:S(2)}) collective-permute-start(bf16[576,128]{1,0:T(8,128)(2,1)S(1)} %collective-permute-done.1), channel_id=1, source_target_pairs={{0,2},{2,0},{4,6},{6,4},{8,10},{10,8},{12,14},{14,12},{1,3},{3,1},... | collective-permute-start | bytes 442376 | tf_op jit(solution)/shard_map/ppermute | solution.py:566
  25.7 8.1 %collective-permute-start.4 = (bf16[576,128]{1,0:T(8,128)(2,1)S(1)}, bf16[576,128]{1,0:T(8,128)(2,1)S(1)}, u32[]{:S(2)}, u32[]{:S(2)}) collective-permute-start(bf16[576,128]{1,0:T(8,128)(2,1)S(1)} %collective-permute-done), channel_id=1, source_target_pairs={{0,2},{2,0},{4,6},{6,4},{8,10},{10,8},{12,14},{14,12},{1,3},{3,1},... | collective-permute-start | bytes 442376 | tf_op jit(solution)/shard_map/ppermute | solution.py:566
  28.1 7.7 %collective-permute-start.7 = (bf16[4,576,128]{2,1,0:T(8,128)(2,1)S(1)}, bf16[4,576,128]{2,1,0:T(8,128)(2,1)S(1)}, u32[]{:S(2)}, u32[]{:S(2)}) collective-permute-start(bf16[4,576,128]{2,1,0:T(8,128)(2,1)S(1)} %pad_maximum_fusion.along.own_a), channel_id=1, source_target_pairs={{0,1},{1,0},{2,3},{3,2},{4,5},{5,4},{6,7},{7,6},{8,9},{9,8},{10,11... | collective-permute-start | bytes 1769480 | tf_op jit(solution)/shard_map/ppermute | solution.py:566
  57.6 7.2 %collective-permute-start.13 = (bf16[4,192,128]{2,1,0:T(8,128)(2,1)S(1)}, bf16[4,192,128]{2,1,0:T(8,128)(2,1)S(1)}, u32[]{:S(2)}, u32[]{:S(2)}) collective-permute-start(bf16[4,192,128]{2,1,0:T(8,128)(2,1)S(1)} %add_convert_fusion.6), channel_id=1, source_target_pairs={{0,2},{2,0},{4,6},{6,4},{8,10},{10,8},{12,14},{14,12},{1,3},{3,1},... | collective-permute-start | bytes 589832 | tf_op jit(solution)/shard_map/ppermute | solution.py:566
  63.0 6.8 %collective-permute-start.12 = (bf16[8,256,128]{2,1,0:T(8,128)(2,1)S(1)}, bf16[8,256,128]{2,1,0:T(8,128)(2,1)S(1)}, u32[]{:S(2)}, u32[]{:S(2)}) collective-permute-start(bf16[8,256,128]{2,1,0:T(8,128)(2,1)S(1)} %get-tuple-element.44), channel_id=1, source_target_pairs={{0,1},{1,0},{2,3},{3,2},{4,5},{5,4},{6,7},{7,6},{8,9},{9,8},{10,11... | collective-permute-start | bytes 1572872 | tf_op jit(solution)/shard_map/ppermute | solution.py:566
  73.0 3.3 %collective-permute-start.14 = (bf16[8,128,128]{2,1,0:T(8,128)(2,1)S(1)}, bf16[8,128,128]{2,1,0:T(8,128)(2,1)S(1)}, u32[]{:S(2)}, u32[]{:S(2)}) collective-permute-start(bf16[8,128,128]{2,1,0:T(8,128)(2,1)S(1)} %get-tuple-element.47), channel_id=1, source_target_pairs={{0,1},{1,0},{2,3},{3,2},{4,5},{5,4},{6,7},{7,6},{8,9},{9,8},{10,11... | collective-permute-start | bytes 786440 | tf_op jit(solution)/shard_map/ppermute | solution.py:566
  73.1 8.7 %collective-permute-start.19 = (bf16[4,256,128]{2,1,0:T(8,128)(2,1)S(1)}, bf16[4,256,128]{2,1,0:T(8,128)(2,1)S(1)}, u32[]{:S(2)}, u32[]{:S(2)}) collective-permute-start(bf16[4,256,128]{2,1,0:T(8,128)(2,1)S(1)} %add_convert_fusion.3), channel_id=1, source_target_pairs={{0,2},{2,0},{4,6},{6,4},{8,10},{10,8},{12,14},{14,12},{1,3},{3,1},... | collective-permute-start | bytes 786440 | tf_op jit(solution)/shard_map/ppermute | solution.py:566
  73.7 14.8 %collective-permute-start.25 = (bf16[192,128]{1,0:T(8,128)(2,1)S(1)}, bf16[192,128]{1,0:T(8,128)(2,1)S(1)}, u32[]{:S(2)}, u32[]{:S(2)}) collective-permute-start(bf16[192,128]{1,0:T(8,128)(2,1)S(1)} %get-tuple-element.57), channel_id=1, source_target_pairs={{0,12},{2,14},{4,8},{6,10},{8,4},{10,6},{12,0},{14,2},{1,13},{3,15... | collective-permute-start | bytes 147464 | tf_op jit(solution)/shard_map/ppermute | solution.py:566
  76.2 14.9 %collective-permute-start.24 = (bf16[192,128]{1,0:T(8,128)(2,1)S(1)}, bf16[192,128]{1,0:T(8,128)(2,1)S(1)}, u32[]{:S(2)}, u32[]{:S(2)}) collective-permute-start(bf16[192,128]{1,0:T(8,128)(2,1)S(1)} %get-tuple-element.58), channel_id=1, source_target_pairs={{0,8},{2,10},{4,12},{6,14},{8,0},{10,2},{12,4},{14,6},{1,9},{3,11}... | collective-permute-start | bytes 147464 | tf_op jit(solution)/shard_map/ppermute | solution.py:566
  76.3 8.1 %collective-permute-start.15 = (bf16[2,128,128]{2,1,0:T(8,128)(2,1)S(1)}, bf16[2,128,128]{2,1,0:T(8,128)(2,1)S(1)}, u32[]{:S(2)}, u32[]{:S(2)}) collective-permute-start(bf16[2,128,128]{2,1,0:T(8,128)(2,1)S(1)} %get-tuple-element.54), channel_id=1, source_target_pairs={{0,4},{2,6},{4,0},{6,2},{8,12},{10,14},{12,8},{14,10},{1,5},{3,7},... | collective-permute-start | bytes 196616 | tf_op jit(solution)/shard_map/ppermute | solution.py:566
  78.3 6.2 %collective-permute-start.16 = (bf16[2,128,128]{2,1,0:T(8,128)(2,1)S(1)}, bf16[2,128,128]{2,1,0:T(8,128)(2,1)S(1)}, u32[]{:S(2)}, u32[]{:S(2)}) collective-permute-start(bf16[2,128,128]{2,1,0:T(8,128)(2,1)S(1)} %get-tuple-element.55), channel_id=1, source_target_pairs={{0,8},{2,10},{4,12},{6,14},{8,0},{10,2},{12,4},{14,6},{1,9},{3,11}... | collective-permute-start | bytes 196616 | tf_op jit(solution)/shard_map/ppermute | solution.py:566
  81.8 6.1 %collective-permute-start.17 = (bf16[2,128,128]{2,1,0:T(8,128)(2,1)S(1)}, bf16[2,128,128]{2,1,0:T(8,128)(2,1)S(1)}, u32[]{:S(2)}, u32[]{:S(2)}) collective-permute-start(bf16[2,128,128]{2,1,0:T(8,128)(2,1)S(1)} %get-tuple-element.56), channel_id=1, source_target_pairs={{0,12},{2,14},{4,8},{6,10},{8,4},{10,6},{12,0},{14,2},{1,13},{3,15... | collective-permute-start | bytes 196616 | tf_op jit(solution)/shard_map/ppermute | solution.py:566
  84.4 7.4 %collective-permute-start.23 = (bf16[192,128]{1,0:T(8,128)(2,1)S(1)}, bf16[192,128]{1,0:T(8,128)(2,1)S(1)}, u32[]{:S(2)}, u32[]{:S(2)}) collective-permute-start(bf16[192,128]{1,0:T(8,128)(2,1)S(1)} %get-tuple-element.59), channel_id=1, source_target_pairs={{0,4},{2,6},{4,0},{6,2},{8,12},{10,14},{12,8},{14,10},{1,5},{3,7},... | collective-permute-start | bytes 147464 | tf_op jit(solution)/shard_map/ppermute | solution.py:566
  84.5 7.3 %collective-permute-start.22 = (bf16[256,128]{1,0:T(8,128)(2,1)S(1)}, bf16[256,128]{1,0:T(8,128)(2,1)S(1)}, u32[]{:S(2)}, u32[]{:S(2)}) collective-permute-start(bf16[256,128]{1,0:T(8,128)(2,1)S(1)} %get-tuple-element.50), channel_id=1, source_target_pairs={{0,12},{2,14},{4,8},{6,10},{8,4},{10,6},{12,0},{14,2},{1,13},{3,15... | collective-permute-start | bytes 196616 | tf_op jit(solution)/shard_map/ppermute | solution.py:566
  87.9 6.0 %collective-permute-start.21 = (bf16[256,128]{1,0:T(8,128)(2,1)S(1)}, bf16[256,128]{1,0:T(8,128)(2,1)S(1)}, u32[]{:S(2)}, u32[]{:S(2)}) collective-permute-start(bf16[256,128]{1,0:T(8,128)(2,1)S(1)} %get-tuple-element.51), channel_id=1, source_target_pairs={{0,8},{2,10},{4,12},{6,14},{8,0},{10,2},{12,4},{14,6},{1,9},{3,11}... | collective-permute-start | bytes 196616 | tf_op jit(solution)/shard_map/ppermute | solution.py:566
  88.5 5.8 %collective-permute-start.20 = (bf16[256,128]{1,0:T(8,128)(2,1)S(1)}, bf16[256,128]{1,0:T(8,128)(2,1)S(1)}, u32[]{:S(2)}, u32[]{:S(2)}) collective-permute-start(bf16[256,128]{1,0:T(8,128)(2,1)S(1)} %get-tuple-element.52), channel_id=1, source_target_pairs={{0,4},{2,6},{4,0},{6,2},{8,12},{10,14},{12,8},{14,10},{1,5},{3,7},... | collective-permute-start | bytes 196616 | tf_op jit(solution)/shard_map/ppermute | solution.py:566
  91.2 4.0 %collective-permute-start.18 = (bf16[128,128]{1,0:T(8,128)(2,1)S(1)}, bf16[128,128]{1,0:T(8,128)(2,1)S(1)}, u32[]{:S(2)}, u32[]{:S(2)}) collective-permute-start(bf16[128,128]{1,0:T(8,128)(2,1)S(1)} %get-tuple-element.61), channel_id=1, source_target_pairs={{0,2},{2,0},{4,6},{6,4},{8,10},{10,8},{12,14},{14,12},{1,3},{3,1},... | collective-permute-start | bytes 98312 | tf_op jit(solution)/shard_map/ppermute | solution.py:566
  (6 other events, 78.0 us)

commit v4 on v3

--- a/solution.py
+++ b/solution.py
@@ -19,6 +19,7 @@
 f32 = jnp.float32
 bf16 = jnp.bfloat16
 
+STEPS = (0, 2, 1, 3)
 FIRST = 128
 REST = 448
 RD_AT = 256
@@ -68,20 +69,12 @@
     return jnp.concatenate(parts, axis=1)
 
 
-def prepare_body(where, *refs):
-    shards, (x, y, packed, x_out, y_out), (lg, rg, lu, ru, ld, rd) = refs[:6], refs[6:11], refs[11:17]
-    sems, shard_sems = refs[17:]
-    half = x_out.shape[0]
-    off = pl.multiple_of((1 - where[1]) * half, half)
+def prepare_body(*refs):
+    shards, packed, (lg, rg, lu, ru, ld, rd), sems = refs[:6], refs[6], refs[7:13], refs[13]
     loads = [
-        pltpu.make_async_copy(shard, ref, shard_sems.at[i])
-        for i, (shard, ref) in enumerate(zip(shards, refs[11:17]))
+        pltpu.make_async_copy(shard, ref, sems.at[i]) for i, (shard, ref) in enumerate(zip(shards, refs[7:13]))
     ]
-    copies = [
-        pltpu.make_async_copy(x.at[pl.ds(off, half), :], x_out, sems.at[0]),
-        pltpu.make_async_copy(y.at[pl.ds(off, half), :], y_out, sems.at[1]),
-    ]
-    for copy in loads + copies:
+    for copy in loads:
         copy.start()
     for copy in loads:
         copy.wait()
@@ -106,8 +99,6 @@
     for g in range(4):
         part = jnp.concatenate([q[g] for q in quarters], axis=0).astype(bf16)
         packed[pl.ds(FIRST + LD_AT + g * 32, 32), :] = part
-    for copy in copies:
-        copy.wait()
 
 
 def finish_body(first, rights, downs, lg, rg, lu, ru, ld, rd):
@@ -174,29 +165,30 @@
     return [jnp.where(slot == u, 1.0, 0.0).astype(bf16) for u in range(GROUP)]
 
 
+def tokens_at(ref, side, toks):
+    return pl.ds(0, toks) if ref.shape[0] == toks else pl.ds(pl.multiple_of(side * toks, toks), toks)
+
+
 def chunk_of(me, r):
-    return me ^ (2 * (r % 4)) ^ (r // 4)
-
-
-def inner_body(other, where, along, across, x, inner, t_l, xs, sem):
-    me, side = where[0], where[1]
-    toks = xs.shape[0]
-    off = 0 if other else pl.multiple_of(side * toks, toks)
-    copy = pltpu.make_async_copy(x.at[pl.ds(off, toks), :], xs, sem)
-    copy.start()
+    return me ^ (2 * STEPS[r % 4]) ^ (r // 4)
+
+
+def inner_body(where, along, across, x, inner, t_l):
+    me = where[0]
+    toks = inner.shape[2]
+    at = tokens_at(x, where[1], toks)
     masks = [jnp.concatenate([mask, mask], axis=1) for mask in unit_masks()]
     for r in range(CHUNKS):
         piece = (along, across)[r // 4]
         for gg in range(8):
             t_l[gg, rows(chunk_of(me, r)), :] = piece[r % 4, pl.ds(gg * 16, 16), :]
-    copy.wait()
 
     def step(i, _):
         both = jnp.concatenate([t_l[i], t_l[4 + i]], axis=1)
         total = jnp.zeros((toks, 256), f32)
         for p in range(GROUP // 2):
             w = jnp.concatenate([both * masks[2 * p + h] for h in range(2)], axis=0)
-            total += nn(xs[:, lanes(i * GROUP // 2 + p, 256)], w)
+            total += nn(x[at, lanes(i * GROUP // 2 + p, 256)], w)
         for gu in range(2):
             inner[gu, rows(i, 128), :] = rounded(total[:, gu * 128 : (gu + 1) * 128].T)
         return 0
@@ -213,16 +205,11 @@
 def middle_body(
     scale, where, order, own_a, own_b, oth_a, oth_b, inner_own, inner_oth, y, y_got, keep, send,
     inner, ret, t_r, n_ld, act_own, act_oth, slope_own, slope_oth,
-    ys, sems, r_lo, r_hi, s_rd, n_r, n_rd, t_rd, t_ld, g_out, down, hid_s,
+    r_lo, r_hi, s_rd, n_r, n_rd, t_rd, t_ld, g_out, down, hid_s,
 ):
     me, side = where[0], where[1]
-    toks = ys.shape[1]
-    copies = [
-        pltpu.make_async_copy(y.at[pl.ds(pl.multiple_of(side * toks, toks), toks), :], ys.at[0], sems.at[0]),
-        pltpu.make_async_copy(y_got, ys.at[1], sems.at[1]),
-    ]
-    for copy in copies:
-        copy.start()
+    toks = inner.shape[1]
+    ats = [tokens_at(v, side, toks) for v in (y, y_got)]
     masks = unit_masks()
     s_r = (r_lo, r_hi)
     for gu in range(2):
@@ -301,7 +288,6 @@
             g_out[b, pl.ds(base + al * HALF, 8, stride=DOWN), :] = value[al * 8 : (al + 1) * 8]
 
     for b in range(2):
-        copies[b].wait()
 
         def third(i, _, b=b):
             g = (side ^ b) * 4 + i
@@ -310,7 +296,7 @@
             student = nn(spread(turned, masks), n_rd[g])
             deltas = []
             for u, k in blocks(g):
-                target = ys[b, :, lanes(i * GROUP + u)].astype(f32)
+                target = (y, y_got)[b][ats[b], lanes(i * GROUP + u)].astype(f32)
                 part = student[u * toks : (u + 1) * toks]
                 deltas.append(((part - target) * scale).astype(bf16))
             total = chosen(nn(jnp.concatenate(deltas, axis=0), t_rd[g]), toks)
@@ -397,19 +383,13 @@
         grads_out[r] = g_out[rows(chunk_of(me, r), RIGHT), :].astype(bf16)
 
 
-def left_body(where, back, x, x_got, keep, send, turned, xs, sems):
+def left_body(where, back, x, x_got, keep, send, turned):
     me, side = where[0], where[1]
-    toks = xs.shape[1]
-    copies = [
-        pltpu.make_async_copy(x.at[pl.ds(pl.multiple_of(side * toks, toks), toks), :], xs.at[0], sems.at[0]),
-        pltpu.make_async_copy(x_got, xs.at[1], sems.at[1]),
-    ]
-    for copy in copies:
-        copy.start()
-    for b, out in enumerate([keep, send]):
-        copies[b].wait()
-
-        def step(i, _, b=b):
+    toks = back.shape[1]
+    ats = [tokens_at(v, side, toks) for v in (x, x_got)]
+    for b, (ref, out) in enumerate([(x, keep), (x_got, send)]):
+
+        def step(i, _, b=b, ref=ref):
             parts = ([], [])
             for q in range(2):
                 both = []
@@ -418,7 +398,7 @@
                     both += [back[rows(j), :], back[rows(j + NB), :]]
                 both = jnp.concatenate(both, axis=0).astype(bf16)
                 at = i * 4 + 2 * q
-                x4 = jnp.concatenate([xs[b, :, lanes(at, 256)], xs[b, :, lanes(at + 1, 256)]], axis=0)
+                x4 = jnp.concatenate([ref[ats[b], lanes(at, 256)], ref[ats[b], lanes(at + 1, 256)]], axis=0)
                 grads = nn(crossed_pair(both[:64], both[64:]), x4)
                 for e in range(4):
                     for gu in range(2):
@@ -446,17 +426,15 @@
 VMEM_RIGHT = 10 * 2**20
 
 
-def prepare_call(where, factors, x, y):
-    sent = jax.ShapeDtypeStruct((x.shape[0] // 2, x.shape[1]), bf16)
+def prepare_call(factors):
     return pl.pallas_call(
         prepare_body,
-        out_shape=(jax.ShapeDtypeStruct((FIRST + REST, 128), bf16), sent, sent),
-        in_specs=[SMEM] + [HBM] * 8,
-        out_specs=(VMEM, VMEM, VMEM),
-        scratch_shapes=[pltpu.VMEM(v.shape, bf16) for v in factors]
-        + [pltpu.SemaphoreType.DMA((2,)), pltpu.SemaphoreType.DMA((6,))],
+        out_shape=jax.ShapeDtypeStruct((FIRST + REST, 128), bf16),
+        in_specs=[HBM] * 6,
+        out_specs=VMEM,
+        scratch_shapes=[pltpu.VMEM(v.shape, bf16) for v in factors] + [pltpu.SemaphoreType.DMA((6,))],
         compiler_params=pltpu.CompilerParams(vmem_limit_bytes=60 * 2**20),
-    )(where, *factors, x, y)
+    )(*factors)
 
 
 def finish_call(first, rights, downs):
@@ -472,26 +450,22 @@
     )(*first, *rights, *downs)
 
 
-def inner_call(other, where, along, across, x, toks):
+def inner_call(where, along, across, x, toks):
     front = pl.BlockSpec((4, FIRST, 128), lambda i: (0, 0, 0))
     return pl.pallas_call(
-        functools.partial(inner_body, other),
+        inner_body,
         grid=(1,),
         out_shape=jax.ShapeDtypeStruct((2, NB * RANK // 2, toks), f32),
-        in_specs=[SMEM, front, front, ANY],
+        in_specs=[SMEM, front, front, VMEM],
         out_specs=VMEM,
-        scratch_shapes=[
-            pltpu.VMEM((8, BIN, 128), bf16),
-            pltpu.VMEM((toks, x.shape[1]), bf16),
-            pltpu.SemaphoreType.DMA,
-        ],
-        compiler_params=pltpu.CompilerParams(vmem_limit_bytes=16 * 2**20),
+        scratch_shapes=[pltpu.VMEM((8, BIN, 128), bf16)],
+        compiler_params=pltpu.CompilerParams(vmem_limit_bytes=10 * 2**20),
         cost_estimate=pl.CostEstimate(flops=10**9, bytes_accessed=10**7, transcendentals=0),
     )(where, along, across, x)
 
 
 def middle_call(scale, where, order, pieces, inner, y, y_got):
-    toks = y_got.shape[0]
+    toks = y_got.shape[0] // 2
     down = jax.ShapeDtypeStruct((CHUNKS, DOWN, 128), bf16)
     kept = jax.ShapeDtypeStruct((HALF, toks, WIDE), f32)
     return pl.pallas_call(
@@ -508,11 +482,9 @@
             kept,
             kept,
         ),
-        in_specs=[SMEM, SMEM] + [VMEM] * 6 + [ANY] * 2,
+        in_specs=[SMEM, SMEM] + [VMEM] * 8,
         out_specs=(VMEM,) * 10,
         scratch_shapes=[
-            pltpu.VMEM((2,) + y_got.shape, bf16),
-            pltpu.SemaphoreType.DMA((2,)),
             pltpu.VMEM((RANK * 128, 128), f32),
             pltpu.VMEM((RANK * 128, 128), f32),
             pltpu.VMEM((RANK * NB, 128), f32),
@@ -550,12 +522,10 @@
     return pl.pallas_call(
         left_body,
         out_shape=(grads, grads),
-        in_specs=[SMEM, VMEM, ANY, ANY],
+        in_specs=[SMEM] + [VMEM] * 3,
         out_specs=(VMEM, VMEM),
         scratch_shapes=[
             pltpu.VMEM((8 * 128, 128), bf16),
-            pltpu.VMEM((2,) + x_got.shape, bf16),
-            pltpu.SemaphoreType.DMA((2,)),
         ],
         compiler_params=pltpu.CompilerParams(vmem_limit_bytes=16 * 2**20),
         cost_estimate=pl.CostEstimate(flops=10**9, bytes_accessed=10**7, transcendentals=0),
@@ -571,10 +541,12 @@
 
 
 def gathered(mine, n):
-    along = [mine] + [swap(mine, "dp", 2 * s, n) for s in range(1, 4)]
-    across = [swap(v, "dp", 1, n) for v in along]
-    along, across = jnp.stack(along), jnp.stack(across)
-    return along, across, sibling(along), sibling(across)
+    z1, z2, z3 = [swap(mine, "dp", 2 * s, n) for s in range(1, 4)]
+    x0, x1, x2, x3 = [swap(v, "dp", 1, n) for v in (mine, z1, z2, z3)]
+    pair = (x0, x1)
+    along = jnp.stack([mine, z2, z1, z3])
+    across = jnp.stack([pair[0], x2, pair[1], x3])
+    return (z1, z3), along, across, sibling(along), sibling(across)
 
 
 def add(a, b):
@@ -585,18 +557,17 @@
     return lax.optimization_barrier((value,) + others)[0]
 
 
-def along_z(line, n):
-    return [swap(line[s], "dp", 2 * s, n) for s in range(1, 4)]
-
-
-def by_z_then_x(keep, got, n):
-    both = add(keep, got)
-    both = both.reshape((2, 4) + both.shape[1:])
-    pair = both[:, 0].astype(f32)
-    for s in range(1, 4):
-        pair = pair + swap(both[:, s], "dp", 2 * s, n).astype(f32)
-    pair = pair.astype(bf16)
-    return [pair[0], swap(pair[1], "dp", 1, n)]
+def over_x(keep, got, n):
+    away = add(keep[4:], got[4:])
+    return away, swap(away, "dp", 1, n)
+
+
+def line_of(keep, got, crossed):
+    return (keep[:4].astype(f32) + got[:4].astype(f32) + crossed.astype(f32)).astype(bf16)
+
+
+def over_z(line, n):
+    return add(line[:2], swap(line[2:], "dp", 2, n))
 
 
 def on_device(activations, teacher_out, block_order, *factors):
@@ -608,53 +579,55 @@
     direct = n == CHUNKS
     if direct:
         where = jnp.stack([me, side]).astype(jnp.int32)
-        mine, x_sent, y_sent = prepare_call(where, factors, activations, teacher_out)
-        pieces = gathered(mine, n)
+        ready, *pieces = gathered(prepare_call(factors), n)
+        start = side * toks
     else:
+        start = side * toks
         where = jnp.stack([jnp.zeros_like(side), side]).astype(jnp.int32)
         whole = [lax.all_gather(v, "dp", axis=1, tiled=True) for v in factors]
         cut = [jnp.moveaxis(v.reshape(HALF, CHUNKS, -1), 1, 0) for v in whole]
         packed = jnp.concatenate(jax.vmap(pack)(*cut), axis=1)
-        pieces = (packed[0::2], packed[1::2], sibling(packed[0::2]), sibling(packed[1::2]))
-        x_sent, y_sent = [
-            lax.dynamic_slice_in_dim(v, (1 - side) * toks, toks, 0) for v in (activations, teacher_out)
-        ]
-    x_got, y_got = sibling(x_sent), sibling(y_sent)
+        packed = packed.reshape((4, 2) + packed.shape[1:])[jnp.array(STEPS)]
+        pieces = (packed[:, 0], packed[:, 1], sibling(packed[:, 0]), sibling(packed[:, 1]))
+    x, y = [lax.dynamic_slice_in_dim(v, start, toks, 0) for v in (activations, teacher_out)]
+    x_got, y_got = sibling(activations), sibling(teacher_out)
     inner = (
-        inner_call(False, where, pieces[0], pieces[1], activations, toks),
-        inner_call(True, where, pieces[2], pieces[3], x_got, toks),
+        inner_call(where, pieces[0], pieces[1], x, toks),
+        inner_call(where, pieces[2], pieces[3], x_got, toks),
     )
-    keep, send, *state = middle_call(scale, where, block_order, pieces, inner, teacher_out, y_got)
+    keep, send, *state = middle_call(scale, where, block_order, pieces, inner, y, y_got)
     shared, (act_own, act_oth, slope_own, slope_oth) = state[:4], state[4:]
     got = sibling(send)
     right_send, back = right_call(1, where, block_order, *shared, act_oth, slope_oth)
     right_got = sibling(right_send)
     if direct:
-        away = add(keep[4:], got[4:])
-        here = add(keep[:4], got[:4])
-        crossed = swap(away, "dp", 1, n)
-        back = tie(back, away, here)
+        _, crossed = over_x(keep, got, n)
+        line = line_of(keep, got, crossed)
+        back = tie(back, line)
     right_keep, back = right_call(0, where, block_order, *shared, act_own, slope_own, back)
     if direct:
-        right_away = add(right_keep[4:], right_got[4:])
-        right_here = add(right_keep[:4], right_got[:4])
-        right_crossed = swap(right_away, "dp", 1, n)
-        line = add(here, crossed)
-        down = [line[0]] + along_z(line, n)
-        back = tie(back, right_away, line)
-    left_keep, left_send = left_call(where, back, activations, x_got)
+        half = over_z(line, n)
+        right_away, right_crossed = over_x(right_keep, right_got, n)
+        back = tie(back, half, right_away)
+    left_keep, left_send = left_call(where, back, x, x_got)
     left_got = sibling(left_send)
     if direct:
-        right_line = add(right_here, right_crossed)
-        right = [right_line[0]] + along_z(right_line, n)
-        left = by_z_then_x(left_keep, left_got, n)
+        down = [half[0], swap(half[1], "dp", 4, n)]
+        left_got = tie(left_got, down[1])
+        right_half = over_z(line_of(right_keep, right_got, right_crossed), n)
+        left_away = tie(add(left_keep[4:], left_got[4:]), right_crossed)
+        left_crossed = swap(left_away, "dp", 1, n)
+        left_half = over_z(line_of(left_keep, left_got, left_crossed), n)
+        right = [right_half[0], swap(right_half[1], "dp", 4, n)]
+        left = [left_half[0], swap(left_half[1], "dp", 4, n)]
         return finish_call(left, right, down)
     rest = (jnp.concatenate([right_keep, keep], axis=1), jnp.concatenate([right_got, got], axis=1))
     sums = []
     rest = [jnp.concatenate(v, axis=1) for v in ((right_keep, keep), (right_send, send))]
     for own, away in ((left_keep, left_got), rest):
         total = own.astype(f32) + away.astype(f32)
-        sums.append(jnp.stack([total[:4], total[4:]], axis=1).reshape(total.shape))
+        ranks = jnp.array(STEPS)
+        sums.append(jnp.stack([total[:4][ranks], total[4:][ranks]], axis=1).reshape(total.shape))
     parts = jax.vmap(unpack)(*sums)
     parts = [jnp.moveaxis(v, 0, 1).reshape(HALF, -1) for v in parts]
     return tuple(lax.psum_scatter(v, "dp", scatter_dimension=1, tiled=True) for v in parts)

time: 96.5 us -> 92.4 us (0.958)
  starting transfers between devices: 26.4 us -> 22.8 us
  Pallas kernels: 39.3 us -> 37.7 us
  local copies, waits for them, and re-layouts: 0.07 us -> 1.5 us
    ppermute x26 -> x23, starting transfers between devices: 26.4 us -> 22.8 us  [swap(): return lax.ppermute(v, axis, [(i, i ^ bit) for i in range(size)])]
    pallas_call x4, Pallas kernels: 10.8 us -> 8.38 us  [the longest x2 3.64 us: inner_call(): pl.pallas_call(inner_body, grid=(1,), out_shape=jax.ShapeDtypeStruct((2,...]
    dynamic_slice x0 -> x1, local copies, waits for them, and re-layouts: none -> 1.44 us  [on_device(): lax.dynamic_slice_in_dim(v, start, toks, 0)]
    ppermute x26 -> x23, waiting for transfers between devices: 27.4 us -> 27.4 us  [swap(): return lax.ppermute(v, axis, [(i, i ^ bit) for i in range(size)])]
  transfers between devices with their start and end apart: 26 -> 23, of which waited for: 12 -> 14; matrix products, arithmetic and copies ran while one was open for 1% -> 3% of each run, Pallas kernels for 14% -> 20%
where the time goes in v4:
time: 92.4 us; the launch traced here: 92.1 us
  Pallas kernels  37.7 us (41%)
  waiting for transfers between devices  27.4 us (30%)
  starting transfers between devices  22.8 us (25%)
  other arithmetic  1.78 us (2%)
  local copies, waits for them, and re-layouts  1.5 us (2%)
    ppermute x23, waiting for transfers between devices, swap(): return lax.ppermute(v, axis, [(i, i ^ bit) for i in range(size)])  27.4 us
    ppermute x23, starting transfers between devices, swap(): return lax.ppermute(v, axis, [(i, i ^ bit) for i in range(size)])  22.8 us
    pallas_call x1, Pallas kernels, middle_call(): pl.pallas_call(functools.partial(middle_body, scale), out_shape=(down, do...  18.7 us
    pallas_call x2, Pallas kernels, right_call(): pl.pallas_call(functools.partial(right_body, b), out_shape=(jax.ShapeDtyp...  9.6 us
    pallas_call x2, Pallas kernels, inner_call(): pl.pallas_call(inner_body, grid=(1,), out_shape=jax.ShapeDtypeStruct((2,...  3.64 us
    pallas_call x1, Pallas kernels, left_call(): pl.pallas_call(left_body, out_shape=(grads, grads), in_specs=[SMEM] + [VM...  2.95 us
  transfers between devices with their start and end apart: 23, of which 14 were waited for; matrix products, arithmetic and copies ran while one was open for 3% of the time, Pallas kernels for 20%

profile of v4, /device:TPU:0, one launch (start us, length us, event | category | flops | bytes accessed | tf_op | source)
XLA Modules:
  0.0 92.1 jit_solution(15473286530584325754)
XLA Ops:
  1.2 1.8 %shard_map.136 = bf16[576,128]{1,0:T(8,128)(2,1)} custom-call(bf16[32,256]{1,0:T(8,128)(2,1)} %refs_0_.1, bf16[32,448]{1,0:T(8,128)(2,1)} %refs_1_.1, bf16[32,256]{1,0:T(8,128)(2,1)} %refs_2_.1, bf16[32,448]{1,0:T(8,128)(2,1)} %refs_3_.1, bf16[32,448]{1,0:T(8,128)(2,1)} %refs_4_.1, bf16[32,256]{1,0:T(8,128)(2,1)} %refs_5_.1), custom_call_target="tpu_custom_call" | custom-call | tf_op jit(solution)/shard_map/pallas_call | solution.py:430
  3.0 3.0 %collective-permute-start.3 = (bf16[576,128]{1,0:T(8,128)(2,1)}, bf16[576,128]{1,0:T(8,128)(2,1)S(1)}, u32[]{:S(2)}, u32[]{:S(2)}) collective-permute-start(bf16[576,128]{1,0:T(8,128)(2,1)} %shard_map.136), channel_id=1, source_target_pairs={{0,2},{2,0},{4,6},{6,4},{8,10},{10,8},{12,14},{14,12},{1,3},{3,1},... | collective-permute-start | bytes 442376 | tf_op jit(solution)/shard_map/ppermute | solution.py:536
  6.0 3.6 %collective-permute-start.2 = (bf16[576,128]{1,0:T(8,128)(2,1)}, bf16[576,128]{1,0:T(8,128)(2,1)S(1)}, u32[]{:S(2)}, u32[]{:S(2)}) collective-permute-start(bf16[576,128]{1,0:T(8,128)(2,1)} %shard_map.136), channel_id=1, source_target_pairs={{0,12},{2,14},{4,8},{6,10},{8,4},{10,6},{12,0},{14,2},{1,13},{3,15... | collective-permute-start | bytes 442376 | tf_op jit(solution)/shard_map/ppermute | solution.py:536
  10.3 2.8 %collective-permute-start = (bf16[576,128]{1,0:T(8,128)(2,1)}, bf16[576,128]{1,0:T(8,128)(2,1)S(1)}, u32[]{:S(2)}, u32[]{:S(2)}) collective-permute-start(bf16[576,128]{1,0:T(8,128)(2,1)} %shard_map.136), channel_id=1, source_target_pairs={{0,8},{2,10},{4,12},{6,14},{8,0},{10,2},{12,4},{14,6},{1,9},{3,11}... | collective-permute-start | bytes 442376 | tf_op jit(solution)/shard_map/ppermute | solution.py:536
  13.2 1.6 %collective-permute-done.2 = bf16[576,128]{1,0:T(8,128)(2,1)S(1)} collective-permute-done((bf16[576,128]{1,0:T(8,128)(2,1)}, bf16[576,128]{1,0:T(8,128)(2,1)S(1)}, u32[]{:S(2)}, u32[]{:S(2)}) %collective-permute-start.2) | collective-permute-done | bytes 147488 | tf_op jit(solution)/shard_map/ppermute | solution.py:536
  15.1 2.8 %collective-permute-done.1 = bf16[576,128]{1,0:T(8,128)(2,1)S(1)} collective-permute-done((bf16[576,128]{1,0:T(8,128)(2,1)}, bf16[576,128]{1,0:T(8,128)(2,1)S(1)}, u32[]{:S(2)}, u32[]{:S(2)}) %collective-permute-start.1) | collective-permute-done | bytes 147488 | tf_op jit(solution)/shard_map/ppermute | solution.py:536
  18.5 3.8 %collective-permute-done = bf16[576,128]{1,0:T(8,128)(2,1)S(1)} collective-permute-done((bf16[576,128]{1,0:T(8,128)(2,1)}, bf16[576,128]{1,0:T(8,128)(2,1)S(1)}, u32[]{:S(2)}, u32[]{:S(2)}) %collective-permute-start) | collective-permute-done | bytes 147488 | tf_op jit(solution)/shard_map/ppermute | solution.py:536
  24.1 3.3 %collective-permute-done.4 = bf16[576,128]{1,0:T(8,128)(2,1)S(1)} collective-permute-done((bf16[576,128]{1,0:T(8,128)(2,1)S(1)}, bf16[576,128]{1,0:T(8,128)(2,1)S(1)}, u32[]{:S(2)}, u32[]{:S(2)}) %collective-permute-start.4) | collective-permute-done | bytes 147488 | tf_op jit(solution)/shard_map/ppermute | solution.py:536
  27.6 1.4 %constant_dynamic-slice_fusion = (bf16[128,4096]{1,0:T(8,128)(2,1)S(1)}, bf16[128,4096]{1,0:T(8,128)(2,1)S(1)}) fusion(bf16[256,4096]{1,0:T(8,128)(2,1)} %param.10, s32[]{:T(128)S(6)} %select_n.4, bf16[256,4096]{1,0:T(8,128)(2,1)S(1)} %copy-done.1), kind=kLoop, calls=%fused_computation.18 | loop fusion | bytes 4194308 | tf_op jit(solution)/shard_map/dynamic_slice | solution.py:592
  29.0 1.8 %shard_map.137.inner_own = f32[2,512,128]{2,1,0:T(8,128)S(1)} custom-call(s32[2]{0:T(128)S(1)} %pad_add_fusion.where, bf16[4,576,128]{2,1,0:T(8,128)(2,1)S(1)} %pad_maximum_fusion.along.own_a, bf16[4,576,128]{2,1,0:T(8,128)(2,1)S(1)} %pad_maximum_fusion.1.across.own_b, bf16[128,4096]{1,0:T(8,128)(2,1)S(1)} %get-tuple-element.53.x), custom_call_target="tpu_custom_call" | custom-call | flops 1000000000 | bytes 10000000 | tf_op jit(solution)/shard_map/pallas_call | solution.py:455
  30.9 1.8 %shard_map.138.inner_oth = f32[2,512,128]{2,1,0:T(8,128)S(1)} custom-call(s32[2]{0:T(128)S(1)} %pad_add_fusion.where, bf16[4,576,128]{2,1,0:T(8,128)(2,1)S(1)} %collective-permute-done.7.along.oth_a, bf16[4,576,128]{2,1,0:T(8,128)(2,1)S(1)} %collective-permute-done.8.across.oth_b, bf16[256,4096]{1,0:T(8,128)(2,1)S(1)} %collective-permute-done.9.x.x_got), custom_call_target="tpu_custom_call" | custom-call | flops 1000000000 | bytes 10000000 | tf_op jit(solution)/shard_map/pallas_call | solution.py:455
  32.7 18.7 %shard_map.139 = (bf16[8,192,128]{2,1,0:T(8,128)(2,1)S(1)}, bf16[8,192,128]{2,1,0:T(8,128)(2,1)S(1)}, f32[2048,128]{1,0:T(8,128)S(1)}, f32[1024,128]{1,0:T(8,128...) custom-call(s32[2]{0:T(128)S(1)} %pad_add_fusion.where, ...), custom_call_target="tpu_custom_call" | custom-call | flops 5000000000 | bytes 40000000 | tf_op jit(solution)/shard_map/pallas_call | solution.py:471
  52.0 1.3 %collective-permute-done.11 = bf16[8,192,128]{2,1,0:T(8,128)(2,1)S(1)} collective-permute-done((bf16[8,192,128]{2,1,0:T(8,128)(2,1)S(1)}, bf16[8,192,128]{2,1,0:T(8,128)(2,1)S(1)}, u32[]{:S(2)}, u32[]{:S(2)}) %collective-permute-start.11) | collective-permute-done | bytes 393248 | tf_op jit(solution)/shard_map/ppermute | solution.py:536
  54.0 4.8 %shard_map.140 = (bf16[8,256,128]{2,1,0:T(8,128)(2,1)S(1)}, f32[2048,128]{1,0:T(8,128)S(1)}) custom-call(s32[2]{0:T(128)S(1)} %pad_add_fusion.where, s32[64]{0:T(128)S(1)} %copy-done, f32[2048,128]{1,0:T(8,128)S(1)} %get-tuple-element.26.inner, f32[1024,128]{1,0:T(8,128)S(1)} %get-tuple-element.27.ret, bf16[2,8,256,128]{3,2,1,0:T(8,128)(2,1)S(1)} %get-tuple-element.28.t_r, ...), custom_call_target="tpu_custom_call" | custom-call | flops 5000000000 | bytes 20000000 | tf_op jit(solution)/shard_map/pallas_call | solution.py:506
  59.0 1.7 %collective-permute-done.12 = bf16[4,192,128]{2,1,0:T(8,128)(2,1)S(1)} collective-permute-done((bf16[4,192,128]{2,1,0:T(8,128)(2,1)S(1)}, bf16[4,192,128]{2,1,0:T(8,128)(2,1)S(1)}, u32[]{:S(2)}, u32[]{:S(2)}) %collective-permute-start.12) | collective-permute-done | bytes 196640 | tf_op jit(solution)/shard_map/ppermute | solution.py:536
  61.8 4.8 %shard_map.141 = (bf16[8,256,128]{2,1,0:T(8,128)(2,1)S(1)}, f32[2048,128]{1,0:T(8,128)S(1)}) custom-call(s32[2]{0:T(128)S(1)} %pad_add_fusion.where, s32[64]{0:T(128)S(1)} %copy-done, f32[2048,128]{1,0:T(8,128)S(1)} %get-tuple-element.26.inner, f32[1024,128]{1,0:T(8,128)S(1)} %get-tuple-element.27.ret, bf16[2,8,256,128]{3,2,1,0:T(8,128)(2,1)S(1)} %get-tuple-element.28.t_r, ...), custom_call_target="tpu_custom_call" | custom-call | flops 5000000000 | bytes 20000000 | tf_op jit(solution)/shard_map/pallas_call | solution.py:506
  67.3 3.0 %shard_map.142 = (bf16[8,128,128]{2,1,0:T(8,128)(2,1)S(1)}, bf16[8,128,128]{2,1,0:T(8,128)(2,1)S(1)}) custom-call(s32[2]{0:T(128)S(1)} %pad_add_fusion.where, f32[2048,128]{1,0:T(8,128)S(1)} %get-tuple-element.41.back, bf16[128,4096]{1,0:T(8,128)(2,1)S(1)} %get-tuple-element.53.x, bf16[256,4096]{1,0:T(8,128)(2,1)S(1)} %collective-permute-done.9.x.x_got), custom_call_target="tpu_custom_call" | custom-call | flops 1000000000 | bytes 10000000 | tf_op jit(solution)/shard_map/pallas_call | solution.py:522
  70.4 2.2 %collective-permute-start.16 = (bf16[192,128]{1,0:T(8,128)(2,1)S(1)}, bf16[192,128]{1,0:T(8,128)(2,1)S(1)}, u32[]{:S(2)}, u32[]{:S(2)}) collective-permute-start(bf16[192,128]{1,0:T(8,128)(2,1)S(1)} %get-tuple-element.49), channel_id=1, source_target_pairs={{0,8},{2,10},{4,12},{6,14},{8,0},{10,2},{12,4},{14,6},{1,9},{3,11}... | collective-permute-start | bytes 147464 | tf_op jit(solution)/shard_map/ppermute | solution.py:536
  72.5 1.8 %collective-permute-done.17 = bf16[4,256,128]{2,1,0:T(8,128)(2,1)S(1)} collective-permute-done((bf16[4,256,128]{2,1,0:T(8,128)(2,1)S(1)}, bf16[4,256,128]{2,1,0:T(8,128)(2,1)S(1)}, u32[]{:S(2)}, u32[]{:S(2)}) %collective-permute-start.17) | collective-permute-done | bytes 262176 | tf_op jit(solution)/shard_map/ppermute | solution.py:536
  76.7 1.6 %collective-permute-start.18 = (bf16[4,128,128]{2,1,0:T(8,128)(2,1)S(1)}, bf16[4,128,128]{2,1,0:T(8,128)(2,1)S(1)}, u32[]{:S(2)}, u32[]{:S(2)}) collective-permute-start(bf16[4,128,128]{2,1,0:T(8,128)(2,1)S(1)} %add_convert_fusion.6), channel_id=1, source_target_pairs={{0,2},{2,0},{4,6},{6,4},{8,10},{10,8},{12,14},{14,12},{1,3},{3,1},... | collective-permute-start | bytes 393224 | tf_op jit(solution)/shard_map/ppermute | solution.py:536
  79.5 2.2 %collective-permute-done.18 = bf16[4,128,128]{2,1,0:T(8,128)(2,1)S(1)} collective-permute-done((bf16[4,128,128]{2,1,0:T(8,128)(2,1)S(1)}, bf16[4,128,128]{2,1,0:T(8,128)(2,1)S(1)}, u32[]{:S(2)}, u32[]{:S(2)}) %collective-permute-start.18) | collective-permute-done | bytes 131104 | tf_op jit(solution)/shard_map/ppermute | solution.py:536
  81.9 2.0 %collective-permute-start.22 = (bf16[256,128]{1,0:T(8,128)(2,1)S(1)}, bf16[256,128]{1,0:T(8,128)(2,1)S(1)}, u32[]{:S(2)}, u32[]{:S(2)}) collective-permute-start(bf16[256,128]{1,0:T(8,128)(2,1)S(1)} %get-tuple-element.46), channel_id=1, source_target_pairs={{0,8},{2,10},{4,12},{6,14},{8,0},{10,2},{12,4},{14,6},{1,9},{3,11}... | collective-permute-start | bytes 196616 | tf_op jit(solution)/shard_map/ppermute | solution.py:536
  84.0 2.2 %collective-permute-done.19 = bf16[2,128,128]{2,1,0:T(8,128)(2,1)S(1)} collective-permute-done((bf16[2,128,128]{2,1,0:T(8,128)(2,1)S(1)}, bf16[2,128,128]{2,1,0:T(8,128)(2,1)S(1)}, u32[]{:S(2)}, u32[]{:S(2)}) %collective-permute-start.19) | collective-permute-done | bytes 65568 | tf_op jit(solution)/shard_map/ppermute | solution.py:536
  87.9 3.2 %collective-permute-done.20.refs_1_ = bf16[128,128]{1,0:T(8,128)(2,1)S(1)} collective-permute-done((bf16[128,128]{1,0:T(8,128)(2,1)S(1)}, bf16[128,128]{1,0:T(8,128)(2,1)S(1)}, u32[]{:S(2)}, u32[]{:S(2)}) %collective-permute-start.20) | collective-permute-done | bytes 32800 | tf_op jit(solution)/shard_map/ppermute | solution.py:536
  (53 shorter events, 14.0 us)
Async XLA Ops:
  0.6 30.3 %collective-permute-start.9 = (bf16[256,4096]{1,0:T(8,128)(2,1)}, bf16[256,4096]{1,0:T(8,128)(2,1)S(1)}, u32[]{:S(2)}, u32[]{:S(2)}) collective-permute-start(bf16[256,4096]{1,0:T(8,128)(2,1)} %param.9), channel_id=1, source_target_pairs={{0,1},{1,0},{2,3},{3,2},{4,5},{5,4},{6,7},{7,6},{8,9},{9,8},{10,11... | collective-permute-start | bytes 6291464 | tf_op jit(solution)/shard_map/ppermute | solution.py:536
  1.2 31.6 %collective-permute-start.10 = (bf16[256,4096]{1,0:T(8,128)(2,1)}, bf16[256,4096]{1,0:T(8,128)(2,1)}, u32[]{:S(2)}, u32[]{:S(2)}) collective-permute-start(bf16[256,4096]{1,0:T(8,128)(2,1)} %param.10), channel_id=1, source_target_pairs={{0,1},{1,0},{2,3},{3,2},{4,5},{5,4},{6,7},{7,6},{8,9},{9,8},{10,11... | collective-permute-start | bytes 6291464 | tf_op jit(solution)/shard_map/ppermute | solution.py:536
  3.0 7.3 %collective-permute-start.3 = (bf16[576,128]{1,0:T(8,128)(2,1)}, bf16[576,128]{1,0:T(8,128)(2,1)S(1)}, u32[]{:S(2)}, u32[]{:S(2)}) collective-permute-start(bf16[576,128]{1,0:T(8,128)(2,1)} %shard_map.136), channel_id=1, source_target_pairs={{0,2},{2,0},{4,6},{6,4},{8,10},{10,8},{12,14},{14,12},{1,3},{3,1},... | collective-permute-start | bytes 442376 | tf_op jit(solution)/shard_map/ppermute | solution.py:536
  6.0 8.7 %collective-permute-start.2 = (bf16[576,128]{1,0:T(8,128)(2,1)}, bf16[576,128]{1,0:T(8,128)(2,1)S(1)}, u32[]{:S(2)}, u32[]{:S(2)}) collective-permute-start(bf16[576,128]{1,0:T(8,128)(2,1)} %shard_map.136), channel_id=1, source_target_pairs={{0,12},{2,14},{4,8},{6,10},{8,4},{10,6},{12,0},{14,2},{1,13},{3,15... | collective-permute-start | bytes 442376 | tf_op jit(solution)/shard_map/ppermute | solution.py:536
  9.6 8.3 %collective-permute-start.1 = (bf16[576,128]{1,0:T(8,128)(2,1)}, bf16[576,128]{1,0:T(8,128)(2,1)S(1)}, u32[]{:S(2)}, u32[]{:S(2)}) collective-permute-start(bf16[576,128]{1,0:T(8,128)(2,1)} %shard_map.136), channel_id=1, source_target_pairs={{0,4},{2,6},{4,0},{6,2},{8,12},{10,14},{12,8},{14,10},{1,5},{3,7},... | collective-permute-start | bytes 442376 | tf_op jit(solution)/shard_map/ppermute | solution.py:536
  10.3 12.0 %collective-permute-start = (bf16[576,128]{1,0:T(8,128)(2,1)}, bf16[576,128]{1,0:T(8,128)(2,1)S(1)}, u32[]{:S(2)}, u32[]{:S(2)}) collective-permute-start(bf16[576,128]{1,0:T(8,128)(2,1)} %shard_map.136), channel_id=1, source_target_pairs={{0,8},{2,10},{4,12},{6,14},{8,0},{10,2},{12,4},{14,6},{1,9},{3,11}... | collective-permute-start | bytes 442376 | tf_op jit(solution)/shard_map/ppermute | solution.py:536
  14.8 9.3 %collective-permute-start.6 = (bf16[576,128]{1,0:T(8,128)(2,1)S(1)}, bf16[576,128]{1,0:T(8,128)(2,1)S(1)}, u32[]{:S(2)}, u32[]{:S(2)}) collective-permute-start(bf16[576,128]{1,0:T(8,128)(2,1)S(1)} %collective-permute-done.2), channel_id=1, source_target_pairs={{0,2},{2,0},{4,6},{6,4},{8,10},{10,8},{12,14},{14,12},{1,3},{3,1},... | collective-permute-start | bytes 442376 | tf_op jit(solution)/shard_map/ppermute | solution.py:536
  17.9 6.2 %collective-permute-start.5 = (bf16[576,128]{1,0:T(8,128)(2,1)S(1)}, bf16[576,128]{1,0:T(8,128)(2,1)S(1)}, u32[]{:S(2)}, u32[]{:S(2)}) collective-permute-start(bf16[576,128]{1,0:T(8,128)(2,1)S(1)} %collective-permute-done.1), channel_id=1, source_target_pairs={{0,2},{2,0},{4,6},{6,4},{8,10},{10,8},{12,14},{14,12},{1,3},{3,1},... | collective-permute-start | bytes 442376 | tf_op jit(solution)/shard_map/ppermute | solution.py:536
  22.3 5.1 %collective-permute-start.4 = (bf16[576,128]{1,0:T(8,128)(2,1)S(1)}, bf16[576,128]{1,0:T(8,128)(2,1)S(1)}, u32[]{:S(2)}, u32[]{:S(2)}) collective-permute-start(bf16[576,128]{1,0:T(8,128)(2,1)S(1)} %collective-permute-done), channel_id=1, source_target_pairs={{0,2},{2,0},{4,6},{6,4},{8,10},{10,8},{12,14},{14,12},{1,3},{3,1},... | collective-permute-start | bytes 442376 | tf_op jit(solution)/shard_map/ppermute | solution.py:536
  22.9 4.7 %copy-start.1 = (bf16[256,4096]{1,0:T(8,128)(2,1)S(1)}, bf16[256,4096]{1,0:T(8,128)(2,1)}, u32[]{:S(2)}) copy-start(bf16[256,4096]{1,0:T(8,128)(2,1)} %param.9) | copy-start | bytes 6291460
  24.0 6.8 %collective-permute-start.7 = (bf16[4,576,128]{2,1,0:T(8,128)(2,1)S(1)}, bf16[4,576,128]{2,1,0:T(8,128)(2,1)S(1)}, u32[]{:S(2)}, u32[]{:S(2)}) collective-permute-start(bf16[4,576,128]{2,1,0:T(8,128)(2,1)S(1)} %pad_maximum_fusion.along.own_a), channel_id=1, source_target_pairs={{0,1},{1,0},{2,3},{3,2},{4,5},{5,4},{6,7},{7,6},{8,9},{9,8},{10,11... | collective-permute-start | bytes 1769480 | tf_op jit(solution)/shard_map/ppermute | solution.py:536
  27.5 3.4 %collective-permute-start.8 = (bf16[4,576,128]{2,1,0:T(8,128)(2,1)S(1)}, bf16[4,576,128]{2,1,0:T(8,128)(2,1)S(1)}, u32[]{:S(2)}, u32[]{:S(2)}) collective-permute-start(bf16[4,576,128]{2,1,0:T(8,128)(2,1)S(1)} %pad_maximum_fusion.1.across.own_b), channel_id=1, source_target_pairs={{0,1},{1,0},{2,3},{3,2},{4,5},{5,4},{6,7},{7,6},{8,9},{9,8},{10,11... | collective-permute-start | bytes 1769480 | tf_op jit(solution)/shard_map/ppermute | solution.py:536
  51.5 1.9 %collective-permute-start.11 = (bf16[8,192,128]{2,1,0:T(8,128)(2,1)S(1)}, bf16[8,192,128]{2,1,0:T(8,128)(2,1)S(1)}, u32[]{:S(2)}, u32[]{:S(2)}) collective-permute-start(bf16[8,192,128]{2,1,0:T(8,128)(2,1)S(1)} %get-tuple-element.36), channel_id=1, source_target_pairs={{0,1},{1,0},{2,3},{3,2},{4,5},{5,4},{6,7},{7,6},{8,9},{9,8},{10,11... | collective-permute-start | bytes 1179656 | tf_op jit(solution)/shard_map/ppermute | solution.py:536
  53.4 7.2 %collective-permute-start.12 = (bf16[4,192,128]{2,1,0:T(8,128)(2,1)S(1)}, bf16[4,192,128]{2,1,0:T(8,128)(2,1)S(1)}, u32[]{:S(2)}, u32[]{:S(2)}) collective-permute-start(bf16[4,192,128]{2,1,0:T(8,128)(2,1)S(1)} %add_convert_fusion.3), channel_id=1, source_target_pairs={{0,2},{2,0},{4,6},{6,4},{8,10},{10,8},{12,14},{14,12},{1,3},{3,1},... | collective-permute-start | bytes 589832 | tf_op jit(solution)/shard_map/ppermute | solution.py:536
  58.8 7.9 %collective-permute-start.14 = (bf16[8,256,128]{2,1,0:T(8,128)(2,1)S(1)}, bf16[8,256,128]{2,1,0:T(8,128)(2,1)S(1)}, u32[]{:S(2)}, u32[]{:S(2)}) collective-permute-start(bf16[8,256,128]{2,1,0:T(8,128)(2,1)S(1)} %get-tuple-element.40), channel_id=1, source_target_pairs={{0,1},{1,0},{2,3},{3,2},{4,5},{5,4},{6,7},{7,6},{8,9},{9,8},{10,11... | collective-permute-start | bytes 1572872 | tf_op jit(solution)/shard_map/ppermute | solution.py:536
  60.8 6.5 %collective-permute-start.13 = (bf16[2,192,128]{2,1,0:T(8,128)(2,1)S(1)}, bf16[2,192,128]{2,1,0:T(8,128)(2,1)S(1)}, u32[]{:S(2)}, u32[]{:S(2)}) collective-permute-start(bf16[2,192,128]{2,1,0:T(8,128)(2,1)S(1)} %slice.99), channel_id=1, source_target_pairs={{0,4},{2,6},{4,0},{6,2},{8,12},{10,14},{12,8},{14,10},{1,5},{3,7},... | collective-permute-start | bytes 294920 | tf_op jit(solution)/shard_map/ppermute | solution.py:536
  66.8 7.6 %collective-permute-start.17 = (bf16[4,256,128]{2,1,0:T(8,128)(2,1)S(1)}, bf16[4,256,128]{2,1,0:T(8,128)(2,1)S(1)}, u32[]{:S(2)}, u32[]{:S(2)}) collective-permute-start(bf16[4,256,128]{2,1,0:T(8,128)(2,1)S(1)} %add_convert_fusion.1), channel_id=1, source_target_pairs={{0,2},{2,0},{4,6},{6,4},{8,10},{10,8},{12,14},{14,12},{1,3},{3,1},... | collective-permute-start | bytes 786440 | tf_op jit(solution)/shard_map/ppermute | solution.py:536
  70.3 6.4 %collective-permute-start.15 = (bf16[8,128,128]{2,1,0:T(8,128)(2,1)S(1)}, bf16[8,128,128]{2,1,0:T(8,128)(2,1)S(1)}, u32[]{:S(2)}, u32[]{:S(2)}) collective-permute-start(bf16[8,128,128]{2,1,0:T(8,128)(2,1)S(1)} %get-tuple-element.43), channel_id=1, source_target_pairs={{0,1},{1,0},{2,3},{3,2},{4,5},{5,4},{6,7},{7,6},{8,9},{9,8},{10,11... | collective-permute-start | bytes 786440 | tf_op jit(solution)/shard_map/ppermute | solution.py:536
  70.4 6.3 %collective-permute-start.16 = (bf16[192,128]{1,0:T(8,128)(2,1)S(1)}, bf16[192,128]{1,0:T(8,128)(2,1)S(1)}, u32[]{:S(2)}, u32[]{:S(2)}) collective-permute-start(bf16[192,128]{1,0:T(8,128)(2,1)S(1)} %get-tuple-element.49), channel_id=1, source_target_pairs={{0,8},{2,10},{4,12},{6,14},{8,0},{10,2},{12,4},{14,6},{1,9},{3,11}... | collective-permute-start | bytes 147464 | tf_op jit(solution)/shard_map/ppermute | solution.py:536
  74.5 5.0 %collective-permute-start.21 = (bf16[2,256,128]{2,1,0:T(8,128)(2,1)S(1)}, bf16[2,256,128]{2,1,0:T(8,128)(2,1)S(1)}, u32[]{:S(2)}, u32[]{:S(2)}) collective-permute-start(bf16[2,256,128]{2,1,0:T(8,128)(2,1)S(1)} %slice.108), channel_id=1, source_target_pairs={{0,4},{2,6},{4,0},{6,2},{8,12},{10,14},{12,8},{14,10},{1,5},{3,7},... | collective-permute-start | bytes 393224 | tf_op jit(solution)/shard_map/ppermute | solution.py:536
  76.7 5.1 %collective-permute-start.18 = (bf16[4,128,128]{2,1,0:T(8,128)(2,1)S(1)}, bf16[4,128,128]{2,1,0:T(8,128)(2,1)S(1)}, u32[]{:S(2)}, u32[]{:S(2)}) collective-permute-start(bf16[4,128,128]{2,1,0:T(8,128)(2,1)S(1)} %add_convert_fusion.6), channel_id=1, source_target_pairs={{0,2},{2,0},{4,6},{6,4},{8,10},{10,8},{12,14},{14,12},{1,3},{3,1},... | collective-permute-start | bytes 393224 | tf_op jit(solution)/shard_map/ppermute | solution.py:536
  81.8 4.3 %collective-permute-start.19 = (bf16[2,128,128]{2,1,0:T(8,128)(2,1)S(1)}, bf16[2,128,128]{2,1,0:T(8,128)(2,1)S(1)}, u32[]{:S(2)}, u32[]{:S(2)}) collective-permute-start(bf16[2,128,128]{2,1,0:T(8,128)(2,1)S(1)} %slice.103), channel_id=1, source_target_pairs={{0,4},{2,6},{4,0},{6,2},{8,12},{10,14},{12,8},{14,10},{1,5},{3,7},... | collective-permute-start | bytes 196616 | tf_op jit(solution)/shard_map/ppermute | solution.py:536
  81.9 5.9 %collective-permute-start.22 = (bf16[256,128]{1,0:T(8,128)(2,1)S(1)}, bf16[256,128]{1,0:T(8,128)(2,1)S(1)}, u32[]{:S(2)}, u32[]{:S(2)}) collective-permute-start(bf16[256,128]{1,0:T(8,128)(2,1)S(1)} %get-tuple-element.46), channel_id=1, source_target_pairs={{0,8},{2,10},{4,12},{6,14},{8,0},{10,2},{12,4},{14,6},{1,9},{3,11}... | collective-permute-start | bytes 196616 | tf_op jit(solution)/shard_map/ppermute | solution.py:536
  86.2 4.9 %collective-permute-start.20 = (bf16[128,128]{1,0:T(8,128)(2,1)S(1)}, bf16[128,128]{1,0:T(8,128)(2,1)S(1)}, u32[]{:S(2)}, u32[]{:S(2)}) collective-permute-start(bf16[128,128]{1,0:T(8,128)(2,1)S(1)} %get-tuple-element.50), channel_id=1, source_target_pairs={{0,8},{2,10},{4,12},{6,14},{8,0},{10,2},{12,4},{14,6},{1,9},{3,11}... | collective-permute-start | bytes 98312 | tf_op jit(solution)/shard_map/ppermute | solution.py:536
  (1 other events, 1.9 us)

commit v5 on v4

--- a/solution.py
+++ b/solution.py
@@ -243,13 +243,12 @@
             for h in range(2):
                 flat = stacked(s_r[h], gu * NB, 128, g)
                 n_r[gu, g, :, pl.ds(h * 128, 128)] = flat.astype(bf16)
-                t_r[gu, g, pl.ds(h * 128, 128), :] = flat.T.astype(bf16)
+                t_r[gu, g, pl.ds(h * 128, 128), :] = flat.astype(bf16).T
         for h in range(2):
-            part = t_ld[g, pl.ds(h * 128, 128), :].astype(f32).T
-            n_ld[g, :, pl.ds(h * 128, 128)] = part.astype(bf16)
+            n_ld[g, :, pl.ds(h * 128, 128)] = t_ld[g, pl.ds(h * 128, 128), :].T
         flat = stacked(s_rd, 0, NB, g)
         n_rd[g] = flat.astype(bf16)
-        t_rd[g] = flat.T.astype(bf16)
+        t_rd[g] = flat.astype(bf16).T
         return 0
 
     lax.fori_loop(0, GROUPS, turn, 0)
@@ -546,7 +545,7 @@
     pair = (x0, x1)
     along = jnp.stack([mine, z2, z1, z3])
     across = jnp.stack([pair[0], x2, pair[1], x3])
-    return (z1, z3), along, across, sibling(along), sibling(across)
+    return along, across, sibling(along), sibling(across)
 
 
 def add(a, b):
@@ -579,17 +578,15 @@
     direct = n == CHUNKS
     if direct:
         where = jnp.stack([me, side]).astype(jnp.int32)
-        ready, *pieces = gathered(prepare_call(factors), n)
-        start = side * toks
+        pieces = gathered(prepare_call(factors), n)
     else:
-        start = side * toks
         where = jnp.stack([jnp.zeros_like(side), side]).astype(jnp.int32)
         whole = [lax.all_gather(v, "dp", axis=1, tiled=True) for v in factors]
         cut = [jnp.moveaxis(v.reshape(HALF, CHUNKS, -1), 1, 0) for v in whole]
         packed = jnp.concatenate(jax.vmap(pack)(*cut), axis=1)
         packed = packed.reshape((4, 2) + packed.shape[1:])[jnp.array(STEPS)]
         pieces = (packed[:, 0], packed[:, 1], sibling(packed[:, 0]), sibling(packed[:, 1]))
-    x, y = [lax.dynamic_slice_in_dim(v, start, toks, 0) for v in (activations, teacher_out)]
+    x, y = [lax.dynamic_slice_in_dim(v, side * toks, toks, 0) for v in (activations, teacher_out)]
     x_got, y_got = sibling(activations), sibling(teacher_out)
     inner = (
         inner_call(where, pieces[0], pieces[1], x, toks),
@@ -601,25 +598,23 @@
     right_send, back = right_call(1, where, block_order, *shared, act_oth, slope_oth)
     right_got = sibling(right_send)
     if direct:
-        _, crossed = over_x(keep, got, n)
-        line = line_of(keep, got, crossed)
-        back = tie(back, line)
+        away, crossed = over_x(keep, tie(got, back), n)
+        back = tie(back, away)
     right_keep, back = right_call(0, where, block_order, *shared, act_own, slope_own, back)
     if direct:
-        half = over_z(line, n)
         right_away, right_crossed = over_x(right_keep, right_got, n)
-        back = tie(back, half, right_away)
+        back = tie(back, right_away)
     left_keep, left_send = left_call(where, back, x, x_got)
     left_got = sibling(left_send)
     if direct:
+        half = over_z(line_of(keep, got, crossed), n)
+        left_away = add(left_keep[4:], left_got[4:])
+        left_crossed = swap(left_away, "dp", 1, n)
+        right_half = over_z(tie(line_of(right_keep, right_got, right_crossed), left_away), n)
         down = [half[0], swap(half[1], "dp", 4, n)]
-        left_got = tie(left_got, down[1])
-        right_half = over_z(line_of(right_keep, right_got, right_crossed), n)
-        left_away = tie(add(left_keep[4:], left_got[4:]), right_crossed)
-        left_crossed = swap(left_away, "dp", 1, n)
         left_half = over_z(line_of(left_keep, left_got, left_crossed), n)
-        right = [right_half[0], swap(right_half[1], "dp", 4, n)]
-        left = [left_half[0], swap(left_half[1], "dp", 4, n)]
+        right = [right_half[0], swap(tie(right_half[1], half), "dp", 4, n)]
+        left = [left_half[0], swap(tie(left_half[1], right_half), "dp", 4, n)]
         return finish_call(left, right, down)
     rest = (jnp.concatenate([right_keep, keep], axis=1), jnp.concatenate([right_got, got], axis=1))
     sums = []

time: 92.4 us -> 88.3 us (0.956)
  waiting for transfers between devices: 27.4 us -> 23 us
    ppermute x23, waiting for transfers between devices: 27.4 us -> 23 us  [swap(): return lax.ppermute(v, axis, [(i, i ^ bit) for i in range(size)])]
  transfers between devices with their start and end apart: 23 -> 23, of which waited for: 14 -> 12; matrix products, arithmetic and copies ran while one was open for 3% -> 4% of each run, Pallas kernels for 20% -> 20%
where the time goes in v5:
time: 88.3 us; the launch traced here: 88 us
  Pallas kernels  37.5 us (42%)
  starting transfers between devices  23.2 us (26%)
  waiting for transfers between devices  23 us (26%)
  other arithmetic  1.78 us (2%)
  local copies, waits for them, and re-layouts  1.5 us (2%)
  between operations  0.91 us (1%)
    ppermute x23, starting transfers between devices, swap(): return lax.ppermute(v, axis, [(i, i ^ bit) for i in range(size)])  23.2 us
    ppermute x23, waiting for transfers between devices, swap(): return lax.ppermute(v, axis, [(i, i ^ bit) for i in range(size)])  23 us
    pallas_call x1, Pallas kernels, middle_call(): pl.pallas_call(functools.partial(middle_body, scale), out_shape=(down, do...  18.5 us
    pallas_call x2, Pallas kernels, right_call(): pl.pallas_call(functools.partial(right_body, b), out_shape=(jax.ShapeDtyp...  9.59 us
    pallas_call x2, Pallas kernels, inner_call(): pl.pallas_call(inner_body, grid=(1,), out_shape=jax.ShapeDtypeStruct((2,...  3.64 us
    pallas_call x1, Pallas kernels, left_call(): pl.pallas_call(left_body, out_shape=(grads, grads), in_specs=[SMEM] + [VM...  2.95 us
    pallas_call x1, Pallas kernels, prepare_call(): pl.pallas_call(prepare_body, out_shape=jax.ShapeDtypeStruct((FIRST + REST...  1.79 us
  transfers between devices with their start and end apart: 23, of which 12 were waited for; matrix products, arithmetic and copies ran while one was open for 4% of the time, Pallas kernels for 20%

profile of v5, /device:TPU:0, one launch (start us, length us, event | category | flops | bytes accessed | tf_op | source)
XLA Modules:
  0.0 88.0 jit_solution(14690964120725044745)
XLA Ops:
  1.2 1.8 %shard_map.136 = bf16[576,128]{1,0:T(8,128)(2,1)} custom-call(bf16[32,256]{1,0:T(8,128)(2,1)} %refs_0_.1, bf16[32,448]{1,0:T(8,128)(2,1)} %refs_1_.1, bf16[32,256]{1,0:T(8,128)(2,1)} %refs_2_.1, bf16[32,448]{1,0:T(8,128)(2,1)} %refs_3_.1, bf16[32,448]{1,0:T(8,128)(2,1)} %refs_4_.1, bf16[32,256]{1,0:T(8,128)(2,1)} %refs_5_.1), custom_call_target="tpu_custom_call" | custom-call | tf_op jit(solution)/shard_map/pallas_call | solution.py:429
  3.0 3.0 %collective-permute-start.3 = (bf16[576,128]{1,0:T(8,128)(2,1)}, bf16[576,128]{1,0:T(8,128)(2,1)S(1)}, u32[]{:S(2)}, u32[]{:S(2)}) collective-permute-start(bf16[576,128]{1,0:T(8,128)(2,1)} %shard_map.136), channel_id=1, source_target_pairs={{0,2},{2,0},{4,6},{6,4},{8,10},{10,8},{12,14},{14,12},{1,3},{3,1},... | collective-permute-start | bytes 442376 | tf_op jit(solution)/shard_map/ppermute | solution.py:535
  6.0 3.6 %collective-permute-start.2 = (bf16[576,128]{1,0:T(8,128)(2,1)}, bf16[576,128]{1,0:T(8,128)(2,1)S(1)}, u32[]{:S(2)}, u32[]{:S(2)}) collective-permute-start(bf16[576,128]{1,0:T(8,128)(2,1)} %shard_map.136), channel_id=1, source_target_pairs={{0,12},{2,14},{4,8},{6,10},{8,4},{10,6},{12,0},{14,2},{1,13},{3,15... | collective-permute-start | bytes 442376 | tf_op jit(solution)/shard_map/ppermute | solution.py:535
  10.3 2.8 %collective-permute-start = (bf16[576,128]{1,0:T(8,128)(2,1)}, bf16[576,128]{1,0:T(8,128)(2,1)S(1)}, u32[]{:S(2)}, u32[]{:S(2)}) collective-permute-start(bf16[576,128]{1,0:T(8,128)(2,1)} %shard_map.136), channel_id=1, source_target_pairs={{0,8},{2,10},{4,12},{6,14},{8,0},{10,2},{12,4},{14,6},{1,9},{3,11}... | collective-permute-start | bytes 442376 | tf_op jit(solution)/shard_map/ppermute | solution.py:535
  13.2 1.6 %collective-permute-done.2 = bf16[576,128]{1,0:T(8,128)(2,1)S(1)} collective-permute-done((bf16[576,128]{1,0:T(8,128)(2,1)}, bf16[576,128]{1,0:T(8,128)(2,1)S(1)}, u32[]{:S(2)}, u32[]{:S(2)}) %collective-permute-start.2) | collective-permute-done | bytes 147488 | tf_op jit(solution)/shard_map/ppermute | solution.py:535
  15.1 2.8 %collective-permute-done.1 = bf16[576,128]{1,0:T(8,128)(2,1)S(1)} collective-permute-done((bf16[576,128]{1,0:T(8,128)(2,1)}, bf16[576,128]{1,0:T(8,128)(2,1)S(1)}, u32[]{:S(2)}, u32[]{:S(2)}) %collective-permute-start.1) | collective-permute-done | bytes 147488 | tf_op jit(solution)/shard_map/ppermute | solution.py:535
  18.5 3.8 %collective-permute-done = bf16[576,128]{1,0:T(8,128)(2,1)S(1)} collective-permute-done((bf16[576,128]{1,0:T(8,128)(2,1)}, bf16[576,128]{1,0:T(8,128)(2,1)S(1)}, u32[]{:S(2)}, u32[]{:S(2)}) %collective-permute-start) | collective-permute-done | bytes 147488 | tf_op jit(solution)/shard_map/ppermute | solution.py:535
  24.1 3.3 %collective-permute-done.4 = bf16[576,128]{1,0:T(8,128)(2,1)S(1)} collective-permute-done((bf16[576,128]{1,0:T(8,128)(2,1)S(1)}, bf16[576,128]{1,0:T(8,128)(2,1)S(1)}, u32[]{:S(2)}, u32[]{:S(2)}) %collective-permute-start.4) | collective-permute-done | bytes 147488 | tf_op jit(solution)/shard_map/ppermute | solution.py:535
  27.6 1.4 %constant_dynamic-slice_fusion = (bf16[128,4096]{1,0:T(8,128)(2,1)S(1)}, bf16[128,4096]{1,0:T(8,128)(2,1)S(1)}) fusion(bf16[256,4096]{1,0:T(8,128)(2,1)} %param.10, s32[]{:T(128)S(6)} %select_n.4, bf16[256,4096]{1,0:T(8,128)(2,1)S(1)} %copy-done.1), kind=kLoop, calls=%fused_computation.18 | loop fusion | bytes 4194308 | tf_op jit(solution)/shard_map/dynamic_slice | solution.py:589
  29.0 1.8 %shard_map.137.inner_own = f32[2,512,128]{2,1,0:T(8,128)S(1)} custom-call(s32[2]{0:T(128)S(1)} %pad_add_fusion.where, bf16[4,576,128]{2,1,0:T(8,128)(2,1)S(1)} %pad_maximum_fusion.along.own_a, bf16[4,576,128]{2,1,0:T(8,128)(2,1)S(1)} %pad_maximum_fusion.1.across.own_b, bf16[128,4096]{1,0:T(8,128)(2,1)S(1)} %get-tuple-element.57.x), custom_call_target="tpu_custom_call" | custom-call | flops 1000000000 | bytes 10000000 | tf_op jit(solution)/shard_map/pallas_call | solution.py:454
  30.9 1.8 %shard_map.138.inner_oth = f32[2,512,128]{2,1,0:T(8,128)S(1)} custom-call(s32[2]{0:T(128)S(1)} %pad_add_fusion.where, bf16[4,576,128]{2,1,0:T(8,128)(2,1)S(1)} %collective-permute-done.7.along.oth_a, bf16[4,576,128]{2,1,0:T(8,128)(2,1)S(1)} %collective-permute-done.8.across.oth_b, bf16[256,4096]{1,0:T(8,128)(2,1)S(1)} %collective-permute-done.9.x.x_got), custom_call_target="tpu_custom_call" | custom-call | flops 1000000000 | bytes 10000000 | tf_op jit(solution)/shard_map/pallas_call | solution.py:454
  32.7 18.5 %shard_map.139 = (bf16[8,192,128]{2,1,0:T(8,128)(2,1)S(1)}, bf16[8,192,128]{2,1,0:T(8,128)(2,1)S(1)}, f32[2048,128]{1,0:T(8,128)S(1)}, f32[1024,128]{1,0:T(8,128...) custom-call(s32[2]{0:T(128)S(1)} %pad_add_fusion.where, ...), custom_call_target="tpu_custom_call" | custom-call | flops 5000000000 | bytes 40000000 | tf_op jit(solution)/shard_map/pallas_call | solution.py:470
  51.8 4.8 %shard_map.140 = (bf16[8,256,128]{2,1,0:T(8,128)(2,1)S(1)}, f32[2048,128]{1,0:T(8,128)S(1)}) custom-call(s32[2]{0:T(128)S(1)} %pad_add_fusion.where, s32[64]{0:T(128)S(1)} %copy-done, f32[2048,128]{1,0:T(8,128)S(1)} %get-tuple-element.28.inner, f32[1024,128]{1,0:T(8,128)S(1)} %get-tuple-element.29.ret, bf16[2,8,256,128]{3,2,1,0:T(8,128)(2,1)S(1)} %get-tuple-element.30.t_r, ...), custom_call_target="tpu_custom_call" | custom-call | flops 5000000000 | bytes 20000000 | tf_op jit(solution)/shard_map/pallas_call | solution.py:505
  57.3 4.8 %shard_map.141 = (bf16[8,256,128]{2,1,0:T(8,128)(2,1)S(1)}, f32[2048,128]{1,0:T(8,128)S(1)}) custom-call(s32[2]{0:T(128)S(1)} %pad_add_fusion.where, s32[64]{0:T(128)S(1)} %copy-done, f32[2048,128]{1,0:T(8,128)S(1)} %get-tuple-element.28.inner, f32[1024,128]{1,0:T(8,128)S(1)} %get-tuple-element.29.ret, bf16[2,8,256,128]{3,2,1,0:T(8,128)(2,1)S(1)} %get-tuple-element.30.t_r, ...), custom_call_target="tpu_custom_call" | custom-call | flops 5000000000 | bytes 20000000 | tf_op jit(solution)/shard_map/pallas_call | solution.py:505
  62.2 1.9 %collective-permute-done.19 = bf16[4,192,128]{2,1,0:T(8,128)(2,1)S(1)} collective-permute-done((bf16[4,192,128]{2,1,0:T(8,128)(2,1)S(1)}, bf16[4,192,128]{2,1,0:T(8,128)(2,1)S(1)}, u32[]{:S(2)}, u32[]{:S(2)}) %collective-permute-start.19) | collective-permute-done | bytes 196640 | tf_op jit(solution)/shard_map/ppermute | solution.py:535
  65.9 2.9 %shard_map.142 = (bf16[8,128,128]{2,1,0:T(8,128)(2,1)S(1)}, bf16[8,128,128]{2,1,0:T(8,128)(2,1)S(1)}) custom-call(s32[2]{0:T(128)S(1)} %pad_add_fusion.where, f32[2048,128]{1,0:T(8,128)S(1)} %get-tuple-element.44.back, bf16[128,4096]{1,0:T(8,128)(2,1)S(1)} %get-tuple-element.57.x, bf16[256,4096]{1,0:T(8,128)(2,1)S(1)} %collective-permute-done.9.x.x_got), custom_call_target="tpu_custom_call" | custom-call | flops 1000000000 | bytes 10000000 | tf_op jit(solution)/shard_map/pallas_call | solution.py:521
  69.0 2.2 %collective-permute-start.22 = (bf16[192,128]{1,0:T(8,128)(2,1)S(1)}, bf16[192,128]{1,0:T(8,128)(2,1)S(1)}, u32[]{:S(2)}, u32[]{:S(2)}) collective-permute-start(bf16[192,128]{1,0:T(8,128)(2,1)S(1)} %get-tuple-element.52), channel_id=1, source_target_pairs={{0,8},{2,10},{4,12},{6,14},{8,0},{10,2},{12,4},{14,6},{1,9},{3,11}... | collective-permute-start | bytes 147464 | tf_op jit(solution)/shard_map/ppermute | solution.py:535
  71.2 1.7 %collective-permute-start.14 = (bf16[4,128,128]{2,1,0:T(8,128)(2,1)S(1)}, bf16[4,128,128]{2,1,0:T(8,128)(2,1)S(1)}, u32[]{:S(2)}, u32[]{:S(2)}) collective-permute-start(bf16[4,128,128]{2,1,0:T(8,128)(2,1)S(1)} %add_convert_fusion.6), channel_id=1, source_target_pairs={{0,2},{2,0},{4,6},{6,4},{8,10},{10,8},{12,14},{14,12},{1,3},{3,1},... | collective-permute-start | bytes 393224 | tf_op jit(solution)/shard_map/ppermute | solution.py:535
  74.2 2.6 %collective-permute-done.14 = bf16[4,128,128]{2,1,0:T(8,128)(2,1)S(1)} collective-permute-done((bf16[4,128,128]{2,1,0:T(8,128)(2,1)S(1)}, bf16[4,128,128]{2,1,0:T(8,128)(2,1)S(1)}, u32[]{:S(2)}, u32[]{:S(2)}) %collective-permute-start.14) | collective-permute-done | bytes 131104 | tf_op jit(solution)/shard_map/ppermute | solution.py:535
  78.4 2.1 %collective-permute-start.21 = (bf16[256,128]{1,0:T(8,128)(2,1)S(1)}, bf16[256,128]{1,0:T(8,128)(2,1)S(1)}, u32[]{:S(2)}, u32[]{:S(2)}) collective-permute-start(bf16[256,128]{1,0:T(8,128)(2,1)S(1)} %get-tuple-element.49), channel_id=1, source_target_pairs={{0,8},{2,10},{4,12},{6,14},{8,0},{10,2},{12,4},{14,6},{1,9},{3,11}... | collective-permute-start | bytes 196616 | tf_op jit(solution)/shard_map/ppermute | solution.py:535
  80.5 1.4 %collective-permute-done.15 = bf16[2,128,128]{2,1,0:T(8,128)(2,1)S(1)} collective-permute-done((bf16[2,128,128]{2,1,0:T(8,128)(2,1)S(1)}, bf16[2,128,128]{2,1,0:T(8,128)(2,1)S(1)}, u32[]{:S(2)}, u32[]{:S(2)}) %collective-permute-start.15) | collective-permute-done | bytes 65568 | tf_op jit(solution)/shard_map/ppermute | solution.py:535
  82.0 1.3 %collective-permute-start.18 = (bf16[128,128]{1,0:T(8,128)(2,1)S(1)}, bf16[128,128]{1,0:T(8,128)(2,1)S(1)}, u32[]{:S(2)}, u32[]{:S(2)}) collective-permute-start(bf16[128,128]{1,0:T(8,128)(2,1)S(1)} %get-tuple-element.48), channel_id=1, source_target_pairs={{0,8},{2,10},{4,12},{6,14},{8,0},{10,2},{12,4},{14,6},{1,9},{3,11}... | collective-permute-start | bytes 98312 | tf_op jit(solution)/shard_map/ppermute | solution.py:535
  83.3 1.7 %collective-permute-done.21.refs_3_ = bf16[256,128]{1,0:T(8,128)(2,1)S(1)} collective-permute-done((bf16[256,128]{1,0:T(8,128)(2,1)S(1)}, bf16[256,128]{1,0:T(8,128)(2,1)S(1)}, u32[]{:S(2)}, u32[]{:S(2)}) %collective-permute-start.21) | collective-permute-done | bytes 65568 | tf_op jit(solution)/shard_map/ppermute | solution.py:535
  84.9 2.0 %collective-permute-done.18.refs_1_ = bf16[128,128]{1,0:T(8,128)(2,1)S(1)} collective-permute-done((bf16[128,128]{1,0:T(8,128)(2,1)S(1)}, bf16[128,128]{1,0:T(8,128)(2,1)S(1)}, u32[]{:S(2)}, u32[]{:S(2)}) %collective-permute-start.18) | collective-permute-done | bytes 32800 | tf_op jit(solution)/shard_map/ppermute | solution.py:535
  (53 shorter events, 11.5 us)
Async XLA Ops:
  0.6 30.3 %collective-permute-start.9 = (bf16[256,4096]{1,0:T(8,128)(2,1)}, bf16[256,4096]{1,0:T(8,128)(2,1)S(1)}, u32[]{:S(2)}, u32[]{:S(2)}) collective-permute-start(bf16[256,4096]{1,0:T(8,128)(2,1)} %param.9), channel_id=1, source_target_pairs={{0,1},{1,0},{2,3},{3,2},{4,5},{5,4},{6,7},{7,6},{8,9},{9,8},{10,11... | collective-permute-start | bytes 6291464 | tf_op jit(solution)/shard_map/ppermute | solution.py:535
  1.2 31.6 %collective-permute-start.10 = (bf16[256,4096]{1,0:T(8,128)(2,1)}, bf16[256,4096]{1,0:T(8,128)(2,1)}, u32[]{:S(2)}, u32[]{:S(2)}) collective-permute-start(bf16[256,4096]{1,0:T(8,128)(2,1)} %param.10), channel_id=1, source_target_pairs={{0,1},{1,0},{2,3},{3,2},{4,5},{5,4},{6,7},{7,6},{8,9},{9,8},{10,11... | collective-permute-start | bytes 6291464 | tf_op jit(solution)/shard_map/ppermute | solution.py:535
  3.0 7.3 %collective-permute-start.3 = (bf16[576,128]{1,0:T(8,128)(2,1)}, bf16[576,128]{1,0:T(8,128)(2,1)S(1)}, u32[]{:S(2)}, u32[]{:S(2)}) collective-permute-start(bf16[576,128]{1,0:T(8,128)(2,1)} %shard_map.136), channel_id=1, source_target_pairs={{0,2},{2,0},{4,6},{6,4},{8,10},{10,8},{12,14},{14,12},{1,3},{3,1},... | collective-permute-start | bytes 442376 | tf_op jit(solution)/shard_map/ppermute | solution.py:535
  6.0 8.7 %collective-permute-start.2 = (bf16[576,128]{1,0:T(8,128)(2,1)}, bf16[576,128]{1,0:T(8,128)(2,1)S(1)}, u32[]{:S(2)}, u32[]{:S(2)}) collective-permute-start(bf16[576,128]{1,0:T(8,128)(2,1)} %shard_map.136), channel_id=1, source_target_pairs={{0,12},{2,14},{4,8},{6,10},{8,4},{10,6},{12,0},{14,2},{1,13},{3,15... | collective-permute-start | bytes 442376 | tf_op jit(solution)/shard_map/ppermute | solution.py:535
  9.6 8.3 %collective-permute-start.1 = (bf16[576,128]{1,0:T(8,128)(2,1)}, bf16[576,128]{1,0:T(8,128)(2,1)S(1)}, u32[]{:S(2)}, u32[]{:S(2)}) collective-permute-start(bf16[576,128]{1,0:T(8,128)(2,1)} %shard_map.136), channel_id=1, source_target_pairs={{0,4},{2,6},{4,0},{6,2},{8,12},{10,14},{12,8},{14,10},{1,5},{3,7},... | collective-permute-start | bytes 442376 | tf_op jit(solution)/shard_map/ppermute | solution.py:535
  10.3 12.0 %collective-permute-start = (bf16[576,128]{1,0:T(8,128)(2,1)}, bf16[576,128]{1,0:T(8,128)(2,1)S(1)}, u32[]{:S(2)}, u32[]{:S(2)}) collective-permute-start(bf16[576,128]{1,0:T(8,128)(2,1)} %shard_map.136), channel_id=1, source_target_pairs={{0,8},{2,10},{4,12},{6,14},{8,0},{10,2},{12,4},{14,6},{1,9},{3,11}... | collective-permute-start | bytes 442376 | tf_op jit(solution)/shard_map/ppermute | solution.py:535
  14.8 9.3 %collective-permute-start.6 = (bf16[576,128]{1,0:T(8,128)(2,1)S(1)}, bf16[576,128]{1,0:T(8,128)(2,1)S(1)}, u32[]{:S(2)}, u32[]{:S(2)}) collective-permute-start(bf16[576,128]{1,0:T(8,128)(2,1)S(1)} %collective-permute-done.2), channel_id=1, source_target_pairs={{0,2},{2,0},{4,6},{6,4},{8,10},{10,8},{12,14},{14,12},{1,3},{3,1},... | collective-permute-start | bytes 442376 | tf_op jit(solution)/shard_map/ppermute | solution.py:535
  17.9 6.2 %collective-permute-start.5 = (bf16[576,128]{1,0:T(8,128)(2,1)S(1)}, bf16[576,128]{1,0:T(8,128)(2,1)S(1)}, u32[]{:S(2)}, u32[]{:S(2)}) collective-permute-start(bf16[576,128]{1,0:T(8,128)(2,1)S(1)} %collective-permute-done.1), channel_id=1, source_target_pairs={{0,2},{2,0},{4,6},{6,4},{8,10},{10,8},{12,14},{14,12},{1,3},{3,1},... | collective-permute-start | bytes 442376 | tf_op jit(solution)/shard_map/ppermute | solution.py:535
  22.3 5.1 %collective-permute-start.4 = (bf16[576,128]{1,0:T(8,128)(2,1)S(1)}, bf16[576,128]{1,0:T(8,128)(2,1)S(1)}, u32[]{:S(2)}, u32[]{:S(2)}) collective-permute-start(bf16[576,128]{1,0:T(8,128)(2,1)S(1)} %collective-permute-done), channel_id=1, source_target_pairs={{0,2},{2,0},{4,6},{6,4},{8,10},{10,8},{12,14},{14,12},{1,3},{3,1},... | collective-permute-start | bytes 442376 | tf_op jit(solution)/shard_map/ppermute | solution.py:535
  22.9 4.7 %copy-start.1 = (bf16[256,4096]{1,0:T(8,128)(2,1)S(1)}, bf16[256,4096]{1,0:T(8,128)(2,1)}, u32[]{:S(2)}) copy-start(bf16[256,4096]{1,0:T(8,128)(2,1)} %param.9) | copy-start | bytes 6291460
  24.0 6.8 %collective-permute-start.7 = (bf16[4,576,128]{2,1,0:T(8,128)(2,1)S(1)}, bf16[4,576,128]{2,1,0:T(8,128)(2,1)S(1)}, u32[]{:S(2)}, u32[]{:S(2)}) collective-permute-start(bf16[4,576,128]{2,1,0:T(8,128)(2,1)S(1)} %pad_maximum_fusion.along.own_a), channel_id=1, source_target_pairs={{0,1},{1,0},{2,3},{3,2},{4,5},{5,4},{6,7},{7,6},{8,9},{9,8},{10,11... | collective-permute-start | bytes 1769480 | tf_op jit(solution)/shard_map/ppermute | solution.py:535
  27.5 3.4 %collective-permute-start.8 = (bf16[4,576,128]{2,1,0:T(8,128)(2,1)S(1)}, bf16[4,576,128]{2,1,0:T(8,128)(2,1)S(1)}, u32[]{:S(2)}, u32[]{:S(2)}) collective-permute-start(bf16[4,576,128]{2,1,0:T(8,128)(2,1)S(1)} %pad_maximum_fusion.1.across.own_b), channel_id=1, source_target_pairs={{0,1},{1,0},{2,3},{3,2},{4,5},{5,4},{6,7},{7,6},{8,9},{9,8},{10,11... | collective-permute-start | bytes 1769480 | tf_op jit(solution)/shard_map/ppermute | solution.py:535
  51.2 5.4 %collective-permute-start.11 = (bf16[8,192,128]{2,1,0:T(8,128)(2,1)S(1)}, bf16[8,192,128]{2,1,0:T(8,128)(2,1)S(1)}, u32[]{:S(2)}, u32[]{:S(2)}) collective-permute-start(bf16[8,192,128]{2,1,0:T(8,128)(2,1)S(1)} %get-tuple-element.38), channel_id=1, source_target_pairs={{0,1},{1,0},{2,3},{3,2},{4,5},{5,4},{6,7},{7,6},{8,9},{9,8},{10,11... | collective-permute-start | bytes 1179656 | tf_op jit(solution)/shard_map/ppermute | solution.py:535
  56.6 8.7 %collective-permute-start.12 = (bf16[8,256,128]{2,1,0:T(8,128)(2,1)S(1)}, bf16[8,256,128]{2,1,0:T(8,128)(2,1)S(1)}, u32[]{:S(2)}, u32[]{:S(2)}) collective-permute-start(bf16[8,256,128]{2,1,0:T(8,128)(2,1)S(1)} %get-tuple-element.43), channel_id=1, source_target_pairs={{0,1},{1,0},{2,3},{3,2},{4,5},{5,4},{6,7},{7,6},{8,9},{9,8},{10,11... | collective-permute-start | bytes 1572872 | tf_op jit(solution)/shard_map/ppermute | solution.py:535
  56.7 7.4 %collective-permute-start.19 = (bf16[4,192,128]{2,1,0:T(8,128)(2,1)S(1)}, bf16[4,192,128]{2,1,0:T(8,128)(2,1)S(1)}, u32[]{:S(2)}, u32[]{:S(2)}) collective-permute-start(bf16[4,192,128]{2,1,0:T(8,128)(2,1)S(1)} %add_convert_fusion.3), channel_id=1, source_target_pairs={{0,2},{2,0},{4,6},{6,4},{8,10},{10,8},{12,14},{14,12},{1,3},{3,1},... | collective-permute-start | bytes 589832 | tf_op jit(solution)/shard_map/ppermute | solution.py:535
  64.2 4.7 %collective-permute-start.20 = (bf16[2,192,128]{2,1,0:T(8,128)(2,1)S(1)}, bf16[2,192,128]{2,1,0:T(8,128)(2,1)S(1)}, u32[]{:S(2)}, u32[]{:S(2)}) collective-permute-start(bf16[2,192,128]{2,1,0:T(8,128)(2,1)S(1)} %slice.108), channel_id=1, source_target_pairs={{0,4},{2,6},{4,0},{6,2},{8,12},{10,14},{12,8},{14,10},{1,5},{3,7},... | collective-permute-start | bytes 294920 | tf_op jit(solution)/shard_map/ppermute | solution.py:535
  65.4 7.7 %collective-permute-start.16 = (bf16[4,256,128]{2,1,0:T(8,128)(2,1)S(1)}, bf16[4,256,128]{2,1,0:T(8,128)(2,1)S(1)}, u32[]{:S(2)}, u32[]{:S(2)}) collective-permute-start(bf16[4,256,128]{2,1,0:T(8,128)(2,1)S(1)} %add_convert_fusion.1), channel_id=1, source_target_pairs={{0,2},{2,0},{4,6},{6,4},{8,10},{10,8},{12,14},{14,12},{1,3},{3,1},... | collective-permute-start | bytes 786440 | tf_op jit(solution)/shard_map/ppermute | solution.py:535
  68.8 2.3 %collective-permute-start.13 = (bf16[8,128,128]{2,1,0:T(8,128)(2,1)S(1)}, bf16[8,128,128]{2,1,0:T(8,128)(2,1)S(1)}, u32[]{:S(2)}, u32[]{:S(2)}) collective-permute-start(bf16[8,128,128]{2,1,0:T(8,128)(2,1)S(1)} %get-tuple-element.46), channel_id=1, source_target_pairs={{0,1},{1,0},{2,3},{3,2},{4,5},{5,4},{6,7},{7,6},{8,9},{9,8},{10,11... | collective-permute-start | bytes 786440 | tf_op jit(solution)/shard_map/ppermute | solution.py:535
  69.0 14.3 %collective-permute-start.22 = (bf16[192,128]{1,0:T(8,128)(2,1)S(1)}, bf16[192,128]{1,0:T(8,128)(2,1)S(1)}, u32[]{:S(2)}, u32[]{:S(2)}) collective-permute-start(bf16[192,128]{1,0:T(8,128)(2,1)S(1)} %get-tuple-element.52), channel_id=1, source_target_pairs={{0,8},{2,10},{4,12},{6,14},{8,0},{10,2},{12,4},{14,6},{1,9},{3,11}... | collective-permute-start | bytes 147464 | tf_op jit(solution)/shard_map/ppermute | solution.py:535
  71.2 5.7 %collective-permute-start.14 = (bf16[4,128,128]{2,1,0:T(8,128)(2,1)S(1)}, bf16[4,128,128]{2,1,0:T(8,128)(2,1)S(1)}, u32[]{:S(2)}, u32[]{:S(2)}) collective-permute-start(bf16[4,128,128]{2,1,0:T(8,128)(2,1)S(1)} %add_convert_fusion.6), channel_id=1, source_target_pairs={{0,2},{2,0},{4,6},{6,4},{8,10},{10,8},{12,14},{14,12},{1,3},{3,1},... | collective-permute-start | bytes 393224 | tf_op jit(solution)/shard_map/ppermute | solution.py:535
  73.2 5.2 %collective-permute-start.17 = (bf16[2,256,128]{2,1,0:T(8,128)(2,1)S(1)}, bf16[2,256,128]{2,1,0:T(8,128)(2,1)S(1)}, u32[]{:S(2)}, u32[]{:S(2)}) collective-permute-start(bf16[2,256,128]{2,1,0:T(8,128)(2,1)S(1)} %slice.87), channel_id=1, source_target_pairs={{0,4},{2,6},{4,0},{6,2},{8,12},{10,14},{12,8},{14,10},{1,5},{3,7},... | collective-permute-start | bytes 393224 | tf_op jit(solution)/shard_map/ppermute | solution.py:535
  76.9 5.0 %collective-permute-start.15 = (bf16[2,128,128]{2,1,0:T(8,128)(2,1)S(1)}, bf16[2,128,128]{2,1,0:T(8,128)(2,1)S(1)}, u32[]{:S(2)}, u32[]{:S(2)}) collective-permute-start(bf16[2,128,128]{2,1,0:T(8,128)(2,1)S(1)} %slice.100), channel_id=1, source_target_pairs={{0,4},{2,6},{4,0},{6,2},{8,12},{10,14},{12,8},{14,10},{1,5},{3,7},... | collective-permute-start | bytes 196616 | tf_op jit(solution)/shard_map/ppermute | solution.py:535
  78.4 6.5 %collective-permute-start.21 = (bf16[256,128]{1,0:T(8,128)(2,1)S(1)}, bf16[256,128]{1,0:T(8,128)(2,1)S(1)}, u32[]{:S(2)}, u32[]{:S(2)}) collective-permute-start(bf16[256,128]{1,0:T(8,128)(2,1)S(1)} %get-tuple-element.49), channel_id=1, source_target_pairs={{0,8},{2,10},{4,12},{6,14},{8,0},{10,2},{12,4},{14,6},{1,9},{3,11}... | collective-permute-start | bytes 196616 | tf_op jit(solution)/shard_map/ppermute | solution.py:535
  82.0 4.9 %collective-permute-start.18 = (bf16[128,128]{1,0:T(8,128)(2,1)S(1)}, bf16[128,128]{1,0:T(8,128)(2,1)S(1)}, u32[]{:S(2)}, u32[]{:S(2)}) collective-permute-start(bf16[128,128]{1,0:T(8,128)(2,1)S(1)} %get-tuple-element.48), channel_id=1, source_target_pairs={{0,8},{2,10},{4,12},{6,14},{8,0},{10,2},{12,4},{14,6},{1,9},{3,11}... | collective-permute-start | bytes 98312 | tf_op jit(solution)/shard_map/ppermute | solution.py:535
  (1 other events, 1.9 us)

commit v6 on v5

--- a/solution.py
+++ b/solution.py
@@ -193,7 +193,7 @@
             inner[gu, rows(i, 128), :] = rounded(total[:, gu * 128 : (gu + 1) * 128].T)
         return 0
 
-    lax.fori_loop(0, 4, step, 0)
+    lax.fori_loop(0, 4, step, 0, unroll=4)
 
 
 def by_parity(ref, m):
@@ -280,7 +280,7 @@
         return 0
 
     for b in range(2):
-        lax.fori_loop(0, 4, functools.partial(second, b=b), 0)
+        lax.fori_loop(0, 4, functools.partial(second, b=b), 0, unroll=4)
 
     def put(b, base, value):
         for al in range(2):
@@ -315,7 +315,7 @@
                 ret[pl.ds(order[k], RANK, stride=NB), :] = total[u * RANK : (u + 1) * RANK]
             return 0
 
-        lax.fori_loop(0, 4, third, 0)
+        lax.fori_loop(0, 4, third, 0, unroll=4)
 
     def inward(i, _, b):
         g = (side ^ b) * 4 + i
@@ -334,7 +334,7 @@
         return 0
 
     for b in range(2):
-        lax.fori_loop(0, 4, functools.partial(inward, b=b), 0)
+        lax.fori_loop(0, 4, functools.partial(inward, b=b), 0, unroll=4)
 
     for b, out in enumerate([keep, send]):
         for r in range(CHUNKS):
@@ -377,7 +377,7 @@
                         ]
         return 0
 
-    lax.fori_loop(0, 4, step, 0)
+    lax.fori_loop(0, 4, step, 0, unroll=4)
     for r in range(CHUNKS):
         grads_out[r] = g_out[rows(chunk_of(me, r), RIGHT), :].astype(bf16)
 
@@ -407,7 +407,7 @@
                 turned[rows(gu * 4 + i, 128), :] = jnp.concatenate(parts[gu], axis=0).T.astype(bf16)
             return 0
 
-        lax.fori_loop(0, 4, step, 0)
+        lax.fori_loop(0, 4, step, 0, unroll=4)
         for r in range(CHUNKS):
             d = chunk_of(me, r)
             for gg in range(8):

time: 88.3 us -> 81.5 us (0.923)
  Pallas kernels: 37.5 us -> 28 us
  waiting for transfers between devices: 23 us -> 26.7 us
  starting transfers between devices: 23.2 us -> 22.3 us
    pallas_call x1, Pallas kernels: 18.5 us -> 13.2 us  [middle_call(): pl.pallas_call(functools.partial(middle_body, scale), out_shape=(down, do...]
    ppermute x23, waiting for transfers between devices: 23 us -> 26.7 us  [swap(): return lax.ppermute(v, axis, [(i, i ^ bit) for i in range(size)])]
    pallas_call x1, Pallas kernels: 2.95 us -> 1.15 us  [left_call(): pl.pallas_call(left_body, out_shape=(grads, grads), in_specs=[SMEM] + [VM...]
    pallas_call x2, Pallas kernels: 3.64 us -> 2.19 us  [inner_call(): pl.pallas_call(inner_body, grid=(1,), out_shape=jax.ShapeDtypeStruct((2,...]
    pallas_call x2, Pallas kernels: 9.59 us -> 8.58 us  [right_call(): pl.pallas_call(functools.partial(right_body, b), out_shape=(jax.ShapeDtyp...]
    ppermute x23, starting transfers between devices: 23.2 us -> 22.3 us  [swap(): return lax.ppermute(v, axis, [(i, i ^ bit) for i in range(size)])]
  transfers between devices with their start and end apart: 23 -> 23, of which waited for: 12 -> 12; matrix products, arithmetic and copies ran while one was open for 4% -> 4% of each run, Pallas kernels for 20% -> 17%
where the time goes in v6:
time: 81.5 us; the launch traced here: 81.2 us
  Pallas kernels  28 us (34%)
  waiting for transfers between devices  26.7 us (33%)
  starting transfers between devices  22.3 us (27%)
  other arithmetic  1.78 us (2%)
  local copies, waits for them, and re-layouts  1.5 us (2%)
  between operations  0.92 us (1%)
    ppermute x23, waiting for transfers between devices, swap(): return lax.ppermute(v, axis, [(i, i ^ bit) for i in range(size)])  26.7 us
    ppermute x23, starting transfers between devices, swap(): return lax.ppermute(v, axis, [(i, i ^ bit) for i in range(size)])  22.3 us
    pallas_call x1, Pallas kernels, middle_call(): pl.pallas_call(functools.partial(middle_body, scale), out_shape=(down, do...  13.2 us
    pallas_call x2, Pallas kernels, right_call(): pl.pallas_call(functools.partial(right_body, b), out_shape=(jax.ShapeDtyp...  8.58 us
    pallas_call x2, Pallas kernels, inner_call(): pl.pallas_call(inner_body, grid=(1,), out_shape=jax.ShapeDtypeStruct((2,...  2.19 us
    pallas_call x1, Pallas kernels, prepare_call(): pl.pallas_call(prepare_body, out_shape=jax.ShapeDtypeStruct((FIRST + REST...  1.79 us
  transfers between devices with their start and end apart: 23, of which 12 were waited for; matrix products, arithmetic and copies ran while one was open for 4% of the time, Pallas kernels for 17%

profile of v6, /device:TPU:0, one launch (start us, length us, event | category | flops | bytes accessed | tf_op | source)
XLA Modules:
  0.0 81.2 jit_solution(13166401427012518104)
XLA Ops:
  1.2 1.8 %shard_map.136 = bf16[576,128]{1,0:T(8,128)(2,1)} custom-call(bf16[32,256]{1,0:T(8,128)(2,1)} %refs_0_.1, bf16[32,448]{1,0:T(8,128)(2,1)} %refs_1_.1, bf16[32,256]{1,0:T(8,128)(2,1)} %refs_2_.1, bf16[32,448]{1,0:T(8,128)(2,1)} %refs_3_.1, bf16[32,448]{1,0:T(8,128)(2,1)} %refs_4_.1, bf16[32,256]{1,0:T(8,128)(2,1)} %refs_5_.1), custom_call_target="tpu_custom_call" | custom-call | tf_op jit(solution)/shard_map/pallas_call | solution.py:429
  3.0 3.0 %collective-permute-start.3 = (bf16[576,128]{1,0:T(8,128)(2,1)}, bf16[576,128]{1,0:T(8,128)(2,1)S(1)}, u32[]{:S(2)}, u32[]{:S(2)}) collective-permute-start(bf16[576,128]{1,0:T(8,128)(2,1)} %shard_map.136), channel_id=1, source_target_pairs={{0,2},{2,0},{4,6},{6,4},{8,10},{10,8},{12,14},{14,12},{1,3},{3,1},... | collective-permute-start | bytes 442376 | tf_op jit(solution)/shard_map/ppermute | solution.py:535
  6.0 3.6 %collective-permute-start.2 = (bf16[576,128]{1,0:T(8,128)(2,1)}, bf16[576,128]{1,0:T(8,128)(2,1)S(1)}, u32[]{:S(2)}, u32[]{:S(2)}) collective-permute-start(bf16[576,128]{1,0:T(8,128)(2,1)} %shard_map.136), channel_id=1, source_target_pairs={{0,12},{2,14},{4,8},{6,10},{8,4},{10,6},{12,0},{14,2},{1,13},{3,15... | collective-permute-start | bytes 442376 | tf_op jit(solution)/shard_map/ppermute | solution.py:535
  10.3 2.8 %collective-permute-start = (bf16[576,128]{1,0:T(8,128)(2,1)}, bf16[576,128]{1,0:T(8,128)(2,1)S(1)}, u32[]{:S(2)}, u32[]{:S(2)}) collective-permute-start(bf16[576,128]{1,0:T(8,128)(2,1)} %shard_map.136), channel_id=1, source_target_pairs={{0,8},{2,10},{4,12},{6,14},{8,0},{10,2},{12,4},{14,6},{1,9},{3,11}... | collective-permute-start | bytes 442376 | tf_op jit(solution)/shard_map/ppermute | solution.py:535
  13.2 1.6 %collective-permute-done.2 = bf16[576,128]{1,0:T(8,128)(2,1)S(1)} collective-permute-done((bf16[576,128]{1,0:T(8,128)(2,1)}, bf16[576,128]{1,0:T(8,128)(2,1)S(1)}, u32[]{:S(2)}, u32[]{:S(2)}) %collective-permute-start.2) | collective-permute-done | bytes 147488 | tf_op jit(solution)/shard_map/ppermute | solution.py:535
  15.1 2.8 %collective-permute-done.1 = bf16[576,128]{1,0:T(8,128)(2,1)S(1)} collective-permute-done((bf16[576,128]{1,0:T(8,128)(2,1)}, bf16[576,128]{1,0:T(8,128)(2,1)S(1)}, u32[]{:S(2)}, u32[]{:S(2)}) %collective-permute-start.1) | collective-permute-done | bytes 147488 | tf_op jit(solution)/shard_map/ppermute | solution.py:535
  18.5 3.8 %collective-permute-done = bf16[576,128]{1,0:T(8,128)(2,1)S(1)} collective-permute-done((bf16[576,128]{1,0:T(8,128)(2,1)}, bf16[576,128]{1,0:T(8,128)(2,1)S(1)}, u32[]{:S(2)}, u32[]{:S(2)}) %collective-permute-start) | collective-permute-done | bytes 147488 | tf_op jit(solution)/shard_map/ppermute | solution.py:535
  22.9 1.1 %pad_maximum_fusion.along.own_a = bf16[4,576,128]{2,1,0:T(8,128)(2,1)S(1)} fusion(bf16[1,576,128]{2,1,0:T(8,128)(2,1)S(1)} %bitcast.26, bf16[1,576,128]{2,1,0:T(8,128)(2,1)S(1)} %bitcast.24, bf16[1,576,128]{2,1,0:T(8,128)(2,1)S(1)} %bitcast.25, bf16[1,576,128]{2,1,0:T(8,128)(2,1)} %bitcast.22), kind=kLoop, calls=%fused_computation | loop fusion | flops 884736 | bytes 1179648 | tf_op jit(solution)/shard_map/stack | solution.py:546
  24.1 3.3 %collective-permute-done.4 = bf16[576,128]{1,0:T(8,128)(2,1)S(1)} collective-permute-done((bf16[576,128]{1,0:T(8,128)(2,1)S(1)}, bf16[576,128]{1,0:T(8,128)(2,1)S(1)}, u32[]{:S(2)}, u32[]{:S(2)}) %collective-permute-start.4) | collective-permute-done | bytes 147488 | tf_op jit(solution)/shard_map/ppermute | solution.py:535
  27.6 1.4 %constant_dynamic-slice_fusion = (bf16[128,4096]{1,0:T(8,128)(2,1)S(1)}, bf16[128,4096]{1,0:T(8,128)(2,1)S(1)}) fusion(bf16[256,4096]{1,0:T(8,128)(2,1)} %param.10, s32[]{:T(128)S(6)} %select_n.4, bf16[256,4096]{1,0:T(8,128)(2,1)S(1)} %copy-done.1), kind=kLoop, calls=%fused_computation.18 | loop fusion | bytes 4194308 | tf_op jit(solution)/shard_map/dynamic_slice | solution.py:589
  31.3 13.2 %shard_map.139 = (bf16[8,192,128]{2,1,0:T(8,128)(2,1)S(1)}, bf16[8,192,128]{2,1,0:T(8,128)(2,1)S(1)}, f32[2048,128]{1,0:T(8,128)S(1)}, f32[1024,128]{1,0:T(8,128...) custom-call(s32[2]{0:T(128)S(1)} %pad_add_fusion.where, ...), custom_call_target="tpu_custom_call" | custom-call | flops 5000000000 | bytes 40000000 | tf_op jit(solution)/shard_map/pallas_call | solution.py:470
  45.1 4.2 %shard_map.140 = (bf16[8,256,128]{2,1,0:T(8,128)(2,1)S(1)}, f32[2048,128]{1,0:T(8,128)S(1)}) custom-call(s32[2]{0:T(128)S(1)} %pad_add_fusion.where, s32[64]{0:T(128)S(1)} %copy-done, f32[2048,128]{1,0:T(8,128)S(1)} %get-tuple-element.28.inner, f32[1024,128]{1,0:T(8,128)S(1)} %get-tuple-element.29.ret, bf16[2,8,256,128]{3,2,1,0:T(8,128)(2,1)S(1)} %get-tuple-element.30.t_r, ...), custom_call_target="tpu_custom_call" | custom-call | flops 5000000000 | bytes 20000000 | tf_op jit(solution)/shard_map/pallas_call | solution.py:505
  50.0 4.4 %shard_map.141 = (bf16[8,256,128]{2,1,0:T(8,128)(2,1)S(1)}, f32[2048,128]{1,0:T(8,128)S(1)}) custom-call(s32[2]{0:T(128)S(1)} %pad_add_fusion.where, s32[64]{0:T(128)S(1)} %copy-done, f32[2048,128]{1,0:T(8,128)S(1)} %get-tuple-element.28.inner, f32[1024,128]{1,0:T(8,128)S(1)} %get-tuple-element.29.ret, bf16[2,8,256,128]{3,2,1,0:T(8,128)(2,1)S(1)} %get-tuple-element.30.t_r, ...), custom_call_target="tpu_custom_call" | custom-call | flops 5000000000 | bytes 20000000 | tf_op jit(solution)/shard_map/pallas_call | solution.py:505
  54.4 2.3 %collective-permute-done.19 = bf16[4,192,128]{2,1,0:T(8,128)(2,1)S(1)} collective-permute-done((bf16[4,192,128]{2,1,0:T(8,128)(2,1)S(1)}, bf16[4,192,128]{2,1,0:T(8,128)(2,1)S(1)}, u32[]{:S(2)}, u32[]{:S(2)}) %collective-permute-start.19) | collective-permute-done | bytes 196640 | tf_op jit(solution)/shard_map/ppermute | solution.py:535
  58.5 1.1 %shard_map.142 = (bf16[8,128,128]{2,1,0:T(8,128)(2,1)S(1)}, bf16[8,128,128]{2,1,0:T(8,128)(2,1)S(1)}) custom-call(s32[2]{0:T(128)S(1)} %pad_add_fusion.where, f32[2048,128]{1,0:T(8,128)S(1)} %get-tuple-element.44.back, bf16[128,4096]{1,0:T(8,128)(2,1)S(1)} %get-tuple-element.57.x, bf16[256,4096]{1,0:T(8,128)(2,1)S(1)} %collective-permute-done.9.x.x_got), custom_call_target="tpu_custom_call" | custom-call | flops 1000000000 | bytes 10000000 | tf_op jit(solution)/shard_map/pallas_call | solution.py:521
  59.8 1.8 %collective-permute-done.20 = bf16[2,192,128]{2,1,0:T(8,128)(2,1)S(1)} collective-permute-done((bf16[2,192,128]{2,1,0:T(8,128)(2,1)S(1)}, bf16[2,192,128]{2,1,0:T(8,128)(2,1)S(1)}, u32[]{:S(2)}, u32[]{:S(2)}) %collective-permute-start.20) | collective-permute-done | bytes 98336 | tf_op jit(solution)/shard_map/ppermute | solution.py:535
  61.6 1.2 %collective-permute-start.22 = (bf16[192,128]{1,0:T(8,128)(2,1)S(1)}, bf16[192,128]{1,0:T(8,128)(2,1)S(1)}, u32[]{:S(2)}, u32[]{:S(2)}) collective-permute-start(bf16[192,128]{1,0:T(8,128)(2,1)S(1)} %get-tuple-element.52), channel_id=1, source_target_pairs={{0,8},{2,10},{4,12},{6,14},{8,0},{10,2},{12,4},{14,6},{1,9},{3,11}... | collective-permute-start | bytes 147464 | tf_op jit(solution)/shard_map/ppermute | solution.py:535
  63.7 2.8 %collective-permute-done.16 = bf16[4,256,128]{2,1,0:T(8,128)(2,1)S(1)} collective-permute-done((bf16[4,256,128]{2,1,0:T(8,128)(2,1)S(1)}, bf16[4,256,128]{2,1,0:T(8,128)(2,1)S(1)}, u32[]{:S(2)}, u32[]{:S(2)}) %collective-permute-start.16) | collective-permute-done | bytes 262176 | tf_op jit(solution)/shard_map/ppermute | solution.py:535
  66.6 1.2 %collective-permute-start.17 = (bf16[2,256,128]{2,1,0:T(8,128)(2,1)S(1)}, bf16[2,256,128]{2,1,0:T(8,128)(2,1)S(1)}, u32[]{:S(2)}, u32[]{:S(2)}) collective-permute-start(bf16[2,256,128]{2,1,0:T(8,128)(2,1)S(1)} %slice.87), channel_id=1, source_target_pairs={{0,4},{2,6},{4,0},{6,2},{8,12},{10,14},{12,8},{14,10},{1,5},{3,7},... | collective-permute-start | bytes 393224 | tf_op jit(solution)/shard_map/ppermute | solution.py:535
  68.6 1.4 %collective-permute-start.15 = (bf16[2,128,128]{2,1,0:T(8,128)(2,1)S(1)}, bf16[2,128,128]{2,1,0:T(8,128)(2,1)S(1)}, u32[]{:S(2)}, u32[]{:S(2)}) collective-permute-start(bf16[2,128,128]{2,1,0:T(8,128)(2,1)S(1)} %slice.100), channel_id=1, source_target_pairs={{0,4},{2,6},{4,0},{6,2},{8,12},{10,14},{12,8},{14,10},{1,5},{3,7},... | collective-permute-start | bytes 196616 | tf_op jit(solution)/shard_map/ppermute | solution.py:535
  70.0 3.1 %collective-permute-done.17 = bf16[2,256,128]{2,1,0:T(8,128)(2,1)S(1)} collective-permute-done((bf16[2,256,128]{2,1,0:T(8,128)(2,1)S(1)}, bf16[2,256,128]{2,1,0:T(8,128)(2,1)S(1)}, u32[]{:S(2)}, u32[]{:S(2)}) %collective-permute-start.17) | collective-permute-done | bytes 131104 | tf_op jit(solution)/shard_map/ppermute | solution.py:535
  73.1 2.1 %collective-permute-start.21 = (bf16[256,128]{1,0:T(8,128)(2,1)S(1)}, bf16[256,128]{1,0:T(8,128)(2,1)S(1)}, u32[]{:S(2)}, u32[]{:S(2)}) collective-permute-start(bf16[256,128]{1,0:T(8,128)(2,1)S(1)} %get-tuple-element.49), channel_id=1, source_target_pairs={{0,8},{2,10},{4,12},{6,14},{8,0},{10,2},{12,4},{14,6},{1,9},{3,11}... | collective-permute-start | bytes 196616 | tf_op jit(solution)/shard_map/ppermute | solution.py:535
  76.2 2.2 %collective-permute-done.21.refs_3_ = bf16[256,128]{1,0:T(8,128)(2,1)S(1)} collective-permute-done((bf16[256,128]{1,0:T(8,128)(2,1)S(1)}, bf16[256,128]{1,0:T(8,128)(2,1)S(1)}, u32[]{:S(2)}, u32[]{:S(2)}) %collective-permute-start.21) | collective-permute-done | bytes 65568 | tf_op jit(solution)/shard_map/ppermute | solution.py:535
  78.4 1.8 %collective-permute-done.18.refs_1_ = bf16[128,128]{1,0:T(8,128)(2,1)S(1)} collective-permute-done((bf16[128,128]{1,0:T(8,128)(2,1)S(1)}, bf16[128,128]{1,0:T(8,128)(2,1)S(1)}, u32[]{:S(2)}, u32[]{:S(2)}) %collective-permute-start.18) | collective-permute-done | bytes 32800 | tf_op jit(solution)/shard_map/ppermute | solution.py:535
  (53 shorter events, 12.4 us)
Async XLA Ops:
  0.6 29.5 %collective-permute-start.9 = (bf16[256,4096]{1,0:T(8,128)(2,1)}, bf16[256,4096]{1,0:T(8,128)(2,1)S(1)}, u32[]{:S(2)}, u32[]{:S(2)}) collective-permute-start(bf16[256,4096]{1,0:T(8,128)(2,1)} %param.9), channel_id=1, source_target_pairs={{0,1},{1,0},{2,3},{3,2},{4,5},{5,4},{6,7},{7,6},{8,9},{9,8},{10,11... | collective-permute-start | bytes 6291464 | tf_op jit(solution)/shard_map/ppermute | solution.py:535
  1.2 30.1 %collective-permute-start.10 = (bf16[256,4096]{1,0:T(8,128)(2,1)}, bf16[256,4096]{1,0:T(8,128)(2,1)}, u32[]{:S(2)}, u32[]{:S(2)}) collective-permute-start(bf16[256,4096]{1,0:T(8,128)(2,1)} %param.10), channel_id=1, source_target_pairs={{0,1},{1,0},{2,3},{3,2},{4,5},{5,4},{6,7},{7,6},{8,9},{9,8},{10,11... | collective-permute-start | bytes 6291464 | tf_op jit(solution)/shard_map/ppermute | solution.py:535
  3.0 7.3 %collective-permute-start.3 = (bf16[576,128]{1,0:T(8,128)(2,1)}, bf16[576,128]{1,0:T(8,128)(2,1)S(1)}, u32[]{:S(2)}, u32[]{:S(2)}) collective-permute-start(bf16[576,128]{1,0:T(8,128)(2,1)} %shard_map.136), channel_id=1, source_target_pairs={{0,2},{2,0},{4,6},{6,4},{8,10},{10,8},{12,14},{14,12},{1,3},{3,1},... | collective-permute-start | bytes 442376 | tf_op jit(solution)/shard_map/ppermute | solution.py:535
  6.0 8.7 %collective-permute-start.2 = (bf16[576,128]{1,0:T(8,128)(2,1)}, bf16[576,128]{1,0:T(8,128)(2,1)S(1)}, u32[]{:S(2)}, u32[]{:S(2)}) collective-permute-start(bf16[576,128]{1,0:T(8,128)(2,1)} %shard_map.136), channel_id=1, source_target_pairs={{0,12},{2,14},{4,8},{6,10},{8,4},{10,6},{12,0},{14,2},{1,13},{3,15... | collective-permute-start | bytes 442376 | tf_op jit(solution)/shard_map/ppermute | solution.py:535
  9.6 8.3 %collective-permute-start.1 = (bf16[576,128]{1,0:T(8,128)(2,1)}, bf16[576,128]{1,0:T(8,128)(2,1)S(1)}, u32[]{:S(2)}, u32[]{:S(2)}) collective-permute-start(bf16[576,128]{1,0:T(8,128)(2,1)} %shard_map.136), channel_id=1, source_target_pairs={{0,4},{2,6},{4,0},{6,2},{8,12},{10,14},{12,8},{14,10},{1,5},{3,7},... | collective-permute-start | bytes 442376 | tf_op jit(solution)/shard_map/ppermute | solution.py:535
  10.3 12.0 %collective-permute-start = (bf16[576,128]{1,0:T(8,128)(2,1)}, bf16[576,128]{1,0:T(8,128)(2,1)S(1)}, u32[]{:S(2)}, u32[]{:S(2)}) collective-permute-start(bf16[576,128]{1,0:T(8,128)(2,1)} %shard_map.136), channel_id=1, source_target_pairs={{0,8},{2,10},{4,12},{6,14},{8,0},{10,2},{12,4},{14,6},{1,9},{3,11}... | collective-permute-start | bytes 442376 | tf_op jit(solution)/shard_map/ppermute | solution.py:535
  14.8 9.3 %collective-permute-start.6 = (bf16[576,128]{1,0:T(8,128)(2,1)S(1)}, bf16[576,128]{1,0:T(8,128)(2,1)S(1)}, u32[]{:S(2)}, u32[]{:S(2)}) collective-permute-start(bf16[576,128]{1,0:T(8,128)(2,1)S(1)} %collective-permute-done.2), channel_id=1, source_target_pairs={{0,2},{2,0},{4,6},{6,4},{8,10},{10,8},{12,14},{14,12},{1,3},{3,1},... | collective-permute-start | bytes 442376 | tf_op jit(solution)/shard_map/ppermute | solution.py:535
  17.9 6.2 %collective-permute-start.5 = (bf16[576,128]{1,0:T(8,128)(2,1)S(1)}, bf16[576,128]{1,0:T(8,128)(2,1)S(1)}, u32[]{:S(2)}, u32[]{:S(2)}) collective-permute-start(bf16[576,128]{1,0:T(8,128)(2,1)S(1)} %collective-permute-done.1), channel_id=1, source_target_pairs={{0,2},{2,0},{4,6},{6,4},{8,10},{10,8},{12,14},{14,12},{1,3},{3,1},... | collective-permute-start | bytes 442376 | tf_op jit(solution)/shard_map/ppermute | solution.py:535
  22.3 5.1 %collective-permute-start.4 = (bf16[576,128]{1,0:T(8,128)(2,1)S(1)}, bf16[576,128]{1,0:T(8,128)(2,1)S(1)}, u32[]{:S(2)}, u32[]{:S(2)}) collective-permute-start(bf16[576,128]{1,0:T(8,128)(2,1)S(1)} %collective-permute-done), channel_id=1, source_target_pairs={{0,2},{2,0},{4,6},{6,4},{8,10},{10,8},{12,14},{14,12},{1,3},{3,1},... | collective-permute-start | bytes 442376 | tf_op jit(solution)/shard_map/ppermute | solution.py:535
  22.9 4.7 %copy-start.1 = (bf16[256,4096]{1,0:T(8,128)(2,1)S(1)}, bf16[256,4096]{1,0:T(8,128)(2,1)}, u32[]{:S(2)}) copy-start(bf16[256,4096]{1,0:T(8,128)(2,1)} %param.9) | copy-start | bytes 6291460
  24.0 6.1 %collective-permute-start.7 = (bf16[4,576,128]{2,1,0:T(8,128)(2,1)S(1)}, bf16[4,576,128]{2,1,0:T(8,128)(2,1)S(1)}, u32[]{:S(2)}, u32[]{:S(2)}) collective-permute-start(bf16[4,576,128]{2,1,0:T(8,128)(2,1)S(1)} %pad_maximum_fusion.along.own_a), channel_id=1, source_target_pairs={{0,1},{1,0},{2,3},{3,2},{4,5},{5,4},{6,7},{7,6},{8,9},{9,8},{10,11... | collective-permute-start | bytes 1769480 | tf_op jit(solution)/shard_map/ppermute | solution.py:535
  27.5 2.7 %collective-permute-start.8 = (bf16[4,576,128]{2,1,0:T(8,128)(2,1)S(1)}, bf16[4,576,128]{2,1,0:T(8,128)(2,1)S(1)}, u32[]{:S(2)}, u32[]{:S(2)}) collective-permute-start(bf16[4,576,128]{2,1,0:T(8,128)(2,1)S(1)} %pad_maximum_fusion.1.across.own_b), channel_id=1, source_target_pairs={{0,1},{1,0},{2,3},{3,2},{4,5},{5,4},{6,7},{7,6},{8,9},{9,8},{10,11... | collective-permute-start | bytes 1769480 | tf_op jit(solution)/shard_map/ppermute | solution.py:535
  44.5 4.8 %collective-permute-start.11 = (bf16[8,192,128]{2,1,0:T(8,128)(2,1)S(1)}, bf16[8,192,128]{2,1,0:T(8,128)(2,1)S(1)}, u32[]{:S(2)}, u32[]{:S(2)}) collective-permute-start(bf16[8,192,128]{2,1,0:T(8,128)(2,1)S(1)} %get-tuple-element.38), channel_id=1, source_target_pairs={{0,1},{1,0},{2,3},{3,2},{4,5},{5,4},{6,7},{7,6},{8,9},{9,8},{10,11... | collective-permute-start | bytes 1179656 | tf_op jit(solution)/shard_map/ppermute | solution.py:535
  49.2 8.7 %collective-permute-start.12 = (bf16[8,256,128]{2,1,0:T(8,128)(2,1)S(1)}, bf16[8,256,128]{2,1,0:T(8,128)(2,1)S(1)}, u32[]{:S(2)}, u32[]{:S(2)}) collective-permute-start(bf16[8,256,128]{2,1,0:T(8,128)(2,1)S(1)} %get-tuple-element.43), channel_id=1, source_target_pairs={{0,1},{1,0},{2,3},{3,2},{4,5},{5,4},{6,7},{7,6},{8,9},{9,8},{10,11... | collective-permute-start | bytes 1572872 | tf_op jit(solution)/shard_map/ppermute | solution.py:535
  49.4 7.4 %collective-permute-start.19 = (bf16[4,192,128]{2,1,0:T(8,128)(2,1)S(1)}, bf16[4,192,128]{2,1,0:T(8,128)(2,1)S(1)}, u32[]{:S(2)}, u32[]{:S(2)}) collective-permute-start(bf16[4,192,128]{2,1,0:T(8,128)(2,1)S(1)} %add_convert_fusion.3), channel_id=1, source_target_pairs={{0,2},{2,0},{4,6},{6,4},{8,10},{10,8},{12,14},{14,12},{1,3},{3,1},... | collective-permute-start | bytes 589832 | tf_op jit(solution)/shard_map/ppermute | solution.py:535
  56.8 4.7 %collective-permute-start.20 = (bf16[2,192,128]{2,1,0:T(8,128)(2,1)S(1)}, bf16[2,192,128]{2,1,0:T(8,128)(2,1)S(1)}, u32[]{:S(2)}, u32[]{:S(2)}) collective-permute-start(bf16[2,192,128]{2,1,0:T(8,128)(2,1)S(1)} %slice.108), channel_id=1, source_target_pairs={{0,4},{2,6},{4,0},{6,2},{8,12},{10,14},{12,8},{14,10},{1,5},{3,7},... | collective-permute-start | bytes 294920 | tf_op jit(solution)/shard_map/ppermute | solution.py:535
  58.0 8.5 %collective-permute-start.16 = (bf16[4,256,128]{2,1,0:T(8,128)(2,1)S(1)}, bf16[4,256,128]{2,1,0:T(8,128)(2,1)S(1)}, u32[]{:S(2)}, u32[]{:S(2)}) collective-permute-start(bf16[4,256,128]{2,1,0:T(8,128)(2,1)S(1)} %add_convert_fusion.1), channel_id=1, source_target_pairs={{0,2},{2,0},{4,6},{6,4},{8,10},{10,8},{12,14},{14,12},{1,3},{3,1},... | collective-permute-start | bytes 786440 | tf_op jit(solution)/shard_map/ppermute | solution.py:535
  59.7 3.1 %collective-permute-start.13 = (bf16[8,128,128]{2,1,0:T(8,128)(2,1)S(1)}, bf16[8,128,128]{2,1,0:T(8,128)(2,1)S(1)}, u32[]{:S(2)}, u32[]{:S(2)}) collective-permute-start(bf16[8,128,128]{2,1,0:T(8,128)(2,1)S(1)} %get-tuple-element.46), channel_id=1, source_target_pairs={{0,1},{1,0},{2,3},{3,2},{4,5},{5,4},{6,7},{7,6},{8,9},{9,8},{10,11... | collective-permute-start | bytes 786440 | tf_op jit(solution)/shard_map/ppermute | solution.py:535
  61.6 14.6 %collective-permute-start.22 = (bf16[192,128]{1,0:T(8,128)(2,1)S(1)}, bf16[192,128]{1,0:T(8,128)(2,1)S(1)}, u32[]{:S(2)}, u32[]{:S(2)}) collective-permute-start(bf16[192,128]{1,0:T(8,128)(2,1)S(1)} %get-tuple-element.52), channel_id=1, source_target_pairs={{0,8},{2,10},{4,12},{6,14},{8,0},{10,2},{12,4},{14,6},{1,9},{3,11}... | collective-permute-start | bytes 147464 | tf_op jit(solution)/shard_map/ppermute | solution.py:535
  62.9 5.7 %collective-permute-start.14 = (bf16[4,128,128]{2,1,0:T(8,128)(2,1)S(1)}, bf16[4,128,128]{2,1,0:T(8,128)(2,1)S(1)}, u32[]{:S(2)}, u32[]{:S(2)}) collective-permute-start(bf16[4,128,128]{2,1,0:T(8,128)(2,1)S(1)} %add_convert_fusion.6), channel_id=1, source_target_pairs={{0,2},{2,0},{4,6},{6,4},{8,10},{10,8},{12,14},{14,12},{1,3},{3,1},... | collective-permute-start | bytes 393224 | tf_op jit(solution)/shard_map/ppermute | solution.py:535
  66.6 6.4 %collective-permute-start.17 = (bf16[2,256,128]{2,1,0:T(8,128)(2,1)S(1)}, bf16[2,256,128]{2,1,0:T(8,128)(2,1)S(1)}, u32[]{:S(2)}, u32[]{:S(2)}) collective-permute-start(bf16[2,256,128]{2,1,0:T(8,128)(2,1)S(1)} %slice.87), channel_id=1, source_target_pairs={{0,4},{2,6},{4,0},{6,2},{8,12},{10,14},{12,8},{14,10},{1,5},{3,7},... | collective-permute-start | bytes 393224 | tf_op jit(solution)/shard_map/ppermute | solution.py:535
  68.6 6.6 %collective-permute-start.15 = (bf16[2,128,128]{2,1,0:T(8,128)(2,1)S(1)}, bf16[2,128,128]{2,1,0:T(8,128)(2,1)S(1)}, u32[]{:S(2)}, u32[]{:S(2)}) collective-permute-start(bf16[2,128,128]{2,1,0:T(8,128)(2,1)S(1)} %slice.100), channel_id=1, source_target_pairs={{0,4},{2,6},{4,0},{6,2},{8,12},{10,14},{12,8},{14,10},{1,5},{3,7},... | collective-permute-start | bytes 196616 | tf_op jit(solution)/shard_map/ppermute | solution.py:535
  73.1 5.3 %collective-permute-start.21 = (bf16[256,128]{1,0:T(8,128)(2,1)S(1)}, bf16[256,128]{1,0:T(8,128)(2,1)S(1)}, u32[]{:S(2)}, u32[]{:S(2)}) collective-permute-start(bf16[256,128]{1,0:T(8,128)(2,1)S(1)} %get-tuple-element.49), channel_id=1, source_target_pairs={{0,8},{2,10},{4,12},{6,14},{8,0},{10,2},{12,4},{14,6},{1,9},{3,11}... | collective-permute-start | bytes 196616 | tf_op jit(solution)/shard_map/ppermute | solution.py:535
  75.3 4.9 %collective-permute-start.18 = (bf16[128,128]{1,0:T(8,128)(2,1)S(1)}, bf16[128,128]{1,0:T(8,128)(2,1)S(1)}, u32[]{:S(2)}, u32[]{:S(2)}) collective-permute-start(bf16[128,128]{1,0:T(8,128)(2,1)S(1)} %get-tuple-element.48), channel_id=1, source_target_pairs={{0,8},{2,10},{4,12},{6,14},{8,0},{10,2},{12,4},{14,6},{1,9},{3,11}... | collective-permute-start | bytes 98312 | tf_op jit(solution)/shard_map/ppermute | solution.py:535
  (1 other events, 1.2 us)
